TPU v7x, 512 devices: a whole 4x4x16 slice. The times are simulated.
512 devices in a mesh: dp: 16 (over z), seq: 32 (over y, x, core).
Axes of the slice: x: 4, y: 4, z: 16, core: 2. Of those that a mesh axis runs over, the one named last changes fastest.
Arguments:
- inputs: bfloat16 [16, 128, 4096], P('dp', None, 'seq'), may hold values from -6 to 6
- gate_values: bfloat16 [16, 128, 4096], P('dp', None, 'seq'), may hold values from -6 to 6
- grad_out: bfloat16 [16, 128, 4096], P('dp', None, 'seq'), may hold values from -6 to 6
- filter_raw: bfloat16 [128, 4096], P(None, 'seq'), may hold values from -6 to 6
- skip_gain: float32 [128], replicated, may hold values from 0.5 to 2
Outputs:
- d_input: bfloat16 [16, 128, 4096], P('dp', None, 'seq')
- d_gate: bfloat16 [16, 128, 4096], P('dp', None, 'seq')
- d_filter: float32 [128, 4096], P(None, 'seq')
All inputs are finite; a program needn't handle non-finite values.
Results may differ from a plain program's by a relative error of at most 0.001.
Values may be sent and summed in bfloat16 or wider, within the bound.
No kernel may reach another device: no remote copies, remote signals or barrier semaphores. Data moves between devices by JAX's collectives and lax.ppermute only.
A program may use at most 64 MiB of HBM per device.

v0:
```python
import math

import jax
import jax.numpy as jnp
from jax import lax
from jax.sharding import PartitionSpec as P

SPLIT_ROWS = 1
SPLIT_COLS = 128


TWO_PI = 2.0 * math.pi


def partner_2(block, axis, stride):
    count = lax.axis_size(axis)
    route = []
    for low in range(count):
        high = low | 1 << stride
        if high != low and high < count:
            route += [(low, high), (high, low)]
    return lax.ppermute(block, axis, route)


def exact_sum(form, left, right):
    return jnp.einsum(form, left, right, precision=lax.Precision.HIGHEST)


def cdot(form, left, right):
    left_re, left_im = left
    right_re, right_im = right
    real_part = exact_sum(form, left_re, right_re) - exact_sum(form, left_im, right_im)
    imag_part = exact_sum(form, left_re, right_im) + exact_sum(form, left_im, right_re)
    return (real_part, imag_part)


def pair_mul(left, right):
    return (left[0] * right[0] - left[1] * right[1], left[0] * right[1] + left[1] * right[0])


def conj_mul(left, right):
    return (left[0] * right[0] + left[1] * right[1], left[1] * right[0] - left[0] * right[1])


def turn(field, w_re, w_im):
    return jnp.stack([field[0] * w_re - field[1] * w_im, field[0] * w_im + field[1] * w_re])


def dft_table(count, sign):
    index = jnp.arange(count, dtype=jnp.int32)
    product = index[:, None] * index[None, :] % count
    angle = product.astype(jnp.float32) * (TWO_PI / count)
    return (jnp.cos(angle), sign * jnp.sin(angle))


def twiddle_table(rows, cols, sign):
    rows_idx = jnp.arange(rows, dtype=jnp.int32)
    cols_idx = jnp.arange(cols, dtype=jnp.int32)
    product = rows_idx[:, None] * cols_idx[None, :] % (rows * cols)
    angle = product.astype(jnp.float32) * (TWO_PI / (rows * cols))
    return (jnp.cos(angle), sign * jnp.sin(angle))


def local_forward(field, rows, cols):
    shape = field.shape
    blocks = field.reshape(shape[:-1] + (rows, cols))
    first = cdot("ca,...ab->...cb", dft_table(rows, -1.0), (blocks[0], blocks[1]))
    turned = pair_mul(first, twiddle_table(rows, cols, -1.0))
    last = cdot("...cb,db->...cd", turned, dft_table(cols, -1.0))
    return jnp.stack(last).reshape(shape)


def local_inverse(field, rows, cols):
    shape = field.shape
    blocks = field.reshape(shape[:-1] + (rows, cols))
    first = cdot("...cd,db->...cb", (blocks[0], blocks[1]), dft_table(cols, 1.0))
    turned = pair_mul(first, twiddle_table(rows, cols, 1.0))
    last = cdot("ca,...cb->...ab", dft_table(rows, 1.0), turned)
    scale = 1.0 / (rows * cols)
    return (jnp.stack(last) * scale).reshape(shape)


def device_section(field, inverse):
    count = lax.axis_size("seq")
    place = lax.axis_index("seq")
    levels = count.bit_length() - 1
    order = list(range(levels)) if inverse else list(range(levels - 1, -1, -1))
    for level in order:
        half = 1 << level
        partner = partner_2(field, "seq", level)
        upper = place >> level & 1 == 1
        angle = (place % half).astype(jnp.float32) * (TWO_PI / (2 * half))
        if inverse:
            w_re = jnp.cos(angle)
            w_im = jnp.sin(angle)
            lower_out = 0.5 * (field + turn(partner, w_re, w_im))
            upper_out = 0.5 * (partner - turn(field, w_re, w_im))
        else:
            w_re = jnp.cos(angle)
            w_im = -jnp.sin(angle)
            lower_out = field + partner
            upper_out = turn(partner - field, w_re, w_im)
        field = jnp.where(upper, upper_out, lower_out)
    return field


def held_block(place, count):
    levels = count.bit_length() - 1
    result = jnp.zeros((), jnp.int32)
    for level in range(levels):
        result = result + ((place >> level & 1) << levels - 1 - level)
    return result


def position_plan(inputs, gate_values, grad_out, filter_raw, skip_gain):
    count = lax.axis_size("seq")
    place = lax.axis_index("seq")
    length_dev = inputs.shape[-1]
    chans = inputs.shape[1]
    seq_len = length_dev * count
    total = 2 * seq_len
    signal = inputs[0].astype(jnp.float32)
    gate_f = gate_values[0].astype(jnp.float32)
    grad_f = grad_out[0].astype(jnp.float32)
    kernel = filter_raw.astype(jnp.float32) / math.sqrt(seq_len)
    grad_conv = grad_f * gate_f
    shift_angle = place.astype(jnp.float32) * (TWO_PI / (2 * count))
    shift_re = jnp.cos(shift_angle)
    shift_im = jnp.sin(shift_angle)
    real_parts = jnp.stack([signal, grad_conv, kernel])
    nothing = jnp.zeros_like(real_parts)
    field = jnp.stack(
        [
            jnp.concatenate([real_parts, real_parts * shift_re]),
            jnp.concatenate([nothing, -real_parts * shift_im]),
        ]
    )
    field = device_section(field, False)
    held = held_block(place, count)
    positions = jnp.arange(length_dev, dtype=jnp.int32)
    turns = jnp.stack([positions * (2 * held) % total, positions * (2 * held + 1) % total])
    angles = turns.astype(jnp.float32)[:, None, None, :] * (TWO_PI / total)
    field = field.reshape(2, 2, 3, chans, length_dev)
    field = turn(field, jnp.cos(angles), -jnp.sin(angles))
    spectra = local_forward(field, SPLIT_ROWS, SPLIT_COLS)
    signal_hat = (spectra[0, :, 0], spectra[1, :, 0])
    grad_hat = (spectra[0, :, 1], spectra[1, :, 1])
    kernel_hat = (spectra[0, :, 2], spectra[1, :, 2])
    forward_prod = pair_mul(signal_hat, kernel_hat)
    backward_prod = conj_mul(grad_hat, kernel_hat)
    filter_prod = conj_mul(grad_hat, signal_hat)
    first_re = forward_prod[0] - backward_prod[1]
    first_im = forward_prod[1] + backward_prod[0]
    products = jnp.stack(
        [jnp.stack([first_re, filter_prod[0]], 1), jnp.stack([first_im, filter_prod[1]], 1)]
    )
    times_back = local_inverse(products, SPLIT_ROWS, SPLIT_COLS)
    times_back = turn(times_back, jnp.cos(angles), jnp.sin(angles))
    times_back = device_section(times_back.reshape(2, 4, chans, length_dev), True)
    times_back = times_back.reshape(2, 2, 2, chans, length_dev)
    combined = 0.5 * (times_back[:, 0] + turn(times_back[:, 1], shift_re, shift_im))
    conv = combined[0, 0]
    corr = combined[1, 0]
    filt = combined[0, 1]
    gains = skip_gain[:, None]
    d_gate = (grad_f * (conv + gains * signal)).astype(jnp.bfloat16)
    d_input = (corr + gains * grad_conv).astype(jnp.bfloat16)
    return (d_input, d_gate, filt)


def body(inputs, gate_values, grad_out, filter_raw, skip_gain):
    seq_len = inputs.shape[-1] * lax.axis_size("seq")
    d_input, d_gate, filt = position_plan(inputs, gate_values, grad_out, filter_raw, skip_gain)
    d_filter = lax.psum(filt, "dp") / math.sqrt(seq_len)
    return (d_input[None], d_gate[None], d_filter)


def solution(mesh):
    return jax.shard_map(
        body,
        mesh=mesh,
        in_specs=(
            P("dp", None, "seq"),
            P("dp", None, "seq"),
            P("dp", None, "seq"),
            P(None, "seq"),
            P(),
        ),
        out_specs=(P("dp", None, "seq"), P("dp", None, "seq"), P(None, "seq")),
        check_vma=False,
    )
```

profile of v0, /device:TPU:2, one launch (start us, length us, event | category | flops | bytes accessed | tf_op | source)
XLA Modules:
  0.0 319.7 jit_solution(919940789642997246)
XLA Ops:
  9.1 5.1 %collective-permute-start = (f32[2,6,128,128]{3,2,1,0:T(8,128)S(1)}, f32[2,6,128,128]{3,2,1,0:T(8,128)S(1)}, u32[]{:S(2)}, u32[]{:S(2)}) collective-permute-start(f32[2,6,128,128]{3,2,1,0:T(8,128)S(1)} %pad_maximum_fusion), channel_id=1, source_target_pairs={{0,16},{16,0},{1,17},{17,1},{2,18},{18,2},{3,19},{19,3},{4,20},{20... | collective-permute-start | bytes 2359304 | tf_op jit(solution)/shard_map/ppermute | solution.py:22
  14.4 17.4 %collective-permute-done = f32[2,6,128,128]{3,2,1,0:T(8,128)S(1)} collective-permute-done((f32[2,6,128,128]{3,2,1,0:T(8,128)S(1)}, f32[2,6,128,128]{3,2,1,0:T(8,128)S(1)}, u32[]{:S(2)}, u32[]{:S(2)}) %collective-permute-start) | collective-permute-done | bytes 786464 | tf_op jit(solution)/shard_map/ppermute | solution.py:22
  32.0 1.0 maximum_select_fusion
  33.0 3.5 %collective-permute-start.1 = (f32[2,6,128,128]{3,2,1,0:T(8,128)}, f32[2,6,128,128]{3,2,1,0:T(8,128)S(1)}, u32[]{:S(2)}, u32[]{:S(2)}) collective-permute-start(f32[2,6,128,128]{3,2,1,0:T(8,128)} %maximum_select_fusion), channel_id=1, source_target_pairs={{0,8},{8,0},{1,9},{9,1},{2,10},{10,2},{3,11},{11,3},{4,12},{12,4},... | collective-permute-start | bytes 2359304 | tf_op jit(solution)/shard_map/ppermute | solution.py:22
  36.6 16.9 %collective-permute-done.1 = f32[2,6,128,128]{3,2,1,0:T(8,128)S(1)} collective-permute-done((f32[2,6,128,128]{3,2,1,0:T(8,128)}, f32[2,6,128,128]{3,2,1,0:T(8,128)S(1)}, u32[]{:S(2)}, u32[]{:S(2)}) %collective-permute-start.1) | collective-permute-done | bytes 786464 | tf_op jit(solution)/shard_map/ppermute | solution.py:22
  54.5 1.4 maximum_select_fusion.1
  55.9 4.0 %collective-permute-start.2 = (f32[2,6,128,128]{3,2,1,0:T(8,128)S(1)}, f32[2,6,128,128]{3,2,1,0:T(8,128)S(1)}, u32[]{:S(2)}, u32[]{:S(2)}) collective-permute-start(f32[2,6,128,128]{3,2,1,0:T(8,128)S(1)} %maximum_select_fusion.1), channel_id=1, source_target_pairs={{0,4},{4,0},{1,5},{5,1},{2,6},{6,2},{3,7},{7,3},{8,12},{12,8},{9,1... | collective-permute-start | bytes 2359304 | tf_op jit(solution)/shard_map/ppermute | solution.py:22
  60.1 16.7 %collective-permute-done.2 = f32[2,6,128,128]{3,2,1,0:T(8,128)S(1)} collective-permute-done((f32[2,6,128,128]{3,2,1,0:T(8,128)S(1)}, f32[2,6,128,128]{3,2,1,0:T(8,128)S(1)}, u32[]{:S(2)}, u32[]{:S(2)}) %collective-permute-start.2) | collective-permute-done | bytes 786464 | tf_op jit(solution)/shard_map/ppermute | solution.py:22
  77.1 2.2 collective-permute-start.3
  79.5 16.1 %collective-permute-done.3 = f32[2,6,128,128]{3,2,1,0:T(8,128)S(1)} collective-permute-done((f32[2,6,128,128]{3,2,1,0:T(8,128)S(1)}, f32[2,6,128,128]{3,2,1,0:T(8,128)S(1)}, u32[]{:S(2)}, u32[]{:S(2)}) %collective-permute-start.3) | collective-permute-done | bytes 786464 | tf_op jit(solution)/shard_map/ppermute | solution.py:22
  95.9 1.9 collective-permute-start.4
  98.0 2.1 collective-permute-done.4
  106.5 2.0 collective-permute-start.5
  108.6 1.7 collective-permute-done.5
  110.5 2.2 collective-permute-start.6
  112.7 13.6 %collective-permute-done.6 = f32[2,4,128,128]{3,2,1,0:T(8,128)S(1)} collective-permute-done((f32[2,4,128,128]{3,2,1,0:T(8,128)S(1)}, f32[2,4,128,128]{3,2,1,0:T(8,128)S(1)}, u32[]{:S(2)}, u32[]{:S(2)}) %collective-permute-start.6) | collective-permute-done | bytes 524320 | tf_op jit(solution)/shard_map/ppermute | solution.py:22
  126.7 4.0 %collective-permute-start.7 = (f32[2,4,128,128]{3,2,1,0:T(8,128)S(1)}, f32[2,4,128,128]{3,2,1,0:T(8,128)S(1)}, u32[]{:S(2)}, u32[]{:S(2)}) collective-permute-start(f32[2,4,128,128]{3,2,1,0:T(8,128)S(1)} %fusion.6), channel_id=1, source_target_pairs={{0,4},{4,0},{1,5},{5,1},{2,6},{6,2},{3,7},{7,3},{8,12},{12,8},{9,1... | collective-permute-start | bytes 1572872 | tf_op jit(solution)/shard_map/ppermute | solution.py:22
  130.8 12.4 %collective-permute-done.7 = f32[2,4,128,128]{3,2,1,0:T(8,128)S(1)} collective-permute-done((f32[2,4,128,128]{3,2,1,0:T(8,128)S(1)}, f32[2,4,128,128]{3,2,1,0:T(8,128)S(1)}, u32[]{:S(2)}, u32[]{:S(2)}) %collective-permute-start.7) | collective-permute-done | bytes 524320 | tf_op jit(solution)/shard_map/ppermute | solution.py:22
  143.4 3.5 %collective-permute-start.8 = (f32[2,4,128,128]{3,2,1,0:T(8,128)S(1)}, f32[2,4,128,128]{3,2,1,0:T(8,128)S(1)}, u32[]{:S(2)}, u32[]{:S(2)}) collective-permute-start(f32[2,4,128,128]{3,2,1,0:T(8,128)S(1)} %fusion.9), channel_id=1, source_target_pairs={{0,8},{8,0},{1,9},{9,1},{2,10},{10,2},{3,11},{11,3},{4,12},{12,4},... | collective-permute-start | bytes 1572872 | tf_op jit(solution)/shard_map/ppermute | solution.py:22
  147.0 10.5 %collective-permute-done.8 = f32[2,4,128,128]{3,2,1,0:T(8,128)S(1)} collective-permute-done((f32[2,4,128,128]{3,2,1,0:T(8,128)S(1)}, f32[2,4,128,128]{3,2,1,0:T(8,128)S(1)}, u32[]{:S(2)}, u32[]{:S(2)}) %collective-permute-start.8) | collective-permute-done | bytes 524320 | tf_op jit(solution)/shard_map/ppermute | solution.py:22
  157.7 5.1 %collective-permute-start.9 = (f32[2,4,128,128]{3,2,1,0:T(8,128)S(1)}, f32[2,4,128,128]{3,2,1,0:T(8,128)S(1)}, u32[]{:S(2)}, u32[]{:S(2)}) collective-permute-start(f32[2,4,128,128]{3,2,1,0:T(8,128)S(1)} %fusion.12), channel_id=1, source_target_pairs={{0,16},{16,0},{1,17},{17,1},{2,18},{18,2},{3,19},{19,3},{4,20},{20... | collective-permute-start | bytes 1572872 | tf_op jit(solution)/shard_map/ppermute | solution.py:22
  162.9 9.5 %collective-permute-done.9 = f32[2,4,128,128]{3,2,1,0:T(8,128)S(1)} collective-permute-done((f32[2,4,128,128]{3,2,1,0:T(8,128)S(1)}, f32[2,4,128,128]{3,2,1,0:T(8,128)S(1)}, u32[]{:S(2)}, u32[]{:S(2)}) %collective-permute-start.9) | collective-permute-done | bytes 524320 | tf_op jit(solution)/shard_map/ppermute | solution.py:22
  174.8 136.6 %all-reduce.3.cloned.1.call-done = f32[128,128]{1,0:T(8,128)} async-done(((f32[128,128]{1,0:T(8,128)}), f32[128,128]{1,0:T(8,128)}) %all-reduce.3.cloned.1.call-update) | async-done | bytes 65552 | tf_op jit(solution)/shard_map/psum | solution.py:174
  311.4 1.5 broadcast_multiply_fusion
  (77 shorter events, 13.3 us)
Async XLA Ops:
  7.2 304.2 %all-reduce.3.cloned.1.call-start = ((), (), s32[]{:S(2)}) async-start(), calls=%async_computation | async-start | bytes 131072 | tf_op jit(solution)/shard_map/psum | solution.py:174
  7.4 0.8 copy-start.4
  8.2 0.8 copy-start.2
  8.2 0.8 copy-start.3
  9.1 22.7 %collective-permute-start = (f32[2,6,128,128]{3,2,1,0:T(8,128)S(1)}, f32[2,6,128,128]{3,2,1,0:T(8,128)S(1)}, u32[]{:S(2)}, u32[]{:S(2)}) collective-permute-start(f32[2,6,128,128]{3,2,1,0:T(8,128)S(1)} %pad_maximum_fusion), channel_id=1, source_target_pairs={{0,16},{16,0},{1,17},{17,1},{2,18},{18,2},{3,19},{19,3},{4,20},{20... | collective-permute-start | bytes 2359304 | tf_op jit(solution)/shard_map/ppermute | solution.py:22
  33.0 20.5 %collective-permute-start.1 = (f32[2,6,128,128]{3,2,1,0:T(8,128)}, f32[2,6,128,128]{3,2,1,0:T(8,128)S(1)}, u32[]{:S(2)}, u32[]{:S(2)}) collective-permute-start(f32[2,6,128,128]{3,2,1,0:T(8,128)} %maximum_select_fusion), channel_id=1, source_target_pairs={{0,8},{8,0},{1,9},{9,1},{2,10},{10,2},{3,11},{11,3},{4,12},{12,4},... | collective-permute-start | bytes 2359304 | tf_op jit(solution)/shard_map/ppermute | solution.py:22
  53.5 0.9 copy-start
  55.9 20.9 %collective-permute-start.2 = (f32[2,6,128,128]{3,2,1,0:T(8,128)S(1)}, f32[2,6,128,128]{3,2,1,0:T(8,128)S(1)}, u32[]{:S(2)}, u32[]{:S(2)}) collective-permute-start(f32[2,6,128,128]{3,2,1,0:T(8,128)S(1)} %maximum_select_fusion.1), channel_id=1, source_target_pairs={{0,4},{4,0},{1,5},{5,1},{2,6},{6,2},{3,7},{7,3},{8,12},{12,8},{9,1... | collective-permute-start | bytes 2359304 | tf_op jit(solution)/shard_map/ppermute | solution.py:22
  77.1 18.5 %collective-permute-start.3 = (f32[2,6,128,128]{3,2,1,0:T(8,128)S(1)}, f32[2,6,128,128]{3,2,1,0:T(8,128)S(1)}, u32[]{:S(2)}, u32[]{:S(2)}) collective-permute-start(f32[2,6,128,128]{3,2,1,0:T(8,128)S(1)} %maximum_select_fusion.2), channel_id=1, source_target_pairs={{0,2},{2,0},{1,3},{3,1},{4,6},{6,4},{5,7},{7,5},{8,10},{10,8},{9,1... | collective-permute-start | bytes 2359304 | tf_op jit(solution)/shard_map/ppermute | solution.py:22
  95.9 4.2 %collective-permute-start.4 = (f32[2,6,128,128]{3,2,1,0:T(8,128)S(1)}, f32[2,6,128,128]{3,2,1,0:T(8,128)S(1)}, u32[]{:S(2)}, u32[]{:S(2)}) collective-permute-start(f32[2,6,128,128]{3,2,1,0:T(8,128)S(1)} %maximum_select_fusion.3), channel_id=1, source_target_pairs={{0,1},{1,0},{2,3},{3,2},{4,5},{5,4},{6,7},{7,6},{8,9},{9,8},{10,11... | collective-permute-start | bytes 2359304 | tf_op jit(solution)/shard_map/ppermute | solution.py:22
  106.5 3.8 %collective-permute-start.5 = (f32[2,4,128,128]{3,2,1,0:T(8,128)S(1)}, f32[2,4,128,128]{3,2,1,0:T(8,128)S(1)}, u32[]{:S(2)}, u32[]{:S(2)}) collective-permute-start(f32[2,4,128,128]{3,2,1,0:T(8,128)S(1)} %pad_maximum_fusion.1), channel_id=1, source_target_pairs={{0,1},{1,0},{2,3},{3,2},{4,5},{5,4},{6,7},{7,6},{8,9},{9,8},{10,11... | collective-permute-start | bytes 1572872 | tf_op jit(solution)/shard_map/ppermute | solution.py:22
  110.5 15.9 %collective-permute-start.6 = (f32[2,4,128,128]{3,2,1,0:T(8,128)S(1)}, f32[2,4,128,128]{3,2,1,0:T(8,128)S(1)}, u32[]{:S(2)}, u32[]{:S(2)}) collective-permute-start(f32[2,4,128,128]{3,2,1,0:T(8,128)S(1)} %fusion.3), channel_id=1, source_target_pairs={{0,2},{2,0},{1,3},{3,1},{4,6},{6,4},{5,7},{7,5},{8,10},{10,8},{9,1... | collective-permute-start | bytes 1572872 | tf_op jit(solution)/shard_map/ppermute | solution.py:22
  126.7 16.5 %collective-permute-start.7 = (f32[2,4,128,128]{3,2,1,0:T(8,128)S(1)}, f32[2,4,128,128]{3,2,1,0:T(8,128)S(1)}, u32[]{:S(2)}, u32[]{:S(2)}) collective-permute-start(f32[2,4,128,128]{3,2,1,0:T(8,128)S(1)} %fusion.6), channel_id=1, source_target_pairs={{0,4},{4,0},{1,5},{5,1},{2,6},{6,2},{3,7},{7,3},{8,12},{12,8},{9,1... | collective-permute-start | bytes 1572872 | tf_op jit(solution)/shard_map/ppermute | solution.py:22
  143.4 14.1 %collective-permute-start.8 = (f32[2,4,128,128]{3,2,1,0:T(8,128)S(1)}, f32[2,4,128,128]{3,2,1,0:T(8,128)S(1)}, u32[]{:S(2)}, u32[]{:S(2)}) collective-permute-start(f32[2,4,128,128]{3,2,1,0:T(8,128)S(1)} %fusion.9), channel_id=1, source_target_pairs={{0,8},{8,0},{1,9},{9,1},{2,10},{10,2},{3,11},{11,3},{4,12},{12,4},... | collective-permute-start | bytes 1572872 | tf_op jit(solution)/shard_map/ppermute | solution.py:22
  157.7 14.7 %collective-permute-start.9 = (f32[2,4,128,128]{3,2,1,0:T(8,128)S(1)}, f32[2,4,128,128]{3,2,1,0:T(8,128)S(1)}, u32[]{:S(2)}, u32[]{:S(2)}) collective-permute-start(f32[2,4,128,128]{3,2,1,0:T(8,128)S(1)} %fusion.12), channel_id=1, source_target_pairs={{0,16},{16,0},{1,17},{17,1},{2,18},{18,2},{3,19},{19,3},{4,20},{20... | collective-permute-start | bytes 1572872 | tf_op jit(solution)/shard_map/ppermute | solution.py:22
  173.3 0.8 copy-start.1
  173.3 0.8 copy-start.5
Sparse Core Ops, SparseCore 0:
  173.5 137.8 all-reduce.2
where the time goes:
time: 320 us
  waiting for transfers between devices  253 us (79%)
  starting transfers between devices  33.7 us (11%)
  between operations  15.4 us (5%)
  other arithmetic  8.78 us (3%)
  matrix products  5.47 us (2%)
    psum x1, waiting for transfers between devices, body(): d_filter = lax.psum(filt, 'dp') / math.sqrt(seq_len)  137 us
    ppermute x10, waiting for transfers between devices, partner_2(): return lax.ppermute(block, axis, route)  117 us
    ppermute x10, starting transfers between devices, partner_2(): return lax.ppermute(block, axis, route)  33.6 us
  transfers between devices with their start and end apart: 11, of which 11 were waited for; matrix products, arithmetic and copies ran while one was open for 0% of the time, Pallas kernels for 0%

commit v1 on v0

v1 whole, which is shorter than its diff:
```python
import jax
import jax.numpy as jnp
from jax import lax
from jax.experimental import pallas as pl
from jax.experimental.pallas import tpu as pltpu
from jax.sharding import Mesh, PartitionSpec as P

LANES = 128
GROUP = 4
ROLES = 4

F32 = jnp.float32
BF16 = jnp.bfloat16


def iota(shape, dim):
    return lax.broadcasted_iota(jnp.int32, shape, dim)


def pack_kernel(u_ref, g_ref, y_ref, k_ref, out_ref, rows):
    chans = u_ref.shape[0]
    for role, ref in enumerate((u_ref, g_ref, y_ref, k_ref)):
        rows[pl.ds(role, chans, stride=ROLES), :] = ref[...].astype(F32)
    out_ref[...] = rows[...].astype(BF16)


def flip_rows(count, span):
    row, col = iota((count, count), 0), iota((count, count), 1)
    same = row // span == col // span
    return jnp.where(same & (row % span + col % span == span - 1), 1.0, 0.0).astype(BF16)


def conv_kernel(blocks, chan_ref, gain_ref, in_ref, gate_ref, input_ref, filt_ref, rows, padded, filt_rows):
    count = GROUP * blocks
    rows[...] = in_ref[...].astype(F32)
    u = rows[pl.ds(0, count, stride=ROLES), :]
    g = rows[pl.ds(1, count, stride=ROLES), :]
    y = rows[pl.ds(2, count, stride=ROLES), :]
    k = rows[pl.ds(3, blocks, stride=ROLES), :]
    gc = g * y
    high = gc.astype(BF16)
    low = (gc - high.astype(F32)).astype(BF16)

    lane_flip = flip_rows(LANES, LANES)
    flip = flip_rows(2 * count, blocks)
    both = jnp.concatenate([high, low], axis=0)
    both = jnp.dot(both, lane_flip, preferred_element_type=F32).astype(BF16)
    both = jnp.dot(flip, both, preferred_element_type=F32)
    turned_u = jnp.dot(flip[:count, :count], u.astype(BF16), preferred_element_type=F32)
    left = jnp.transpose(turned_u).astype(BF16)
    left = jnp.concatenate([left, left], axis=1)

    for part in range(3 * GROUP):
        padded[part, :blocks, :] = jnp.zeros((blocks, LANES), F32)
        if part < GROUP:
            value = u[part * blocks : (part + 1) * blocks]
        else:
            at = (part - GROUP) * blocks
            value = both[at : at + blocks]
        padded[part, blocks:, :] = value

    row, col = iota((LANES, LANES), 0), iota((LANES, LANES), 1)
    inside = col >= row
    zero = jnp.zeros((LANES, LANES), F32)
    before = zero
    total = jnp.zeros((3 * count, LANES), F32)
    held = None
    for pair in range(blocks // 2):
        shifted, toeplitz = [], []
        for d in (2 * pair, 2 * pair + 1):
            shifted.append(
                jnp.concatenate([padded[part, blocks - d : 2 * blocks - d, :] for part in range(3 * GROUP)], axis=0).astype(BF16)
            )
            spread = jnp.broadcast_to(k[d : d + 1, :], (LANES, LANES))
            rolled = pltpu.roll(spread, 0, 1, stride=1, stride_axis=0)
            toeplitz.append(jnp.where(inside, rolled, before).astype(BF16))
            before = rolled
        wide = jnp.concatenate(shifted, axis=1)
        total = total + jnp.dot(wide, jnp.concatenate(toeplitz, axis=0), preferred_element_type=F32)
        products = jnp.dot(left, wide[count:], preferred_element_type=F32)
        for half in range(2):
            d = 2 * pair + half
            turned = pltpu.roll(products[:, half * LANES : (half + 1) * LANES], 0, 1, stride=1, stride_axis=0)
            if held is not None:
                filt_rows[d - 1 : d, :] = jnp.sum(jnp.where(inside, held, turned), axis=0, keepdims=True)
            held = turned
    filt_rows[blocks - 1 : blocks, :] = jnp.sum(jnp.where(inside, held, 0.0), axis=0, keepdims=True)

    scale = 1.0 / 64.0
    gain = gain_ref[chan_ref[0]]
    gate_ref[...] = (y * (total[:count] * scale + gain * u)).astype(BF16)
    corr = total[count : 2 * count] + total[2 * count :]
    turned_gc = both[:count] + both[count:]
    d_input = (corr * scale + gain * turned_gc).astype(BF16)
    d_input = jnp.dot(d_input, lane_flip, preferred_element_type=F32).astype(BF16)
    input_ref[...] = jnp.dot(flip[:count, :count], d_input, preferred_element_type=F32).astype(BF16)
    filt = jnp.dot(filt_rows[...], lane_flip.astype(F32), precision=lax.Precision.HIGHEST, preferred_element_type=F32)
    for copy in range(filt_ref.shape[0]):
        filt_ref[copy] = filt


def spread_kernel(blocks, gate_ref, input_ref, filt_ref, out_ref, rows):
    count = GROUP * blocks
    filt = filt_ref[0]
    for copy in range(1, filt_ref.shape[0]):
        filt = filt + filt_ref[copy]
    high = filt.astype(BF16).astype(F32)
    low = filt - high
    rows[pl.ds(0, count, stride=ROLES), :] = gate_ref[...].astype(F32)
    rows[pl.ds(1, count, stride=ROLES), :] = input_ref[...].astype(F32)
    for part in range(GROUP):
        at = part * blocks * ROLES
        rows[pl.ds(at + 2, blocks, stride=ROLES), :] = high
        rows[pl.ds(at + 3, blocks, stride=ROLES), :] = low
    out_ref[...] = rows[...].astype(BF16)


def unpack_kernel(in_ref, input_ref, gate_ref, filt_ref, rows):
    chans = input_ref.shape[0]
    rows[...] = in_ref[...].astype(F32)
    gate_ref[...] = rows[pl.ds(0, chans, stride=ROLES), :].astype(BF16)
    input_ref[...] = rows[pl.ds(1, chans, stride=ROLES), :].astype(BF16)
    filt = rows[pl.ds(2, chans, stride=ROLES), :] + rows[pl.ds(3, chans, stride=ROLES), :]
    filt_ref[...] = filt * (1.0 / 64.0)


VMEM = pl.BlockSpec(memory_space=pltpu.VMEM)
SMEM = pl.BlockSpec(memory_space=pltpu.SMEM)


def shape(dims, dtype):
    return jax.ShapeDtypeStruct(dims, dtype)


def body(inputs, gate_values, grad_out, filter_raw, skip_gain):
    blocks = lax.axis_size("seq")
    far = lax.axis_size("far")
    chans = inputs.shape[1]
    count = GROUP * blocks
    params = pltpu.CompilerParams(vmem_limit_bytes=48 * 1024 * 1024)
    packed = pl.pallas_call(
        pack_kernel,
        out_shape=shape((chans * ROLES, LANES), BF16),
        in_specs=[VMEM] * 4,
        out_specs=VMEM,
        scratch_shapes=[pltpu.VMEM((chans * ROLES, LANES), F32)],
        compiler_params=params,
    )(inputs[0], gate_values[0], grad_out[0], filter_raw)
    packed = lax.all_to_all(packed, ("near", "seq"), 0, 0, tiled=True)
    chan = (lax.axis_index("near") * blocks + lax.axis_index("seq")).reshape(1)
    gate, d_in, filt = pl.pallas_call(
        lambda *refs: conv_kernel(blocks, *refs),
        out_shape=(shape((count, LANES), BF16), shape((count, LANES), BF16), shape((far, blocks, LANES), F32)),
        in_specs=[SMEM, SMEM, VMEM],
        out_specs=(VMEM, VMEM, VMEM),
        scratch_shapes=[
            pltpu.VMEM((count * ROLES, LANES), F32),
            pltpu.VMEM((3 * GROUP, 2 * blocks, LANES), F32),
            pltpu.VMEM((blocks, LANES), F32),
        ],
        compiler_params=params,
    )(chan, skip_gain, packed)
    filt = lax.all_to_all(filt, "far", 0, 0, tiled=True)
    packed = pl.pallas_call(
        lambda *refs: spread_kernel(blocks, *refs),
        out_shape=shape((count * ROLES, LANES), BF16),
        in_specs=[VMEM] * 3,
        out_specs=VMEM,
        scratch_shapes=[pltpu.VMEM((count * ROLES, LANES), F32)],
        compiler_params=params,
    )(gate, d_in, filt)
    packed = lax.all_to_all(packed, ("near", "seq"), 0, 0, tiled=True)
    d_input, d_gate, d_filter = pl.pallas_call(
        unpack_kernel,
        out_shape=(shape((chans, LANES), BF16), shape((chans, LANES), BF16), shape((chans, LANES), F32)),
        in_specs=[VMEM],
        out_specs=(VMEM, VMEM, VMEM),
        scratch_shapes=[pltpu.VMEM((chans * ROLES, LANES), F32)],
        compiler_params=params,
    )(packed)
    return d_input[None], d_gate[None], d_filter


def solution(mesh):
    sizes = mesh.devices.shape
    mesh = Mesh(mesh.devices.reshape(sizes[0] // GROUP, GROUP, sizes[1]), ("far", "near", "seq"))
    signal = P(("far", "near"), None, "seq")
    return jax.shard_map(
        body,
        mesh=mesh,
        in_specs=(signal, signal, signal, P(None, "seq"), P()),
        out_specs=(signal, signal, P(None, "seq")),
        check_vma=False,
    )
```

time: 320 us -> 75.4 us (0.24)
  the two profiles are of different devices: /device:TPU:2 before, /device:TPU:1 now
where the time goes in v1:
time: 75.4 us; the launch traced here: 74.8 us
  blocking collectives  41.8 us (55%)
  starting transfers between devices  13.8 us (18%)
  waiting for transfers between devices  10.9 us (14%)
  Pallas kernels  3.89 us (5%)
  local copies, waits for them, and re-layouts  3.68 us (5%)
    all_to_all x1, blocking collectives, body(): filt = lax.all_to_all(filt, 'far', 0, 0, tiled=True)  23.6 us
    all_to_all x1, blocking collectives, body(): packed = lax.all_to_all(packed, ('near', 'seq'), 0, 0, tiled=True)  18.3 us
    all_to_all x1, starting transfers between devices, body(): packed = lax.all_to_all(packed, ('near', 'seq'), 0, 0, tiled=True)  13.8 us
    all_to_all x1, waiting for transfers between devices, body(): packed = lax.all_to_all(packed, ('near', 'seq'), 0, 0, tiled=True)  10.9 us
    unnamed x10, local copies, waits for them, and re-layouts  3.68 us
    pallas_call x1, Pallas kernels, body(): pl.pallas_call(lambda *refs: conv_kernel(blocks, *refs), out_shape=(shape...  2.48 us
  transfers between devices with their start and end apart: 1, of which 1 were waited for; matrix products, arithmetic and copies ran while one was open for 0% of the time, Pallas kernels for 0%

profile of v1, /device:TPU:1, one launch (start us, length us, event | category | flops | bytes accessed | tf_op | source)
XLA Modules:
  0.0 74.8 jit_solution(6605188232787065989)
XLA Ops:
  0.6 0.0 copy-start
  0.6 0.7 %copy-done = bf16[1,128,128]{2,1,0:T(8,128)(2,1)S(1)} copy-done((bf16[1,128,128]{2,1,0:T(8,128)(2,1)S(1)}, bf16[1,128,128]{2,1,0:T(8,128)(2,1)}, u32[]{:S(2)}) %copy-start) | copy-done | bytes 32792
  1.4 0.0 copy-start.1
  1.4 0.8 %copy-done.1 = bf16[1,128,128]{2,1,0:T(8,128)(2,1)S(1)} copy-done((bf16[1,128,128]{2,1,0:T(8,128)(2,1)S(1)}, bf16[1,128,128]{2,1,0:T(8,128)(2,1)}, u32[]{:S(2)}) %copy-start.1) | copy-done | bytes 32792
  2.1 0.0 copy-start.2
  2.2 0.8 %copy-done.2 = bf16[1,128,128]{2,1,0:T(8,128)(2,1)S(1)} copy-done((bf16[1,128,128]{2,1,0:T(8,128)(2,1)S(1)}, bf16[1,128,128]{2,1,0:T(8,128)(2,1)}, u32[]{:S(2)}) %copy-start.2) | copy-done | bytes 32792
  2.9 0.0 copy-start.3
  2.9 0.8 %copy-done.3 = bf16[128,128]{1,0:T(8,128)(2,1)S(1)} copy-done((bf16[128,128]{1,0:T(8,128)(2,1)S(1)}, bf16[128,128]{1,0:T(8,128)(2,1)}, u32[]{:S(2)}) %copy-start.3) | copy-done | bytes 32792
  3.7 0.7 shard_map.76
  4.4 13.8 %all-to-all-start = ((bf16[128,4,128]{2,1,0:T(4,128)(2,1)}), bf16[128,4,128]{2,1,0:T(4,128)(2,1)S(1)}, u32[]{:S(2)}, u32[]{:S(2)}) async-start(bf16[128,4,128]{2,1,0:T(4,128)(2,1)} %bitcast.4), calls=%async_computation | async-start | bytes 262144 | tf_op jit(solution)/shard_map/all_to_all | solution.py:149
  18.2 10.9 %all-to-all-done = bf16[128,4,128]{2,1,0:T(4,128)(2,1)S(1)} async-done(((bf16[128,4,128]{2,1,0:T(4,128)(2,1)}), bf16[128,4,128]{2,1,0:T(4,128)(2,1)S(1)}, u32[]{:S(2)}, u32[]{:S(2)}) %all-to-all-start) | async-done | bytes 131104 | tf_op jit(solution)/shard_map/all_to_all | solution.py:149
  29.1 0.0 copy-start.4
  29.1 0.7 copy-done.4
  29.8 2.5 %shard_map.77 = (bf16[128,128]{1,0:T(8,128)(2,1)S(1)}, bf16[128,128]{1,0:T(8,128)(2,1)S(1)}, f32[4,32,128]{2,1,0:T(8,128)S(1)}) custom-call(s32[1]{0:T(128)} %bitcast.refs_0_, f32[128]{0:T(128)S(1)} %copy-done.4, bf16[512,128]{1,0:T(8,128)(2,1)S(1)} %bitcast.10), custom_call_target="tpu_custom_call" | custom-call | tf_op jit(solution)/shard_map/pallas_call | solution.py:151
  32.3 23.6 %all_to_all.27.refs_2_ = f32[4,32,128]{2,1,0:T(8,128)S(1)} all-to-all(f32[4,32,128]{2,1,0:T(8,128)S(1)} %get-tuple-element.11), channel_id=1, replica_groups=mesh['far'=4,'near'=4,'seq'=32] {'far'}, dimensions={0} | all-to-all | bytes 131072 | tf_op jit(solution)/shard_map/all_to_all | solution.py:163
  55.9 18.3 %all_to_all.28 = bf16[128,4,128]{2,1,0:T(4,128)(2,1)S(1)} all-to-all(bf16[128,4,128]{2,1,0:T(4,128)(2,1)S(1)} %bitcast.12), channel_id=1, replica_groups=mesh['far'=4,'near'=4,'seq'=32] {'near','seq'}, dimensions={0} | all-to-all | bytes 262144 | tf_op jit(solution)/shard_map/all_to_all | solution.py:172
  74.2 0.7 shard_map.79
  (1 shorter events, 0.0 us)
Async XLA Ops:
  0.6 0.8 %copy-start = (bf16[1,128,128]{2,1,0:T(8,128)(2,1)S(1)}, bf16[1,128,128]{2,1,0:T(8,128)(2,1)}, u32[]{:S(2)}) copy-start(bf16[1,128,128]{2,1,0:T(8,128)(2,1)} %param.5) | copy-start | bytes 98308
  1.4 0.8 %copy-start.1 = (bf16[1,128,128]{2,1,0:T(8,128)(2,1)S(1)}, bf16[1,128,128]{2,1,0:T(8,128)(2,1)}, u32[]{:S(2)}) copy-start(bf16[1,128,128]{2,1,0:T(8,128)(2,1)} %param.6) | copy-start | bytes 98308
  2.1 0.8 %copy-start.2 = (bf16[1,128,128]{2,1,0:T(8,128)(2,1)S(1)}, bf16[1,128,128]{2,1,0:T(8,128)(2,1)}, u32[]{:S(2)}) copy-start(bf16[1,128,128]{2,1,0:T(8,128)(2,1)} %param.7) | copy-start | bytes 98308
  2.9 0.8 %copy-start.3 = (bf16[128,128]{1,0:T(8,128)(2,1)S(1)}, bf16[128,128]{1,0:T(8,128)(2,1)}, u32[]{:S(2)}) copy-start(bf16[128,128]{1,0:T(8,128)(2,1)} %k_ref.1) | copy-start | bytes 98308
  4.4 24.8 %all-to-all-start = ((bf16[128,4,128]{2,1,0:T(4,128)(2,1)}), bf16[128,4,128]{2,1,0:T(4,128)(2,1)S(1)}, u32[]{:S(2)}, u32[]{:S(2)}) async-start(bf16[128,4,128]{2,1,0:T(4,128)(2,1)} %bitcast.4), calls=%async_computation | async-start | bytes 262144 | tf_op jit(solution)/shard_map/all_to_all | solution.py:149
  29.1 0.7 copy-start.4

commit v2 on v1

v2 whole, which is shorter than its diff:
```python
import jax
import jax.numpy as jnp
from jax import lax
from jax.experimental import pallas as pl
from jax.experimental.pallas import tpu as pltpu
from jax.sharding import Mesh, PartitionSpec as P

LANES = 128
GROUP = 4
ROLES = 4

F32 = jnp.float32
BF16 = jnp.bfloat16


def iota(shape, dim):
    return lax.broadcasted_iota(jnp.int32, shape, dim)


def pack_kernel(u_ref, g_ref, y_ref, k_ref, out_ref, landed, rows, sems):
    chans = out_ref.shape[0] // ROLES
    copies = [
        pltpu.make_async_copy(ref, landed.at[role], sems.at[role])
        for role, ref in enumerate((u_ref, g_ref, y_ref, k_ref))
    ]
    for copy in copies:
        copy.start()
    for role, copy in enumerate(copies):
        copy.wait()
        rows[pl.ds(role, chans, stride=ROLES), :] = landed[role].astype(F32)
    out_ref[...] = rows[...].astype(BF16)


def flip_rows(count, span):
    row, col = iota((count, count), 0), iota((count, count), 1)
    same = row // span == col // span
    return jnp.where(same & (row % span + col % span == span - 1), 1.0, 0.0).astype(BF16)


def take(rows, role, count):
    return rows[pl.ds(role, count, stride=ROLES), :]


def flipped_pair(gc, flip, lane_flip):
    high = gc.astype(BF16)
    low = (gc - high.astype(F32)).astype(BF16)
    both = jnp.concatenate([high, low], axis=0)
    both = jnp.dot(both, lane_flip, preferred_element_type=F32).astype(BF16)
    return jnp.dot(flip, both, preferred_element_type=F32)


def pad(padded, value, blocks):
    for part in range(padded.shape[0]):
        padded[part, :blocks, :] = jnp.zeros((blocks, LANES), F32)
        padded[part, blocks:, :] = value[part * blocks : (part + 1) * blocks]


def shifted(padded, d, blocks):
    parts = [padded[part, blocks - d : 2 * blocks - d, :] for part in range(padded.shape[0])]
    return jnp.concatenate(parts, axis=0).astype(BF16)


def skew(value):
    return pltpu.roll(value, 0, 1, stride=1, stride_axis=0)


def filt_kernel(blocks, in_ref, filt_ref, rows, padded, filt_rows):
    count = GROUP * blocks
    rows[...] = in_ref[...].astype(F32)
    u = take(rows, 0, count)
    gc = take(rows, 1, count) * take(rows, 2, count)
    lane_flip = flip_rows(LANES, LANES)
    flip = flip_rows(2 * count, blocks)
    pad(padded, flipped_pair(gc, flip, lane_flip), blocks)
    turned_u = jnp.dot(flip[:count, :count], u.astype(BF16), preferred_element_type=F32)
    left = jnp.transpose(turned_u).astype(BF16)
    left = jnp.concatenate([left, left], axis=1)
    inside = iota((LANES, LANES), 1) >= iota((LANES, LANES), 0)
    held = None
    for pair in range(blocks // 2):
        wide = jnp.concatenate([shifted(padded, 2 * pair, blocks), shifted(padded, 2 * pair + 1, blocks)], axis=1)
        products = jnp.dot(left, wide, preferred_element_type=F32)
        for half in range(2):
            d = 2 * pair + half
            turned = skew(products[:, half * LANES : (half + 1) * LANES])
            if held is not None:
                filt_rows[d - 1 : d, :] = jnp.sum(jnp.where(inside, held, turned), axis=0, keepdims=True)
            held = turned
    filt_rows[blocks - 1 : blocks, :] = jnp.sum(jnp.where(inside, held, 0.0), axis=0, keepdims=True)
    filt_ref[...] = jnp.dot(
        filt_rows[...], lane_flip.astype(F32), precision=lax.Precision.HIGHEST, preferred_element_type=F32
    )


def conv_kernel(blocks, chan_ref, gain_ref, in_ref, gate_ref, input_ref, rows, padded, gains, sem):
    count = GROUP * blocks
    fetch = pltpu.make_async_copy(gain_ref, gains, sem)
    fetch.start()
    rows[...] = in_ref[...].astype(F32)
    u = take(rows, 0, count)
    y = take(rows, 2, count)
    gc = take(rows, 1, count) * y
    k = take(rows, 3, blocks)
    lane_flip = flip_rows(LANES, LANES)
    flip = flip_rows(2 * count, blocks)
    both = flipped_pair(gc, flip, lane_flip)
    pad(padded, jnp.concatenate([u, both], axis=0), blocks)
    inside = iota((LANES, LANES), 1) >= iota((LANES, LANES), 0)
    before = jnp.zeros((LANES, LANES), F32)
    total = jnp.zeros((3 * count, LANES), F32)
    for pair in range(blocks // 2):
        signal, toeplitz = [], []
        for d in (2 * pair, 2 * pair + 1):
            signal.append(shifted(padded, d, blocks))
            rolled = skew(jnp.broadcast_to(k[d : d + 1, :], (LANES, LANES)))
            toeplitz.append(jnp.where(inside, rolled, before).astype(BF16))
            before = rolled
        total = total + jnp.dot(
            jnp.concatenate(signal, axis=1), jnp.concatenate(toeplitz, axis=0), preferred_element_type=F32
        )
    scale = 1.0 / 64.0
    fetch.wait()
    gain = gains[chan_ref[0]]
    gate_ref[...] = (y * (total[:count] * scale + gain * u)).astype(BF16)
    corr = total[count : 2 * count] + total[2 * count :]
    d_input = (corr * scale + gain * (both[:count] + both[count:])).astype(BF16)
    d_input = jnp.dot(d_input, lane_flip, preferred_element_type=F32).astype(BF16)
    input_ref[...] = jnp.dot(flip[:count, :count], d_input, preferred_element_type=F32).astype(BF16)


def spread_kernel(blocks, gate_ref, input_ref, near_ref, far_ref, out_ref, rows):
    count = GROUP * blocks
    filt = near_ref[...] + far_ref[...]
    high = filt.astype(BF16).astype(F32)
    low = filt - high
    rows[pl.ds(0, count, stride=ROLES), :] = gate_ref[...].astype(F32)
    rows[pl.ds(1, count, stride=ROLES), :] = input_ref[...].astype(F32)
    for part in range(GROUP):
        at = part * blocks * ROLES
        rows[pl.ds(at + 2, blocks, stride=ROLES), :] = high
        rows[pl.ds(at + 3, blocks, stride=ROLES), :] = low
    out_ref[...] = rows[...].astype(BF16)


def unpack_kernel(in_ref, input_ref, gate_ref, filt_ref, rows):
    chans = input_ref.shape[0]
    rows[...] = in_ref[...].astype(F32)
    gate_ref[...] = take(rows, 0, chans).astype(BF16)
    input_ref[...] = take(rows, 1, chans).astype(BF16)
    filt_ref[...] = (take(rows, 2, chans) + take(rows, 3, chans)) * (1.0 / 64.0)


VMEM = pl.BlockSpec(memory_space=pltpu.VMEM)
SMEM = pl.BlockSpec(memory_space=pltpu.SMEM)


def shape(dims, dtype):
    return jax.ShapeDtypeStruct(dims, dtype)


HBM = pl.BlockSpec(memory_space=pltpu.HBM)


def call(kernel, outs, ins, scratch, limit=48):
    return pl.pallas_call(
        kernel,
        out_shape=outs,
        in_specs=ins,
        out_specs=jax.tree.map(lambda _: VMEM, outs),
        scratch_shapes=scratch,
        compiler_params=pltpu.CompilerParams(vmem_limit_bytes=limit * 1024 * 1024),
    )


def body(inputs, gate_values, grad_out, filter_raw, skip_gain):
    blocks = lax.axis_size("seq")
    far = lax.axis_size("far")
    chans = inputs.shape[1]
    count = GROUP * blocks
    rows = pltpu.VMEM((count * ROLES, LANES), F32)
    packed = call(
        pack_kernel,
        shape((chans * ROLES, LANES), BF16),
        [HBM] * 4,
        [
            pltpu.VMEM((ROLES, chans, LANES), BF16),
            pltpu.VMEM((chans * ROLES, LANES), F32),
            pltpu.SemaphoreType.DMA((ROLES,)),
        ],
        60,
    )(inputs[0], gate_values[0], grad_out[0], filter_raw)
    packed = lax.all_to_all(packed, ("near", "seq"), 0, 0, tiled=True)
    filt = call(
        lambda *refs: filt_kernel(blocks, *refs),
        shape((blocks, LANES), F32),
        [VMEM],
        [rows, pltpu.VMEM((2 * GROUP, 2 * blocks, LANES), F32), pltpu.VMEM((blocks, LANES), F32)],
    )(packed)
    opposite = lax.ppermute(filt, "far", [(i, i ^ 2) for i in range(far)])
    chan = (lax.axis_index("near") * blocks + lax.axis_index("seq")).reshape(1)
    gate, d_in = call(
        lambda *refs: conv_kernel(blocks, *refs),
        (shape((count, LANES), BF16), shape((count, LANES), BF16)),
        [SMEM, HBM, VMEM],
        [
            rows,
            pltpu.VMEM((3 * GROUP, 2 * blocks, LANES), F32),
            pltpu.SMEM(skip_gain.shape, F32),
            pltpu.SemaphoreType.DMA(()),
        ],
    )(chan, skip_gain, packed)
    filt = filt + opposite
    beside = lax.ppermute(filt, "far", [(i, i ^ 1) for i in range(far)])
    packed = call(
        lambda *refs: spread_kernel(blocks, *refs),
        shape((count * ROLES, LANES), BF16),
        [VMEM] * 4,
        [rows],
    )(gate, d_in, filt, beside)
    packed = lax.all_to_all(packed, ("near", "seq"), 0, 0, tiled=True)
    d_input, d_gate, d_filter = call(
        unpack_kernel,
        (shape((chans, LANES), BF16), shape((chans, LANES), BF16), shape((chans, LANES), F32)),
        [VMEM],
        [pltpu.VMEM((chans * ROLES, LANES), F32)],
    )(packed)
    return d_input[None], d_gate[None], d_filter


def solution(mesh):
    sizes = mesh.devices.shape
    mesh = Mesh(mesh.devices.reshape(sizes[0] // GROUP, GROUP, sizes[1]), ("far", "near", "seq"))
    signal = P(("far", "near"), None, "seq")
    return jax.shard_map(
        body,
        mesh=mesh,
        in_specs=(signal, signal, signal, P(None, "seq"), P()),
        out_specs=(signal, signal, P(None, "seq")),
        check_vma=False,
    )
```

time: 75.4 us -> 71.2 us (0.944)
  waiting for transfers between devices: 10.9 us -> 1.12 us
  starting transfers between devices: 13.8 us -> 20.9 us
  local copies, waits for them, and re-layouts: 3.68 us -> 0.65 us
  Pallas kernels: 3.89 us -> 5.12 us
    all_to_all x1 -> x2, blocking collectives: 18.3 us -> 42.4 us  [body(): packed = lax.all_to_all(packed, ('near', 'seq'), 0, 0, tiled=True)]
    all_to_all x1 -> x0, blocking collectives: 23.6 us -> none  [body(): filt = lax.all_to_all(filt, 'far', 0, 0, tiled=True)]
    ppermute x0 -> x2, starting transfers between devices: none -> 20.9 us  [the longest x1 12.8 us: body(): opposite = lax.ppermute(filt, 'far', [(i, i ^ 2) for i in range(far)])]
    all_to_all x1 -> x0, starting transfers between devices: 13.8 us -> none  [body(): packed = lax.all_to_all(packed, ('near', 'seq'), 0, 0, tiled=True)]
    all_to_all x1 -> x0, waiting for transfers between devices: 10.9 us -> none  [body(): packed = lax.all_to_all(packed, ('near', 'seq'), 0, 0, tiled=True)]
    unnamed x10 -> x2, local copies, waits for them, and re-layouts: 3.68 us -> 0.65 us
    pallas_call x4 -> x5, Pallas kernels: 3.89 us -> 5.12 us  [the longest x1 1.57 us: body(): call(lambda *refs: conv_kernel(blocks, *refs), (shape((count, LANES), BF1...]
    ppermute x0 -> x2, waiting for transfers between devices: none -> 1.12 us  [the longest x1 1.11 us: body(): opposite = lax.ppermute(filt, 'far', [(i, i ^ 2) for i in range(far)])]
  transfers between devices with their start and end apart: 1 -> 2, of which waited for: 1 -> 1; matrix products, arithmetic and copies ran while one was open for 0% -> 0% of each run, Pallas kernels for 0% -> 2%
where the time goes in v2:
time: 71.2 us; the launch traced here: 70.9 us
  blocking collectives  42.4 us (60%)
  starting transfers between devices  20.9 us (29%)
  Pallas kernels  5.12 us (7%)
  waiting for transfers between devices  1.12 us (2%)
    all_to_all x2, blocking collectives, body(): packed = lax.all_to_all(packed, ('near', 'seq'), 0, 0, tiled=True)  42.4 us
    ppermute x1, starting transfers between devices, body(): opposite = lax.ppermute(filt, 'far', [(i, i ^ 2) for i in range(far)])  12.8 us
    ppermute x1, starting transfers between devices, body(): beside = lax.ppermute(filt, 'far', [(i, i ^ 1) for i in range(far)])  8.14 us
    pallas_call x1, Pallas kernels, body(): call(lambda *refs: conv_kernel(blocks, *refs), (shape((count, LANES), BF1...  1.57 us
    pallas_call x1, Pallas kernels, body(): call(pack_kernel, shape((chans * ROLES, LANES), BF16), [HBM] * 4, [pltpu....  1.51 us
  transfers between devices with their start and end apart: 2, of which 1 were waited for; matrix products, arithmetic and copies ran while one was open for 0% of the time, Pallas kernels for 2%

profile of v2, /device:TPU:1, one launch (start us, length us, event | category | flops | bytes accessed | tf_op | source)
XLA Modules:
  0.0 70.9 jit_solution(5659050398793869856)
XLA Ops:
  0.6 1.5 %shard_map.76 = bf16[512,128]{1,0:T(8,128)(2,1)} custom-call(bf16[128,128]{1,0:T(8,128)(2,1)} %bitcast.15, bf16[128,128]{1,0:T(8,128)(2,1)} %bitcast.16, bf16[128,128]{1,0:T(8,128)(2,1)} %bitcast.17, bf16[128,128]{1,0:T(8,128)(2,1)} %k_ref.1), custom_call_target="tpu_custom_call" | custom-call | tf_op jit(solution)/shard_map/pallas_call | solution.py:181
  2.2 24.8 %all_to_all.22 = bf16[128,4,128]{2,1,0:T(4,128)(2,1)S(1)} all-to-all(bf16[128,4,128]{2,1,0:T(4,128)(2,1)} %bitcast.14), channel_id=1, replica_groups=mesh['far'=4,'near'=4,'seq'=32] {'near','seq'}, dimensions={0} | all-to-all | bytes 262144 | tf_op jit(solution)/shard_map/all_to_all | solution.py:192
  26.9 1.3 %shard_map.78 = f32[32,128]{1,0:T(8,128)S(1)} custom-call(bf16[512,128]{1,0:T(8,128)(2,1)S(1)} %bitcast.10), custom_call_target="tpu_custom_call" | custom-call | tf_op jit(solution)/shard_map/pallas_call | solution.py:193
  28.3 12.8 %collective-permute-start = (f32[32,128]{1,0:T(8,128)S(1)}, f32[32,128]{1,0:T(8,128)S(1)}, u32[]{:S(2)}, u32[]{:S(2)}) collective-permute-start(f32[32,128]{1,0:T(8,128)S(1)} %shard_map.78), channel_id=1, source_target_pairs={{0,256},{128,384},{256,0},{384,128},{1,257},{129,385},{257,1},{385... | collective-permute-start | bytes 49160 | tf_op jit(solution)/shard_map/ppermute | solution.py:199
  41.1 1.1 %collective-permute-done = f32[32,128]{1,0:T(8,128)S(1)} collective-permute-done((f32[32,128]{1,0:T(8,128)S(1)}, f32[32,128]{1,0:T(8,128)S(1)}, u32[]{:S(2)}, u32[]{:S(2)}) %collective-permute-start) | collective-permute-done | bytes 16416 | tf_op jit(solution)/shard_map/ppermute | solution.py:199
  42.2 8.1 %collective-permute-start.1 = (f32[32,128]{1,0:T(8,128)S(1)}, f32[32,128]{1,0:T(8,128)S(1)}, u32[]{:S(2)}, u32[]{:S(2)}) collective-permute-start(f32[32,128]{1,0:T(8,128)S(1)} %add.7.refs_2_), channel_id=1, source_target_pairs={{0,128},{128,0},{256,384},{384,256},{1,129},{129,1},{257,385},{385... | collective-permute-start | bytes 49160 | tf_op jit(solution)/shard_map/ppermute | solution.py:213
  50.3 0.0 copy-start
  50.4 0.6 copy-done
  51.0 1.6 %shard_map.77 = (bf16[128,128]{1,0:T(8,128)(2,1)S(1)}, bf16[128,128]{1,0:T(8,128)(2,1)S(1)}) custom-call(s32[1]{0:T(128)} %bitcast.refs_0_, f32[128]{0:T(128)S(1)} %copy-done, bf16[512,128]{1,0:T(8,128)(2,1)S(1)} %bitcast.11), custom_call_target="tpu_custom_call" | custom-call | tf_op jit(solution)/shard_map/pallas_call | solution.py:201
  52.6 0.0 collective-permute-done.1.refs_3_
  52.6 17.6 %all_to_all.23 = bf16[128,4,128]{2,1,0:T(4,128)(2,1)S(1)} all-to-all(bf16[128,4,128]{2,1,0:T(4,128)(2,1)S(1)} %bitcast.12), channel_id=1, replica_groups=mesh['far'=4,'near'=4,'seq'=32] {'near','seq'}, dimensions={0} | all-to-all | bytes 262144 | tf_op jit(solution)/shard_map/all_to_all | solution.py:220
  70.2 0.7 shard_map.80
  (2 shorter events, 0.0 us)
Async XLA Ops:
  28.3 13.9 %collective-permute-start = (f32[32,128]{1,0:T(8,128)S(1)}, f32[32,128]{1,0:T(8,128)S(1)}, u32[]{:S(2)}, u32[]{:S(2)}) collective-permute-start(f32[32,128]{1,0:T(8,128)S(1)} %shard_map.78), channel_id=1, source_target_pairs={{0,256},{128,384},{256,0},{384,128},{1,257},{129,385},{257,1},{385... | collective-permute-start | bytes 49160 | tf_op jit(solution)/shard_map/ppermute | solution.py:199
  42.2 10.4 %collective-permute-start.1 = (f32[32,128]{1,0:T(8,128)S(1)}, f32[32,128]{1,0:T(8,128)S(1)}, u32[]{:S(2)}, u32[]{:S(2)}) collective-permute-start(f32[32,128]{1,0:T(8,128)S(1)} %add.7.refs_2_), channel_id=1, source_target_pairs={{0,128},{128,0},{256,384},{384,256},{1,129},{129,1},{257,385},{385... | collective-permute-start | bytes 49160 | tf_op jit(solution)/shard_map/ppermute | solution.py:213
  50.3 0.7 copy-start

commit v3 on v2

--- a/solution.py
+++ b/solution.py
@@ -196,7 +196,7 @@
         [VMEM],
         [rows, pltpu.VMEM((2 * GROUP, 2 * blocks, LANES), F32), pltpu.VMEM((blocks, LANES), F32)],
     )(packed)
-    opposite = lax.ppermute(filt, "far", [(i, i ^ 2) for i in range(far)])
+    around = lax.ppermute(filt, "far", [(i, i ^ 3) for i in range(far)])
     chan = (lax.axis_index("near") * blocks + lax.axis_index("seq")).reshape(1)
     gate, d_in = call(
         lambda *refs: conv_kernel(blocks, *refs),
@@ -209,7 +209,7 @@
             pltpu.SemaphoreType.DMA(()),
         ],
     )(chan, skip_gain, packed)
-    filt = filt + opposite
+    filt = filt + around
     beside = lax.ppermute(filt, "far", [(i, i ^ 1) for i in range(far)])
     packed = call(
         lambda *refs: spread_kernel(blocks, *refs),

time: 71.2 us -> 67.3 us (0.945)
  starting transfers between devices: 20.9 us -> 16.4 us
    ppermute x1, starting transfers between devices: 12.8 us -> 9.81 us  [body(): around = lax.ppermute(filt, 'far', [(i, i ^ 3) for i in range(far)])]
    ppermute x1, starting transfers between devices: 8.14 us -> 6.61 us  [body(): beside = lax.ppermute(filt, 'far', [(i, i ^ 1) for i in range(far)])]
where the time goes in v3:
time: 67.3 us; the launch traced here: 67 us
  blocking collectives  42.9 us (64%)
  starting transfers between devices  16.4 us (24%)
  Pallas kernels  5.12 us (8%)
  waiting for transfers between devices  1.12 us (2%)
  between operations  0.7 us (1%)
    all_to_all x2, blocking collectives, body(): packed = lax.all_to_all(packed, ('near', 'seq'), 0, 0, tiled=True)  42.9 us
    ppermute x1, starting transfers between devices, body(): around = lax.ppermute(filt, 'far', [(i, i ^ 3) for i in range(far)])  9.81 us
    ppermute x1, starting transfers between devices, body(): beside = lax.ppermute(filt, 'far', [(i, i ^ 1) for i in range(far)])  6.61 us
    pallas_call x1, Pallas kernels, body(): call(lambda *refs: conv_kernel(blocks, *refs), (shape((count, LANES), BF1...  1.57 us
    pallas_call x1, Pallas kernels, body(): call(pack_kernel, shape((chans * ROLES, LANES), BF16), [HBM] * 4, [pltpu....  1.51 us
  transfers between devices with their start and end apart: 2, of which 1 were waited for; matrix products, arithmetic and copies ran while one was open for 0% of the time, Pallas kernels for 2%

profile of v3, /device:TPU:1, one launch (start us, length us, event | category | flops | bytes accessed | tf_op | source)
XLA Modules:
  0.0 67.0 jit_solution(1477303129006140450)
XLA Ops:
  0.6 1.5 %shard_map.76 = bf16[512,128]{1,0:T(8,128)(2,1)} custom-call(bf16[128,128]{1,0:T(8,128)(2,1)} %bitcast.15, bf16[128,128]{1,0:T(8,128)(2,1)} %bitcast.16, bf16[128,128]{1,0:T(8,128)(2,1)} %bitcast.17, bf16[128,128]{1,0:T(8,128)(2,1)} %k_ref.1), custom_call_target="tpu_custom_call" | custom-call | tf_op jit(solution)/shard_map/pallas_call | solution.py:181
  2.2 24.8 %all_to_all.22 = bf16[128,4,128]{2,1,0:T(4,128)(2,1)S(1)} all-to-all(bf16[128,4,128]{2,1,0:T(4,128)(2,1)} %bitcast.14), channel_id=1, replica_groups=mesh['far'=4,'near'=4,'seq'=32] {'near','seq'}, dimensions={0} | all-to-all | bytes 262144 | tf_op jit(solution)/shard_map/all_to_all | solution.py:192
  26.9 1.3 %shard_map.78 = f32[32,128]{1,0:T(8,128)S(1)} custom-call(bf16[512,128]{1,0:T(8,128)(2,1)S(1)} %bitcast.10), custom_call_target="tpu_custom_call" | custom-call | tf_op jit(solution)/shard_map/pallas_call | solution.py:193
  28.3 9.8 %collective-permute-start = (f32[32,128]{1,0:T(8,128)S(1)}, f32[32,128]{1,0:T(8,128)S(1)}, u32[]{:S(2)}, u32[]{:S(2)}) collective-permute-start(f32[32,128]{1,0:T(8,128)S(1)} %shard_map.78), channel_id=1, source_target_pairs={{0,384},{128,256},{256,128},{384,0},{1,385},{129,257},{257,129},{3... | collective-permute-start | bytes 49160 | tf_op jit(solution)/shard_map/ppermute | solution.py:199
  38.1 1.1 %collective-permute-done = f32[32,128]{1,0:T(8,128)S(1)} collective-permute-done((f32[32,128]{1,0:T(8,128)S(1)}, f32[32,128]{1,0:T(8,128)S(1)}, u32[]{:S(2)}, u32[]{:S(2)}) %collective-permute-start) | collective-permute-done | bytes 16416 | tf_op jit(solution)/shard_map/ppermute | solution.py:199
  39.2 6.6 %collective-permute-start.1 = (f32[32,128]{1,0:T(8,128)S(1)}, f32[32,128]{1,0:T(8,128)S(1)}, u32[]{:S(2)}, u32[]{:S(2)}) collective-permute-start(f32[32,128]{1,0:T(8,128)S(1)} %add.7.refs_2_), channel_id=1, source_target_pairs={{0,128},{128,0},{256,384},{384,256},{1,129},{129,1},{257,385},{385... | collective-permute-start | bytes 49160 | tf_op jit(solution)/shard_map/ppermute | solution.py:213
  45.8 0.0 copy-start
  45.8 0.6 copy-done
  46.5 1.6 %shard_map.77 = (bf16[128,128]{1,0:T(8,128)(2,1)S(1)}, bf16[128,128]{1,0:T(8,128)(2,1)S(1)}) custom-call(s32[1]{0:T(128)} %bitcast.refs_0_, f32[128]{0:T(128)S(1)} %copy-done, bf16[512,128]{1,0:T(8,128)(2,1)S(1)} %bitcast.11), custom_call_target="tpu_custom_call" | custom-call | tf_op jit(solution)/shard_map/pallas_call | solution.py:201
  48.1 0.0 collective-permute-done.1.refs_3_
  48.1 18.2 %all_to_all.23 = bf16[128,4,128]{2,1,0:T(4,128)(2,1)S(1)} all-to-all(bf16[128,4,128]{2,1,0:T(4,128)(2,1)S(1)} %bitcast.12), channel_id=1, replica_groups=mesh['far'=4,'near'=4,'seq'=32] {'near','seq'}, dimensions={0} | all-to-all | bytes 262144 | tf_op jit(solution)/shard_map/all_to_all | solution.py:220
  66.3 0.7 %shard_map.80 = (bf16[128,128]{1,0:T(8,128)(2,1)}, bf16[128,128]{1,0:T(8,128)(2,1)}, f32[128,128]{1,0:T(8,128)}) custom-call(bf16[512,128]{1,0:T(8,128)(2,1)S(1)} %bitcast.13), custom_call_target="tpu_custom_call" | custom-call | tf_op jit(solution)/shard_map/pallas_call | solution.py:221
  (2 shorter events, 0.0 us)
Async XLA Ops:
  28.3 10.9 %collective-permute-start = (f32[32,128]{1,0:T(8,128)S(1)}, f32[32,128]{1,0:T(8,128)S(1)}, u32[]{:S(2)}, u32[]{:S(2)}) collective-permute-start(f32[32,128]{1,0:T(8,128)S(1)} %shard_map.78), channel_id=1, source_target_pairs={{0,384},{128,256},{256,128},{384,0},{1,385},{129,257},{257,129},{3... | collective-permute-start | bytes 49160 | tf_op jit(solution)/shard_map/ppermute | solution.py:199
  39.2 8.9 %collective-permute-start.1 = (f32[32,128]{1,0:T(8,128)S(1)}, f32[32,128]{1,0:T(8,128)S(1)}, u32[]{:S(2)}, u32[]{:S(2)}) collective-permute-start(f32[32,128]{1,0:T(8,128)S(1)} %add.7.refs_2_), channel_id=1, source_target_pairs={{0,128},{128,0},{256,384},{384,256},{1,129},{129,1},{257,385},{385... | collective-permute-start | bytes 49160 | tf_op jit(solution)/shard_map/ppermute | solution.py:213
  45.8 0.7 copy-start

commit v4 on v3

--- a/solution.py
+++ b/solution.py
@@ -64,32 +64,37 @@
     return pltpu.roll(value, 0, 1, stride=1, stride_axis=0)
 
 
-def filt_kernel(blocks, in_ref, filt_ref, rows, padded, filt_rows):
+def filt_kernel(blocks, in_ref, filt_ref, rows, padded):
     count = GROUP * blocks
     rows[...] = in_ref[...].astype(F32)
     u = take(rows, 0, count)
     gc = take(rows, 1, count) * take(rows, 2, count)
-    lane_flip = flip_rows(LANES, LANES)
-    flip = flip_rows(2 * count, blocks)
-    pad(padded, flipped_pair(gc, flip, lane_flip), blocks)
-    turned_u = jnp.dot(flip[:count, :count], u.astype(BF16), preferred_element_type=F32)
-    left = jnp.transpose(turned_u).astype(BF16)
+    high = gc.astype(BF16).astype(F32)
+    low = gc - high
+    for part in range(2 * GROUP):
+        value = high if part < GROUP else low
+        at = part % GROUP * blocks
+        padded[part, :blocks, :] = value[at : at + blocks]
+        padded[part, blocks:, :] = jnp.zeros((blocks, LANES), F32)
+    left = lax.dot_general(
+        flip_rows(LANES, LANES), u.astype(BF16), (((1,), (1,)), ((), ())), preferred_element_type=F32
+    ).astype(BF16)
     left = jnp.concatenate([left, left], axis=1)
-    inside = iota((LANES, LANES), 1) >= iota((LANES, LANES), 0)
+    wrapped = iota((LANES, LANES), 1) <= iota((LANES, LANES), 0)
     held = None
     for pair in range(blocks // 2):
-        wide = jnp.concatenate([shifted(padded, 2 * pair, blocks), shifted(padded, 2 * pair + 1, blocks)], axis=1)
-        products = jnp.dot(left, wide, preferred_element_type=F32)
+        wide = []
+        for d in (2 * pair, 2 * pair + 1):
+            parts = [padded[part, d : d + blocks, :] for part in range(2 * GROUP)]
+            wide.append(jnp.concatenate(parts, axis=0).astype(BF16))
+        products = jnp.dot(left, jnp.concatenate(wide, axis=1), preferred_element_type=F32)
         for half in range(2):
             d = 2 * pair + half
-            turned = skew(products[:, half * LANES : (half + 1) * LANES])
+            turned = pltpu.roll(products[:, half * LANES : (half + 1) * LANES], 1, 1, stride=1, stride_axis=0)
             if held is not None:
-                filt_rows[d - 1 : d, :] = jnp.sum(jnp.where(inside, held, turned), axis=0, keepdims=True)
+                filt_ref[d - 1 : d, :] = jnp.sum(jnp.where(wrapped, held, turned), axis=0, keepdims=True)
             held = turned
-    filt_rows[blocks - 1 : blocks, :] = jnp.sum(jnp.where(inside, held, 0.0), axis=0, keepdims=True)
-    filt_ref[...] = jnp.dot(
-        filt_rows[...], lane_flip.astype(F32), precision=lax.Precision.HIGHEST, preferred_element_type=F32
-    )
+    filt_ref[blocks - 1 : blocks, :] = jnp.sum(jnp.where(wrapped, held, 0.0), axis=0, keepdims=True)
 
 
 def conv_kernel(blocks, chan_ref, gain_ref, in_ref, gate_ref, input_ref, rows, padded, gains, sem):
@@ -161,14 +166,18 @@
 HBM = pl.BlockSpec(memory_space=pltpu.HBM)
 
 
-def call(kernel, outs, ins, scratch, limit=48):
+def in_hbm(array):
+    return pltpu.with_memory_space_constraint(array, pltpu.HBM)
+
+
+def call(kernel, outs, ins, scratch):
     return pl.pallas_call(
         kernel,
         out_shape=outs,
         in_specs=ins,
         out_specs=jax.tree.map(lambda _: VMEM, outs),
         scratch_shapes=scratch,
-        compiler_params=pltpu.CompilerParams(vmem_limit_bytes=limit * 1024 * 1024),
+        compiler_params=pltpu.CompilerParams(vmem_limit_bytes=48 * 1024 * 1024),
     )
 
 
@@ -187,14 +196,13 @@
             pltpu.VMEM((chans * ROLES, LANES), F32),
             pltpu.SemaphoreType.DMA((ROLES,)),
         ],
-        60,
-    )(inputs[0], gate_values[0], grad_out[0], filter_raw)
+    )(*map(in_hbm, (inputs[0], gate_values[0], grad_out[0], filter_raw)))
     packed = lax.all_to_all(packed, ("near", "seq"), 0, 0, tiled=True)
     filt = call(
         lambda *refs: filt_kernel(blocks, *refs),
         shape((blocks, LANES), F32),
         [VMEM],
-        [rows, pltpu.VMEM((2 * GROUP, 2 * blocks, LANES), F32), pltpu.VMEM((blocks, LANES), F32)],
+        [rows, pltpu.VMEM((2 * GROUP, 2 * blocks, LANES), F32)],
     )(packed)
     around = lax.ppermute(filt, "far", [(i, i ^ 3) for i in range(far)])
     chan = (lax.axis_index("near") * blocks + lax.axis_index("seq")).reshape(1)
@@ -208,7 +216,7 @@
             pltpu.SMEM(skip_gain.shape, F32),
             pltpu.SemaphoreType.DMA(()),
         ],
-    )(chan, skip_gain, packed)
+    )(chan, in_hbm(skip_gain), packed)
     filt = filt + around
     beside = lax.ppermute(filt, "far", [(i, i ^ 1) for i in range(far)])
     packed = call(

time: 67.3 us -> 66 us (0.981)
  Pallas kernels: 5.12 us -> 4.13 us
  transfers between devices with their start and end apart: 2 -> 2, of which waited for: 1 -> 2; matrix products, arithmetic and copies ran while one was open for 0% -> 0% of each run, Pallas kernels for 2% -> 2%
where the time goes in v4:
time: 66 us; the launch traced here: 65.7 us
  blocking collectives  43 us (65%)
  starting transfers between devices  16.3 us (25%)
  Pallas kernels  4.13 us (6%)
  waiting for transfers between devices  1.59 us (2%)
  between operations  0.68 us (1%)
    all_to_all x2, blocking collectives, body(): packed = lax.all_to_all(packed, ('near', 'seq'), 0, 0, tiled=True)  43 us
    ppermute x1, starting transfers between devices, body(): around = lax.ppermute(filt, 'far', [(i, i ^ 3) for i in range(far)])  9.76 us
    ppermute x1, starting transfers between devices, body(): beside = lax.ppermute(filt, 'far', [(i, i ^ 1) for i in range(far)])  6.59 us
    pallas_call x1, Pallas kernels, body(): call(lambda *refs: conv_kernel(blocks, *refs), (shape((count, LANES), BF1...  1.57 us
  transfers between devices with their start and end apart: 2, of which 2 were waited for; matrix products, arithmetic and copies ran while one was open for 0% of the time, Pallas kernels for 2%

profile of v4, /device:TPU:1, one launch (start us, length us, event | category | flops | bytes accessed | tf_op | source)
XLA Modules:
  0.0 65.7 jit_solution(12885777660060042642)
XLA Ops:
  0.6 0.9 %shard_map.76 = bf16[512,128]{1,0:T(8,128)(2,1)S(1)} custom-call(bf16[128,128]{1,0:T(8,128)(2,1)} %bitcast.15, bf16[128,128]{1,0:T(8,128)(2,1)} %bitcast.16, bf16[128,128]{1,0:T(8,128)(2,1)} %bitcast.17, bf16[128,128]{1,0:T(8,128)(2,1)} %k_ref.1), custom_call_target="tpu_custom_call" | custom-call | tf_op jit(solution)/shard_map/pallas_call | solution.py:190
  1.5 24.6 %all_to_all.22 = bf16[128,4,128]{2,1,0:T(4,128)(2,1)S(1)} all-to-all(bf16[128,4,128]{2,1,0:T(4,128)(2,1)S(1)} %bitcast.14), channel_id=1, replica_groups=mesh['far'=4,'near'=4,'seq'=32] {'near','seq'}, dimensions={0} | all-to-all | bytes 262144 | tf_op jit(solution)/shard_map/all_to_all | solution.py:200
  26.1 1.0 %shard_map.78 = f32[32,128]{1,0:T(8,128)S(1)} custom-call(bf16[512,128]{1,0:T(8,128)(2,1)S(1)} %bitcast.10), custom_call_target="tpu_custom_call" | custom-call | tf_op jit(solution)/shard_map/pallas_call | solution.py:201
  27.1 9.8 %collective-permute-start = (f32[32,128]{1,0:T(8,128)S(1)}, f32[32,128]{1,0:T(8,128)S(1)}, u32[]{:S(2)}, u32[]{:S(2)}) collective-permute-start(f32[32,128]{1,0:T(8,128)S(1)} %shard_map.78), channel_id=1, source_target_pairs={{0,384},{128,256},{256,128},{384,0},{1,385},{129,257},{257,129},{3... | collective-permute-start | bytes 49160 | tf_op jit(solution)/shard_map/ppermute | solution.py:207
  36.8 1.1 %collective-permute-done = f32[32,128]{1,0:T(8,128)S(1)} collective-permute-done((f32[32,128]{1,0:T(8,128)S(1)}, f32[32,128]{1,0:T(8,128)S(1)}, u32[]{:S(2)}, u32[]{:S(2)}) %collective-permute-start) | collective-permute-done | bytes 16416 | tf_op jit(solution)/shard_map/ppermute | solution.py:207
  38.0 6.6 %collective-permute-start.1 = (f32[32,128]{1,0:T(8,128)S(1)}, f32[32,128]{1,0:T(8,128)S(1)}, u32[]{:S(2)}, u32[]{:S(2)}) collective-permute-start(f32[32,128]{1,0:T(8,128)S(1)} %add.7.refs_2_), channel_id=1, source_target_pairs={{0,128},{128,0},{256,384},{384,256},{1,129},{129,1},{257,385},{385... | collective-permute-start | bytes 49160 | tf_op jit(solution)/shard_map/ppermute | solution.py:221
  44.6 1.6 %shard_map.77 = (bf16[128,128]{1,0:T(8,128)(2,1)S(1)}, bf16[128,128]{1,0:T(8,128)(2,1)S(1)}) custom-call(s32[1]{0:T(128)} %bitcast.refs_0_, f32[128]{0:T(128)} %refs_1_.1, bf16[512,128]{1,0:T(8,128)(2,1)S(1)} %bitcast.11), custom_call_target="tpu_custom_call" | custom-call | tf_op jit(solution)/shard_map/pallas_call | solution.py:209
  46.1 0.5 collective-permute-done.1.refs_3_
  46.7 18.4 %all_to_all.23 = bf16[128,4,128]{2,1,0:T(4,128)(2,1)S(1)} all-to-all(bf16[128,4,128]{2,1,0:T(4,128)(2,1)S(1)} %bitcast.12), channel_id=1, replica_groups=mesh['far'=4,'near'=4,'seq'=32] {'near','seq'}, dimensions={0} | all-to-all | bytes 262144 | tf_op jit(solution)/shard_map/all_to_all | solution.py:228
  65.0 0.7 %shard_map.80 = (bf16[128,128]{1,0:T(8,128)(2,1)}, bf16[128,128]{1,0:T(8,128)(2,1)}, f32[128,128]{1,0:T(8,128)}) custom-call(bf16[512,128]{1,0:T(8,128)(2,1)S(1)} %bitcast.13), custom_call_target="tpu_custom_call" | custom-call | tf_op jit(solution)/shard_map/pallas_call | solution.py:229
  (2 shorter events, 0.0 us)
Async XLA Ops:
  27.1 10.9 %collective-permute-start = (f32[32,128]{1,0:T(8,128)S(1)}, f32[32,128]{1,0:T(8,128)S(1)}, u32[]{:S(2)}, u32[]{:S(2)}) collective-permute-start(f32[32,128]{1,0:T(8,128)S(1)} %shard_map.78), channel_id=1, source_target_pairs={{0,384},{128,256},{256,128},{384,0},{1,385},{129,257},{257,129},{3... | collective-permute-start | bytes 49160 | tf_op jit(solution)/shard_map/ppermute | solution.py:207
  38.0 8.7 %collective-permute-start.1 = (f32[32,128]{1,0:T(8,128)S(1)}, f32[32,128]{1,0:T(8,128)S(1)}, u32[]{:S(2)}, u32[]{:S(2)}) collective-permute-start(f32[32,128]{1,0:T(8,128)S(1)} %add.7.refs_2_), channel_id=1, source_target_pairs={{0,128},{128,0},{256,384},{384,256},{1,129},{129,1},{257,385},{385... | collective-permute-start | bytes 49160 | tf_op jit(solution)/shard_map/ppermute | solution.py:221

commit v5 on v4

--- a/solution.py
+++ b/solution.py
@@ -17,7 +17,13 @@
     return lax.broadcasted_iota(jnp.int32, shape, dim)
 
 
-def pack_kernel(u_ref, g_ref, y_ref, k_ref, out_ref, landed, rows, sems):
+def swapped(value, odd):
+    up, down = jnp.roll(value, -1, axis=0), jnp.roll(value, 1, axis=0)
+    other = jnp.where(iota(value.shape, 0) % 2 == 0, up, down)
+    return jnp.where(odd, other, value)
+
+
+def pack_kernel(far_ref, u_ref, g_ref, y_ref, k_ref, out_ref, landed, rows, sems):
     chans = out_ref.shape[0] // ROLES
     copies = [
         pltpu.make_async_copy(ref, landed.at[role], sems.at[role])
@@ -25,9 +31,10 @@
     ]
     for copy in copies:
         copy.start()
+    odd = far_ref[0] % 2 == 1
     for role, copy in enumerate(copies):
         copy.wait()
-        rows[pl.ds(role, chans, stride=ROLES), :] = landed[role].astype(F32)
+        rows[pl.ds(role, chans, stride=ROLES), :] = swapped(landed[role].astype(F32), odd)
     out_ref[...] = rows[...].astype(BF16)
 
 
@@ -147,12 +154,13 @@
     out_ref[...] = rows[...].astype(BF16)
 
 
-def unpack_kernel(in_ref, input_ref, gate_ref, filt_ref, rows):
+def unpack_kernel(far_ref, in_ref, input_ref, gate_ref, filt_ref, rows):
     chans = input_ref.shape[0]
+    odd = far_ref[0] % 2 == 1
     rows[...] = in_ref[...].astype(F32)
-    gate_ref[...] = take(rows, 0, chans).astype(BF16)
-    input_ref[...] = take(rows, 1, chans).astype(BF16)
-    filt_ref[...] = (take(rows, 2, chans) + take(rows, 3, chans)) * (1.0 / 64.0)
+    gate_ref[...] = swapped(take(rows, 0, chans), odd).astype(BF16)
+    input_ref[...] = swapped(take(rows, 1, chans), odd).astype(BF16)
+    filt_ref[...] = swapped(take(rows, 2, chans) + take(rows, 3, chans), odd) * (1.0 / 64.0)
 
 
 VMEM = pl.BlockSpec(memory_space=pltpu.VMEM)
@@ -181,22 +189,28 @@
     )
 
 
+def exchange(array, step):
+    far, seq = lax.axis_size("far"), lax.axis_size("seq")
+    pairs = [(i * seq + j, (i ^ step) * seq + (j ^ 1)) for i in range(far) for j in range(seq)]
+    return lax.ppermute(array, ("far", "seq"), pairs)
+
+
 def body(inputs, gate_values, grad_out, filter_raw, skip_gain):
     blocks = lax.axis_size("seq")
-    far = lax.axis_size("far")
+    far = lax.axis_index("far").reshape(1)
     chans = inputs.shape[1]
     count = GROUP * blocks
     rows = pltpu.VMEM((count * ROLES, LANES), F32)
     packed = call(
         pack_kernel,
         shape((chans * ROLES, LANES), BF16),
-        [HBM] * 4,
+        [SMEM] + [HBM] * 4,
         [
             pltpu.VMEM((ROLES, chans, LANES), BF16),
             pltpu.VMEM((chans * ROLES, LANES), F32),
             pltpu.SemaphoreType.DMA((ROLES,)),
         ],
-    )(*map(in_hbm, (inputs[0], gate_values[0], grad_out[0], filter_raw)))
+    )(far, *map(in_hbm, (inputs[0], gate_values[0], grad_out[0], filter_raw)))
     packed = lax.all_to_all(packed, ("near", "seq"), 0, 0, tiled=True)
     filt = call(
         lambda *refs: filt_kernel(blocks, *refs),
@@ -204,8 +218,8 @@
         [VMEM],
         [rows, pltpu.VMEM((2 * GROUP, 2 * blocks, LANES), F32)],
     )(packed)
-    around = lax.ppermute(filt, "far", [(i, i ^ 3) for i in range(far)])
-    chan = (lax.axis_index("near") * blocks + lax.axis_index("seq")).reshape(1)
+    around = exchange(filt, 3)
+    chan = lax.axis_index("near") * blocks + (lax.axis_index("seq") ^ (far & 1))
     gate, d_in = call(
         lambda *refs: conv_kernel(blocks, *refs),
         (shape((count, LANES), BF16), shape((count, LANES), BF16)),
@@ -218,7 +232,7 @@
         ],
     )(chan, in_hbm(skip_gain), packed)
     filt = filt + around
-    beside = lax.ppermute(filt, "far", [(i, i ^ 1) for i in range(far)])
+    beside = exchange(filt, 1)
     packed = call(
         lambda *refs: spread_kernel(blocks, *refs),
         shape((count * ROLES, LANES), BF16),
@@ -229,9 +243,9 @@
     d_input, d_gate, d_filter = call(
         unpack_kernel,
         (shape((chans, LANES), BF16), shape((chans, LANES), BF16), shape((chans, LANES), F32)),
-        [VMEM],
+        [SMEM, VMEM],
         [pltpu.VMEM((chans * ROLES, LANES), F32)],
-    )(packed)
+    )(far, packed)
     return d_input[None], d_gate[None], d_filter
 
 

time: 66 us -> 65.7 us (level)
  blocking collectives: 43 us -> 40.6 us
  starting transfers between devices: 16.3 us -> 17.8 us
    all_to_all x2, blocking collectives: 43 us -> 40.6 us  [body(): packed = lax.all_to_all(packed, ('near', 'seq'), 0, 0, tiled=True)]
    ppermute x2, starting transfers between devices: 16.3 us -> 17.8 us  [exchange(): return lax.ppermute(array, ('far', 'seq'), pairs)]
where the time goes in v5:
time: 65.7 us; the launch traced here: 65.4 us
  blocking collectives  40.6 us (62%)
  starting transfers between devices  17.8 us (27%)
  Pallas kernels  4.19 us (6%)
  waiting for transfers between devices  2.11 us (3%)
  between operations  0.69 us (1%)
    all_to_all x2, blocking collectives, body(): packed = lax.all_to_all(packed, ('near', 'seq'), 0, 0, tiled=True)  40.6 us
    ppermute x2, starting transfers between devices, exchange(): return lax.ppermute(array, ('far', 'seq'), pairs)  17.8 us
    ppermute x2, waiting for transfers between devices, exchange(): return lax.ppermute(array, ('far', 'seq'), pairs)  2.11 us
    pallas_call x1, Pallas kernels, body(): call(lambda *refs: conv_kernel(blocks, *refs), (shape((count, LANES), BF1...  1.57 us
  transfers between devices with their start and end apart: 2, of which 2 were waited for; matrix products, arithmetic and copies ran while one was open for 0% of the time, Pallas kernels for 2%

profile of v5, /device:TPU:1, one launch (start us, length us, event | category | flops | bytes accessed | tf_op | source)
XLA Modules:
  0.0 65.4 jit_solution(13272415869709503951)
XLA Ops:
  0.6 0.9 %shard_map.76 = bf16[512,128]{1,0:T(8,128)(2,1)S(1)} custom-call(s32[1]{0:T(128)} %bitcast.far_ref, bf16[128,128]{1,0:T(8,128)(2,1)} %bitcast.17, bf16[128,128]{1,0:T(8,128)(2,1)} %bitcast.18, bf16[128,128]{1,0:T(8,128)(2,1)} %bitcast.19, bf16[128,128]{1,0:T(8,128)(2,1)} %k_ref.1), custom_call_target="tpu_custom_call" | custom-call | tf_op jit(solution)/shard_map/pallas_call | solution.py:204
  1.5 24.6 %all_to_all.22 = bf16[128,4,128]{2,1,0:T(4,128)(2,1)S(1)} all-to-all(bf16[128,4,128]{2,1,0:T(4,128)(2,1)S(1)} %bitcast.16), channel_id=1, replica_groups=mesh['far'=4,'near'=4,'seq'=32] {'near','seq'}, dimensions={0} | all-to-all | bytes 262144 | tf_op jit(solution)/shard_map/all_to_all | solution.py:214
  26.1 1.0 %shard_map.78 = f32[32,128]{1,0:T(8,128)S(1)} custom-call(bf16[512,128]{1,0:T(8,128)(2,1)S(1)} %bitcast.12), custom_call_target="tpu_custom_call" | custom-call | tf_op jit(solution)/shard_map/pallas_call | solution.py:215
  27.1 10.2 %collective-permute-start = (f32[32,128]{1,0:T(8,128)S(1)}, f32[32,128]{1,0:T(8,128)S(1)}, u32[]{:S(2)}, u32[]{:S(2)}) collective-permute-start(f32[32,128]{1,0:T(8,128)S(1)} %shard_map.78), channel_id=1, source_target_pairs={{0,385},{1,384},{2,387},{3,386},{4,389},{5,388},{6,391},{7,390},{8... | collective-permute-start | bytes 49160 | tf_op jit(solution)/shard_map/ppermute | solution.py:195
  37.3 1.4 %collective-permute-done = f32[32,128]{1,0:T(8,128)S(1)} collective-permute-done((f32[32,128]{1,0:T(8,128)S(1)}, f32[32,128]{1,0:T(8,128)S(1)}, u32[]{:S(2)}, u32[]{:S(2)}) %collective-permute-start) | collective-permute-done | bytes 16416 | tf_op jit(solution)/shard_map/ppermute | solution.py:195
  38.7 7.6 %collective-permute-start.1 = (f32[32,128]{1,0:T(8,128)S(1)}, f32[32,128]{1,0:T(8,128)S(1)}, u32[]{:S(2)}, u32[]{:S(2)}) collective-permute-start(f32[32,128]{1,0:T(8,128)S(1)} %add.11.refs_2_), channel_id=1, source_target_pairs={{0,129},{1,128},{2,131},{3,130},{4,133},{5,132},{6,135},{7,134},{8... | collective-permute-start | bytes 49160 | tf_op jit(solution)/shard_map/ppermute | solution.py:195
  46.4 1.6 %shard_map.77 = (bf16[128,128]{1,0:T(8,128)(2,1)S(1)}, bf16[128,128]{1,0:T(8,128)(2,1)S(1)}) custom-call(s32[1]{0:T(128)S(6)} %add.10.refs_0_, f32[128]{0:T(128)} %refs_1_.1, bf16[512,128]{1,0:T(8,128)(2,1)S(1)} %bitcast.13), custom_call_target="tpu_custom_call" | custom-call | tf_op jit(solution)/shard_map/pallas_call | solution.py:223
  47.9 0.7 %collective-permute-done.1.refs_3_ = f32[32,128]{1,0:T(8,128)S(1)} collective-permute-done((f32[32,128]{1,0:T(8,128)S(1)}, f32[32,128]{1,0:T(8,128)S(1)}, u32[]{:S(2)}, u32[]{:S(2)}) %collective-permute-start.1) | collective-permute-done | bytes 16416 | tf_op jit(solution)/shard_map/ppermute | solution.py:195
  48.7 16.0 %all_to_all.23 = bf16[128,4,128]{2,1,0:T(4,128)(2,1)S(1)} all-to-all(bf16[128,4,128]{2,1,0:T(4,128)(2,1)S(1)} %bitcast.14), channel_id=1, replica_groups=mesh['far'=4,'near'=4,'seq'=32] {'near','seq'}, dimensions={0} | all-to-all | bytes 262144 | tf_op jit(solution)/shard_map/all_to_all | solution.py:242
  64.7 0.7 %shard_map.80 = (bf16[128,128]{1,0:T(8,128)(2,1)}, bf16[128,128]{1,0:T(8,128)(2,1)}, f32[128,128]{1,0:T(8,128)}) custom-call(s32[1]{0:T(128)} %bitcast.far_ref, bf16[512,128]{1,0:T(8,128)(2,1)S(1)} %bitcast.15), custom_call_target="tpu_custom_call" | custom-call | tf_op jit(solution)/shard_map/pallas_call | solution.py:243
  (2 shorter events, 0.0 us)
Async XLA Ops:
  27.1 11.6 %collective-permute-start = (f32[32,128]{1,0:T(8,128)S(1)}, f32[32,128]{1,0:T(8,128)S(1)}, u32[]{:S(2)}, u32[]{:S(2)}) collective-permute-start(f32[32,128]{1,0:T(8,128)S(1)} %shard_map.78), channel_id=1, source_target_pairs={{0,385},{1,384},{2,387},{3,386},{4,389},{5,388},{6,391},{7,390},{8... | collective-permute-start | bytes 49160 | tf_op jit(solution)/shard_map/ppermute | solution.py:195
  38.7 9.9 %collective-permute-start.1 = (f32[32,128]{1,0:T(8,128)S(1)}, f32[32,128]{1,0:T(8,128)S(1)}, u32[]{:S(2)}, u32[]{:S(2)}) collective-permute-start(f32[32,128]{1,0:T(8,128)S(1)} %add.11.refs_2_), channel_id=1, source_target_pairs={{0,129},{1,128},{2,131},{3,130},{4,133},{5,132},{6,135},{7,134},{8... | collective-permute-start | bytes 49160 | tf_op jit(solution)/shard_map/ppermute | solution.py:195

commit v6 on v5

--- a/solution.py
+++ b/solution.py
@@ -31,7 +31,7 @@
     ]
     for copy in copies:
         copy.start()
-    odd = far_ref[0] % 2 == 1
+    odd = swaps(far_ref[0]) == 1
     for role, copy in enumerate(copies):
         copy.wait()
         rows[pl.ds(role, chans, stride=ROLES), :] = swapped(landed[role].astype(F32), odd)
@@ -104,10 +104,11 @@
     filt_ref[blocks - 1 : blocks, :] = jnp.sum(jnp.where(wrapped, held, 0.0), axis=0, keepdims=True)
 
 
-def conv_kernel(blocks, chan_ref, gain_ref, in_ref, gate_ref, input_ref, rows, padded, gains, sem):
+def conv_kernel(blocks, chan_ref, gain_ref, in_ref, filt_ref, gate_ref, input_ref, same_ref, rows, padded, gains, sem):
     count = GROUP * blocks
     fetch = pltpu.make_async_copy(gain_ref, gains, sem)
     fetch.start()
+    same_ref[...] = filt_ref[...]
     rows[...] = in_ref[...].astype(F32)
     u = take(rows, 0, count)
     y = take(rows, 2, count)
@@ -140,9 +141,20 @@
     input_ref[...] = jnp.dot(flip[:count, :count], d_input, preferred_element_type=F32).astype(BF16)
 
 
-def spread_kernel(blocks, gate_ref, input_ref, near_ref, far_ref, out_ref, rows):
-    count = GROUP * blocks
-    filt = near_ref[...] + far_ref[...]
+def add_kernel(left_ref, right_ref, out_ref):
+    out_ref[...] = left_ref[...] + right_ref[...]
+
+
+def total_kernel(far_ref, pair_ref, from_3_or_2_ref, from_2_ref, first_ref, own_ref, out_ref):
+    last = far_ref[0] == 3
+    front = jnp.where(last, first_ref[...], pair_ref[...])
+    out_ref[...] = front + (from_3_or_2_ref[...] + jnp.where(last, own_ref[...], from_2_ref[...]))
+
+
+def spread_kernel(blocks, far_ref, gate_ref, input_ref, total_ref, whole_ref, out_ref, rows):
+    count = GROUP * blocks
+    got = (far_ref[0] == 1) | (far_ref[0] == 2)
+    filt = jnp.where(got, whole_ref[...], total_ref[...])
     high = filt.astype(BF16).astype(F32)
     low = filt - high
     rows[pl.ds(0, count, stride=ROLES), :] = gate_ref[...].astype(F32)
@@ -156,7 +168,7 @@
 
 def unpack_kernel(far_ref, in_ref, input_ref, gate_ref, filt_ref, rows):
     chans = input_ref.shape[0]
-    odd = far_ref[0] % 2 == 1
+    odd = swaps(far_ref[0]) == 1
     rows[...] = in_ref[...].astype(F32)
     gate_ref[...] = swapped(take(rows, 0, chans), odd).astype(BF16)
     input_ref[...] = swapped(take(rows, 1, chans), odd).astype(BF16)
@@ -189,9 +201,13 @@
     )
 
 
-def exchange(array, step):
-    far, seq = lax.axis_size("far"), lax.axis_size("seq")
-    pairs = [(i * seq + j, (i ^ step) * seq + (j ^ 1)) for i in range(far) for j in range(seq)]
+def swaps(group):
+    return (group + 1) // 2 % 2
+
+
+def send(array, *edges):
+    seq = lax.axis_size("seq")
+    pairs = [(i * seq + j, k * seq + (j ^ swaps(i) ^ swaps(k))) for i, k in edges for j in range(seq)]
     return lax.ppermute(array, ("far", "seq"), pairs)
 
 
@@ -218,27 +234,32 @@
         [VMEM],
         [rows, pltpu.VMEM((2 * GROUP, 2 * blocks, LANES), F32)],
     )(packed)
-    around = exchange(filt, 3)
-    chan = lax.axis_index("near") * blocks + (lax.axis_index("seq") ^ (far & 1))
-    gate, d_in = call(
+    chan = lax.axis_index("near") * blocks + (lax.axis_index("seq") ^ swaps(far))
+    gate, d_in, same = call(
         lambda *refs: conv_kernel(blocks, *refs),
-        (shape((count, LANES), BF16), shape((count, LANES), BF16)),
-        [SMEM, HBM, VMEM],
+        (shape((count, LANES), BF16), shape((count, LANES), BF16), shape((blocks, LANES), F32)),
+        [SMEM, HBM, VMEM, VMEM],
         [
             rows,
             pltpu.VMEM((3 * GROUP, 2 * blocks, LANES), F32),
             pltpu.SMEM(skip_gain.shape, F32),
             pltpu.SemaphoreType.DMA(()),
         ],
-    )(chan, in_hbm(skip_gain), packed)
-    filt = filt + around
-    beside = exchange(filt, 1)
+    )(chan, in_hbm(skip_gain), packed, filt)
+    from_2 = send(filt, (2, 0))
+    from_3_or_2 = send(filt, (3, 0), (2, 3))
+    from_1 = send(filt, (1, 0))
+    part = shape(filt.shape, F32)
+    pair = call(add_kernel, part, [VMEM] * 2, [])(same, from_1)
+    first = send(pair, (0, 3))
+    total = call(total_kernel, part, [SMEM] + [VMEM] * 5, [])(far, pair, from_3_or_2, from_2, first, same)
+    whole = send(total, (0, 1), (3, 2))
     packed = call(
         lambda *refs: spread_kernel(blocks, *refs),
         shape((count * ROLES, LANES), BF16),
-        [VMEM] * 4,
+        [SMEM] + [VMEM] * 4,
         [rows],
-    )(gate, d_in, filt, beside)
+    )(far, gate, d_in, total, whole)
     packed = lax.all_to_all(packed, ("near", "seq"), 0, 0, tiled=True)
     d_input, d_gate, d_filter = call(
         unpack_kernel,

time: 65.7 us -> 63.4 us (0.965)
  starting transfers between devices: 17.8 us -> 9.35 us
  waiting for transfers between devices: 2.11 us -> 6.66 us
  blocking collectives: 40.6 us -> 42.1 us
    ppermute x2 -> x5, starting transfers between devices: 17.8 us -> 9.35 us  [send(): return lax.ppermute(array, ('far', 'seq'), pairs)]
    ppermute x2 -> x5, waiting for transfers between devices: 2.11 us -> 6.66 us  [send(): return lax.ppermute(array, ('far', 'seq'), pairs)]
    all_to_all x2, blocking collectives: 40.6 us -> 42.1 us  [body(): packed = lax.all_to_all(packed, ('near', 'seq'), 0, 0, tiled=True)]
  transfers between devices with their start and end apart: 2 -> 5, of which waited for: 2 -> 4; matrix products, arithmetic and copies ran while one was open for 0% -> 0% of each run, Pallas kernels for 2% -> 2%
where the time goes in v6:
time: 63.4 us; the launch traced here: 63.1 us
  blocking collectives  42.1 us (66%)
  starting transfers between devices  9.35 us (15%)
  waiting for transfers between devices  6.66 us (11%)
  Pallas kernels  4.2 us (7%)
  between operations  0.74 us (1%)
    all_to_all x2, blocking collectives, body(): packed = lax.all_to_all(packed, ('near', 'seq'), 0, 0, tiled=True)  42.1 us
    ppermute x5, starting transfers between devices, send(): return lax.ppermute(array, ('far', 'seq'), pairs)  9.35 us
    ppermute x5, waiting for transfers between devices, send(): return lax.ppermute(array, ('far', 'seq'), pairs)  6.66 us
    pallas_call x1, Pallas kernels, body(): call(lambda *refs: conv_kernel(blocks, *refs), (shape((count, LANES), BF1...  1.57 us
  transfers between devices with their start and end apart: 5, of which 4 were waited for; matrix products, arithmetic and copies ran while one was open for 0% of the time, Pallas kernels for 2%

profile of v6, /device:TPU:1, one launch (start us, length us, event | category | flops | bytes accessed | tf_op | source)
XLA Modules:
  0.0 63.1 jit_solution(12969178306633227727)
XLA Ops:
  0.6 0.9 %shard_map.76 = bf16[512,128]{1,0:T(8,128)(2,1)S(1)} custom-call(s32[1]{0:T(128)} %bitcast.far_ref.refs_0_, bf16[128,128]{1,0:T(8,128)(2,1)} %bitcast.17, bf16[128,128]{1,0:T(8,128)(2,1)} %bitcast.18, bf16[128,128]{1,0:T(8,128)(2,1)} %bitcast.19, bf16[128,128]{1,0:T(8,128)(2,1)} %k_ref.1), custom_call_target="tpu_custom_call" | custom-call | tf_op jit(solution)/shard_map/pallas_call | solution.py:220
  1.5 24.6 %all_to_all.22 = bf16[128,4,128]{2,1,0:T(4,128)(2,1)S(1)} all-to-all(bf16[128,4,128]{2,1,0:T(4,128)(2,1)S(1)} %bitcast.16), channel_id=1, replica_groups=mesh['far'=4,'near'=4,'seq'=32] {'near','seq'}, dimensions={0} | all-to-all | bytes 262144 | tf_op jit(solution)/shard_map/all_to_all | solution.py:230
  26.1 1.0 %shard_map.77.refs_3_ = f32[32,128]{1,0:T(8,128)S(1)} custom-call(bf16[512,128]{1,0:T(8,128)(2,1)S(1)} %bitcast.12), custom_call_target="tpu_custom_call" | custom-call | tf_op jit(solution)/shard_map/pallas_call | solution.py:231
  27.1 1.3 %collective-permute-start = (f32[32,128]{1,0:T(8,128)S(1)}, f32[32,128]{1,0:T(8,128)S(1)}, u32[]{:S(2)}, u32[]{:S(2)}) collective-permute-start(f32[32,128]{1,0:T(8,128)S(1)} %shard_map.77.refs_3_), channel_id=1, source_target_pairs={{128,1},{129,0},{130,3},{131,2},{132,5},{133,4},{134,7},{135,6},{1... | collective-permute-start | bytes 49160 | tf_op jit(solution)/shard_map/ppermute | solution.py:211
  28.4 1.3 %collective-permute-start.2 = (f32[32,128]{1,0:T(8,128)S(1)}, f32[32,128]{1,0:T(8,128)S(1)}, u32[]{:S(2)}, u32[]{:S(2)}) collective-permute-start(f32[32,128]{1,0:T(8,128)S(1)} %shard_map.77.refs_3_), channel_id=1, source_target_pairs={{256,1},{257,0},{258,3},{259,2},{260,5},{261,4},{262,7},{263,6},{2... | collective-permute-start | bytes 49160 | tf_op jit(solution)/shard_map/ppermute | solution.py:211
  29.7 1.3 %collective-permute-start.1 = (f32[32,128]{1,0:T(8,128)S(1)}, f32[32,128]{1,0:T(8,128)S(1)}, u32[]{:S(2)}, u32[]{:S(2)}) collective-permute-start(f32[32,128]{1,0:T(8,128)S(1)} %shard_map.77.refs_3_), channel_id=1, source_target_pairs={{384,0},{385,1},{386,2},{387,3},{388,4},{389,5},{390,6},{391,7},{3... | collective-permute-start | bytes 49160 | tf_op jit(solution)/shard_map/ppermute | solution.py:211
  31.0 1.6 %shard_map.78 = (bf16[128,128]{1,0:T(8,128)(2,1)S(1)}, bf16[128,128]{1,0:T(8,128)(2,1)S(1)}, f32[32,128]{1,0:T(8,128)S(1)}) custom-call(s32[1]{0:T(128)S(6)} %add.19.refs_0_, f32[128]{0:T(128)} %refs_1_.1, bf16[512,128]{1,0:T(8,128)(2,1)S(1)} %bitcast.13, f32[32,128]{1,0:T(8,128)S(1)} %shard_map.77.refs_3_), custom_call_target="tpu_custom_call" | custom-call | tf_op jit(solution)/shard_map/pallas_call | solution.py:238
  32.6 5.0 %collective-permute-done.right_ref = f32[32,128]{1,0:T(8,128)S(1)} collective-permute-done((f32[32,128]{1,0:T(8,128)S(1)}, f32[32,128]{1,0:T(8,128)S(1)}, u32[]{:S(2)}, u32[]{:S(2)}) %collective-permute-start) | collective-permute-done | bytes 16416 | tf_op jit(solution)/shard_map/ppermute | solution.py:211
  37.6 4.2 %collective-permute-start.3 = (f32[32,128]{1,0:T(8,128)S(1)}, f32[32,128]{1,0:T(8,128)S(1)}, u32[]{:S(2)}, u32[]{:S(2)}) collective-permute-start(f32[32,128]{1,0:T(8,128)S(1)} %shard_map.79.pair_ref), channel_id=1, source_target_pairs={{0,384},{1,385},{2,386},{3,387},{4,388},{5,389},{6,390},{7,391},{8... | collective-permute-start | bytes 49160 | tf_op jit(solution)/shard_map/ppermute | solution.py:211
  41.8 0.6 collective-permute-done.2.from_2_ref
  42.4 0.0 collective-permute-done.1.from_3_or_2_ref
  42.4 0.2 collective-permute-done.3.first_ref
  42.6 1.3 %collective-permute-start.4 = (f32[32,128]{1,0:T(8,128)S(1)}, f32[32,128]{1,0:T(8,128)S(1)}, u32[]{:S(2)}, u32[]{:S(2)}) collective-permute-start(f32[32,128]{1,0:T(8,128)S(1)} %shard_map.80.refs_3_), channel_id=1, source_target_pairs={{0,129},{1,128},{2,131},{3,130},{4,133},{5,132},{6,135},{7,134},{8... | collective-permute-start | bytes 49160 | tf_op jit(solution)/shard_map/ppermute | solution.py:211
  43.9 0.9 %collective-permute-done.4.refs_4_ = f32[32,128]{1,0:T(8,128)S(1)} collective-permute-done((f32[32,128]{1,0:T(8,128)S(1)}, f32[32,128]{1,0:T(8,128)S(1)}, u32[]{:S(2)}, u32[]{:S(2)}) %collective-permute-start.4) | collective-permute-done | bytes 16416 | tf_op jit(solution)/shard_map/ppermute | solution.py:211
  44.8 17.6 %all_to_all.23 = bf16[128,4,128]{2,1,0:T(4,128)(2,1)S(1)} all-to-all(bf16[128,4,128]{2,1,0:T(4,128)(2,1)S(1)} %bitcast.14), channel_id=1, replica_groups=mesh['far'=4,'near'=4,'seq'=32] {'near','seq'}, dimensions={0} | all-to-all | bytes 262144 | tf_op jit(solution)/shard_map/all_to_all | solution.py:263
  62.4 0.7 %shard_map.82 = (bf16[128,128]{1,0:T(8,128)(2,1)}, bf16[128,128]{1,0:T(8,128)(2,1)}, f32[128,128]{1,0:T(8,128)}) custom-call(s32[1]{0:T(128)} %bitcast.far_ref.refs_0_, bf16[512,128]{1,0:T(8,128)(2,1)S(1)} %bitcast.15), custom_call_target="tpu_custom_call" | custom-call | tf_op jit(solution)/shard_map/pallas_call | solution.py:264
  (3 shorter events, 0.0 us)
Async XLA Ops:
  27.1 10.5 %collective-permute-start = (f32[32,128]{1,0:T(8,128)S(1)}, f32[32,128]{1,0:T(8,128)S(1)}, u32[]{:S(2)}, u32[]{:S(2)}) collective-permute-start(f32[32,128]{1,0:T(8,128)S(1)} %shard_map.77.refs_3_), channel_id=1, source_target_pairs={{128,1},{129,0},{130,3},{131,2},{132,5},{133,4},{134,7},{135,6},{1... | collective-permute-start | bytes 49160 | tf_op jit(solution)/shard_map/ppermute | solution.py:211
  28.4 14.0 %collective-permute-start.2 = (f32[32,128]{1,0:T(8,128)S(1)}, f32[32,128]{1,0:T(8,128)S(1)}, u32[]{:S(2)}, u32[]{:S(2)}) collective-permute-start(f32[32,128]{1,0:T(8,128)S(1)} %shard_map.77.refs_3_), channel_id=1, source_target_pairs={{256,1},{257,0},{258,3},{259,2},{260,5},{261,4},{262,7},{263,6},{2... | collective-permute-start | bytes 49160 | tf_op jit(solution)/shard_map/ppermute | solution.py:211
  29.7 12.7 %collective-permute-start.1 = (f32[32,128]{1,0:T(8,128)S(1)}, f32[32,128]{1,0:T(8,128)S(1)}, u32[]{:S(2)}, u32[]{:S(2)}) collective-permute-start(f32[32,128]{1,0:T(8,128)S(1)} %shard_map.77.refs_3_), channel_id=1, source_target_pairs={{384,0},{385,1},{386,2},{387,3},{388,4},{389,5},{390,6},{391,7},{3... | collective-permute-start | bytes 49160 | tf_op jit(solution)/shard_map/ppermute | solution.py:211
  37.6 5.0 %collective-permute-start.3 = (f32[32,128]{1,0:T(8,128)S(1)}, f32[32,128]{1,0:T(8,128)S(1)}, u32[]{:S(2)}, u32[]{:S(2)}) collective-permute-start(f32[32,128]{1,0:T(8,128)S(1)} %shard_map.79.pair_ref), channel_id=1, source_target_pairs={{0,384},{1,385},{2,386},{3,387},{4,388},{5,389},{6,390},{7,391},{8... | collective-permute-start | bytes 49160 | tf_op jit(solution)/shard_map/ppermute | solution.py:211
  42.6 2.1 %collective-permute-start.4 = (f32[32,128]{1,0:T(8,128)S(1)}, f32[32,128]{1,0:T(8,128)S(1)}, u32[]{:S(2)}, u32[]{:S(2)}) collective-permute-start(f32[32,128]{1,0:T(8,128)S(1)} %shard_map.80.refs_3_), channel_id=1, source_target_pairs={{0,129},{1,128},{2,131},{3,130},{4,133},{5,132},{6,135},{7,134},{8... | collective-permute-start | bytes 49160 | tf_op jit(solution)/shard_map/ppermute | solution.py:211

commit v7 on v6

--- a/solution.py
+++ b/solution.py
@@ -104,11 +104,10 @@
     filt_ref[blocks - 1 : blocks, :] = jnp.sum(jnp.where(wrapped, held, 0.0), axis=0, keepdims=True)
 
 
-def conv_kernel(blocks, chan_ref, gain_ref, in_ref, filt_ref, gate_ref, input_ref, same_ref, rows, padded, gains, sem):
+def convolve(blocks, chan_ref, gain_ref, in_ref, gate_ref, input_ref, rows, padded, gains, sem):
     count = GROUP * blocks
     fetch = pltpu.make_async_copy(gain_ref, gains, sem)
     fetch.start()
-    same_ref[...] = filt_ref[...]
     rows[...] = in_ref[...].astype(F32)
     u = take(rows, 0, count)
     y = take(rows, 2, count)
@@ -141,6 +140,27 @@
     input_ref[...] = jnp.dot(flip[:count, :count], d_input, preferred_element_type=F32).astype(BF16)
 
 
+def early_kernel(blocks, far_ref, chan_ref, gain_ref, in_ref, filt_ref, gate_ref, input_ref, same_ref, *scratch):
+    same_ref[...] = filt_ref[...]
+
+    @pl.when(far_ref[0] == 0)
+    def _():
+        convolve(blocks, chan_ref, gain_ref, in_ref, gate_ref, input_ref, *scratch)
+
+
+def late_kernel(
+    blocks, far_ref, chan_ref, gain_ref, in_ref, early_gate_ref, early_input_ref, after_ref, gate_ref, input_ref, *scratch
+):
+    @pl.when(far_ref[0] == 0)
+    def _():
+        gate_ref[...] = early_gate_ref[...]
+        input_ref[...] = early_input_ref[...]
+
+    @pl.when(far_ref[0] != 0)
+    def _():
+        convolve(blocks, chan_ref, gain_ref, in_ref, gate_ref, input_ref, *scratch)
+
+
 def add_kernel(left_ref, right_ref, out_ref):
     out_ref[...] = left_ref[...] + right_ref[...]
 
@@ -235,25 +255,28 @@
         [rows, pltpu.VMEM((2 * GROUP, 2 * blocks, LANES), F32)],
     )(packed)
     chan = lax.axis_index("near") * blocks + (lax.axis_index("seq") ^ swaps(far))
+    out = shape((count, LANES), BF16)
+    part = shape((blocks, LANES), F32)
+    scratch = [
+        rows,
+        pltpu.VMEM((3 * GROUP, 2 * blocks, LANES), F32),
+        pltpu.SMEM(skip_gain.shape, F32),
+        pltpu.SemaphoreType.DMA(()),
+    ]
+    gain = in_hbm(skip_gain)
     gate, d_in, same = call(
-        lambda *refs: conv_kernel(blocks, *refs),
-        (shape((count, LANES), BF16), shape((count, LANES), BF16), shape((blocks, LANES), F32)),
-        [SMEM, HBM, VMEM, VMEM],
-        [
-            rows,
-            pltpu.VMEM((3 * GROUP, 2 * blocks, LANES), F32),
-            pltpu.SMEM(skip_gain.shape, F32),
-            pltpu.SemaphoreType.DMA(()),
-        ],
-    )(chan, in_hbm(skip_gain), packed, filt)
+        lambda *refs: early_kernel(blocks, *refs), (out, out, part), [SMEM, SMEM, HBM, VMEM, VMEM], scratch
+    )(far, chan, gain, packed, filt)
     from_2 = send(filt, (2, 0))
     from_3_or_2 = send(filt, (3, 0), (2, 3))
     from_1 = send(filt, (1, 0))
-    part = shape(filt.shape, F32)
     pair = call(add_kernel, part, [VMEM] * 2, [])(same, from_1)
     first = send(pair, (0, 3))
     total = call(total_kernel, part, [SMEM] + [VMEM] * 5, [])(far, pair, from_3_or_2, from_2, first, same)
     whole = send(total, (0, 1), (3, 2))
+    gate, d_in = call(
+        lambda *refs: late_kernel(blocks, *refs), (out, out), [SMEM, SMEM, HBM] + [VMEM] * 4, scratch
+    )(far, chan, gain, packed, gate, d_in, total)
     packed = call(
         lambda *refs: spread_kernel(blocks, *refs),
         shape((count * ROLES, LANES), BF16),

time: 63.4 us -> 62.3 us (0.983)
  starting transfers between devices: 9.35 us -> 7.81 us
  waiting for transfers between devices: 6.66 us -> 7.93 us
  blocking collectives: 42.1 us -> 41.3 us
    ppermute x5, starting transfers between devices: 9.35 us -> 7.81 us  [send(): return lax.ppermute(array, ('far', 'seq'), pairs)]
    ppermute x5, waiting for transfers between devices: 6.66 us -> 7.93 us  [send(): return lax.ppermute(array, ('far', 'seq'), pairs)]
    all_to_all x2, blocking collectives: 42.1 us -> 41.3 us  [body(): packed = lax.all_to_all(packed, ('near', 'seq'), 0, 0, tiled=True)]
    pallas_call x1 -> x2, Pallas kernels: 1.57 us -> 1.61 us  [the longest x1 1.58 us: body(): call(lambda *refs: early_kernel(blocks, *refs), (out, out, part), [SMEM,...]
  transfers between devices with their start and end apart: 5 -> 5, of which waited for: 4 -> 3; matrix products, arithmetic and copies ran while one was open for 0% -> 0% of each run, Pallas kernels for 2% -> 3%
where the time goes in v7:
time: 62.3 us; the launch traced here: 62 us
  blocking collectives  41.3 us (66%)
  waiting for transfers between devices  7.93 us (13%)
  starting transfers between devices  7.81 us (13%)
  Pallas kernels  4.24 us (7%)
  between operations  0.75 us (1%)
    all_to_all x2, blocking collectives, body(): packed = lax.all_to_all(packed, ('near', 'seq'), 0, 0, tiled=True)  41.3 us
    ppermute x5, waiting for transfers between devices, send(): return lax.ppermute(array, ('far', 'seq'), pairs)  7.93 us
    ppermute x5, starting transfers between devices, send(): return lax.ppermute(array, ('far', 'seq'), pairs)  7.81 us
    pallas_call x1, Pallas kernels, body(): call(lambda *refs: early_kernel(blocks, *refs), (out, out, part), [SMEM,...  1.58 us
  transfers between devices with their start and end apart: 5, of which 3 were waited for; matrix products, arithmetic and copies ran while one was open for 0% of the time, Pallas kernels for 3%

profile of v7, /device:TPU:1, one launch (start us, length us, event | category | flops | bytes accessed | tf_op | source)
XLA Modules:
  0.0 62.0 jit_solution(13478193960826891767)
XLA Ops:
  0.6 0.9 %shard_map.76 = bf16[512,128]{1,0:T(8,128)(2,1)S(1)} custom-call(s32[1]{0:T(128)} %bitcast.far_ref.refs_0_, bf16[128,128]{1,0:T(8,128)(2,1)} %bitcast.18, bf16[128,128]{1,0:T(8,128)(2,1)} %bitcast.19, bf16[128,128]{1,0:T(8,128)(2,1)} %bitcast.20, bf16[128,128]{1,0:T(8,128)(2,1)} %k_ref.1), custom_call_target="tpu_custom_call" | custom-call | tf_op jit(solution)/shard_map/pallas_call | solution.py:240
  1.5 24.6 %all_to_all.22 = bf16[128,4,128]{2,1,0:T(4,128)(2,1)S(1)} all-to-all(bf16[128,4,128]{2,1,0:T(4,128)(2,1)S(1)} %bitcast.17), channel_id=1, replica_groups=mesh['far'=4,'near'=4,'seq'=32] {'near','seq'}, dimensions={0} | all-to-all | bytes 262144 | tf_op jit(solution)/shard_map/all_to_all | solution.py:250
  26.1 1.0 %shard_map.77.refs_4_ = f32[32,128]{1,0:T(8,128)S(1)} custom-call(bf16[512,128]{1,0:T(8,128)(2,1)S(1)} %bitcast.12), custom_call_target="tpu_custom_call" | custom-call | tf_op jit(solution)/shard_map/pallas_call | solution.py:251
  27.1 1.3 %collective-permute-start = (f32[32,128]{1,0:T(8,128)S(1)}, f32[32,128]{1,0:T(8,128)S(1)}, u32[]{:S(2)}, u32[]{:S(2)}) collective-permute-start(f32[32,128]{1,0:T(8,128)S(1)} %shard_map.77.refs_4_), channel_id=1, source_target_pairs={{128,1},{129,0},{130,3},{131,2},{132,5},{133,4},{134,7},{135,6},{1... | collective-permute-start | bytes 49160 | tf_op jit(solution)/shard_map/ppermute | solution.py:231
  28.4 1.3 %collective-permute-start.2 = (f32[32,128]{1,0:T(8,128)S(1)}, f32[32,128]{1,0:T(8,128)S(1)}, u32[]{:S(2)}, u32[]{:S(2)}) collective-permute-start(f32[32,128]{1,0:T(8,128)S(1)} %shard_map.77.refs_4_), channel_id=1, source_target_pairs={{256,1},{257,0},{258,3},{259,2},{260,5},{261,4},{262,7},{263,6},{2... | collective-permute-start | bytes 49160 | tf_op jit(solution)/shard_map/ppermute | solution.py:231
  29.7 1.3 %collective-permute-start.1 = (f32[32,128]{1,0:T(8,128)S(1)}, f32[32,128]{1,0:T(8,128)S(1)}, u32[]{:S(2)}, u32[]{:S(2)}) collective-permute-start(f32[32,128]{1,0:T(8,128)S(1)} %shard_map.77.refs_4_), channel_id=1, source_target_pairs={{384,0},{385,1},{386,2},{387,3},{388,4},{389,5},{390,6},{391,7},{3... | collective-permute-start | bytes 49160 | tf_op jit(solution)/shard_map/ppermute | solution.py:231
  31.0 1.6 %shard_map.78 = (bf16[128,128]{1,0:T(8,128)(2,1)S(1)}, bf16[128,128]{1,0:T(8,128)(2,1)S(1)}, f32[32,128]{1,0:T(8,128)S(1)}) custom-call(s32[1]{0:T(128)} %bitcast.far_ref.refs_0_, s32[1]{0:T(128)S(6)} %add.19.refs_1_, f32[128]{0:T(128)} %refs_2_.3, bf16[512,128]{1,0:T(8,128)(2,1)S(1)} %bitcast.13, f32[32,128]{1,0:T(8,128)S(1)} %shard_map.77.refs_4_), custom_call_target="tpu_custom_call" | custom-call | tf_op jit(solution)/shard_map/pallas_call | solution.py:267
  32.6 4.9 %collective-permute-done.right_ref = f32[32,128]{1,0:T(8,128)S(1)} collective-permute-done((f32[32,128]{1,0:T(8,128)S(1)}, f32[32,128]{1,0:T(8,128)S(1)}, u32[]{:S(2)}, u32[]{:S(2)}) %collective-permute-start) | collective-permute-done | bytes 16416 | tf_op jit(solution)/shard_map/ppermute | solution.py:231
  37.6 2.6 %collective-permute-start.3 = (f32[32,128]{1,0:T(8,128)S(1)}, f32[32,128]{1,0:T(8,128)S(1)}, u32[]{:S(2)}, u32[]{:S(2)}) collective-permute-start(f32[32,128]{1,0:T(8,128)S(1)} %shard_map.79.pair_ref), channel_id=1, source_target_pairs={{0,384},{1,385},{2,386},{3,387},{4,388},{5,389},{6,390},{7,391},{8... | collective-permute-start | bytes 49160 | tf_op jit(solution)/shard_map/ppermute | solution.py:231
  40.2 2.2 %collective-permute-done.2.from_2_ref = f32[32,128]{1,0:T(8,128)S(1)} collective-permute-done((f32[32,128]{1,0:T(8,128)S(1)}, f32[32,128]{1,0:T(8,128)S(1)}, u32[]{:S(2)}, u32[]{:S(2)}) %collective-permute-start.2) | collective-permute-done | bytes 16416 | tf_op jit(solution)/shard_map/ppermute | solution.py:231
  42.4 0.0 collective-permute-done.1.from_3_or_2_ref
  42.4 0.0 collective-permute-done.3.first_ref
  42.4 1.3 %collective-permute-start.4 = (f32[32,128]{1,0:T(8,128)S(1)}, f32[32,128]{1,0:T(8,128)S(1)}, u32[]{:S(2)}, u32[]{:S(2)}) collective-permute-start(f32[32,128]{1,0:T(8,128)S(1)} %shard_map.80.refs_6_.refs_3_), channel_id=1, source_target_pairs={{0,129},{1,128},{2,131},{3,130},{4,133},{5,132},{6,135},{7,134},{8... | collective-permute-start | bytes 49160 | tf_op jit(solution)/shard_map/ppermute | solution.py:231
  43.7 0.8 %collective-permute-done.4.refs_4_ = f32[32,128]{1,0:T(8,128)S(1)} collective-permute-done((f32[32,128]{1,0:T(8,128)S(1)}, f32[32,128]{1,0:T(8,128)S(1)}, u32[]{:S(2)}, u32[]{:S(2)}) %collective-permute-start.4) | collective-permute-done | bytes 16416 | tf_op jit(solution)/shard_map/ppermute | solution.py:231
  44.6 16.7 %all_to_all.23 = bf16[128,4,128]{2,1,0:T(4,128)(2,1)S(1)} all-to-all(bf16[128,4,128]{2,1,0:T(4,128)(2,1)S(1)} %bitcast.15), channel_id=1, replica_groups=mesh['far'=4,'near'=4,'seq'=32] {'near','seq'}, dimensions={0} | all-to-all | bytes 262144 | tf_op jit(solution)/shard_map/all_to_all | solution.py:286
  61.3 0.7 %shard_map.83 = (bf16[128,128]{1,0:T(8,128)(2,1)}, bf16[128,128]{1,0:T(8,128)(2,1)}, f32[128,128]{1,0:T(8,128)}) custom-call(s32[1]{0:T(128)} %bitcast.far_ref.refs_0_, bf16[512,128]{1,0:T(8,128)(2,1)S(1)} %bitcast.16), custom_call_target="tpu_custom_call" | custom-call | tf_op jit(solution)/shard_map/pallas_call | solution.py:287
  (4 shorter events, 0.1 us)
Async XLA Ops:
  27.1 10.5 %collective-permute-start = (f32[32,128]{1,0:T(8,128)S(1)}, f32[32,128]{1,0:T(8,128)S(1)}, u32[]{:S(2)}, u32[]{:S(2)}) collective-permute-start(f32[32,128]{1,0:T(8,128)S(1)} %shard_map.77.refs_4_), channel_id=1, source_target_pairs={{128,1},{129,0},{130,3},{131,2},{132,5},{133,4},{134,7},{135,6},{1... | collective-permute-start | bytes 49160 | tf_op jit(solution)/shard_map/ppermute | solution.py:231
  28.4 14.0 %collective-permute-start.2 = (f32[32,128]{1,0:T(8,128)S(1)}, f32[32,128]{1,0:T(8,128)S(1)}, u32[]{:S(2)}, u32[]{:S(2)}) collective-permute-start(f32[32,128]{1,0:T(8,128)S(1)} %shard_map.77.refs_4_), channel_id=1, source_target_pairs={{256,1},{257,0},{258,3},{259,2},{260,5},{261,4},{262,7},{263,6},{2... | collective-permute-start | bytes 49160 | tf_op jit(solution)/shard_map/ppermute | solution.py:231
  29.7 12.7 %collective-permute-start.1 = (f32[32,128]{1,0:T(8,128)S(1)}, f32[32,128]{1,0:T(8,128)S(1)}, u32[]{:S(2)}, u32[]{:S(2)}) collective-permute-start(f32[32,128]{1,0:T(8,128)S(1)} %shard_map.77.refs_4_), channel_id=1, source_target_pairs={{384,0},{385,1},{386,2},{387,3},{388,4},{389,5},{390,6},{391,7},{3... | collective-permute-start | bytes 49160 | tf_op jit(solution)/shard_map/ppermute | solution.py:231
  37.6 4.8 %collective-permute-start.3 = (f32[32,128]{1,0:T(8,128)S(1)}, f32[32,128]{1,0:T(8,128)S(1)}, u32[]{:S(2)}, u32[]{:S(2)}) collective-permute-start(f32[32,128]{1,0:T(8,128)S(1)} %shard_map.79.pair_ref), channel_id=1, source_target_pairs={{0,384},{1,385},{2,386},{3,387},{4,388},{5,389},{6,390},{7,391},{8... | collective-permute-start | bytes 49160 | tf_op jit(solution)/shard_map/ppermute | solution.py:231
  42.4 2.1 %collective-permute-start.4 = (f32[32,128]{1,0:T(8,128)S(1)}, f32[32,128]{1,0:T(8,128)S(1)}, u32[]{:S(2)}, u32[]{:S(2)}) collective-permute-start(f32[32,128]{1,0:T(8,128)S(1)} %shard_map.80.refs_6_.refs_3_), channel_id=1, source_target_pairs={{0,129},{1,128},{2,131},{3,130},{4,133},{5,132},{6,135},{7,134},{8... | collective-permute-start | bytes 49160 | tf_op jit(solution)/shard_map/ppermute | solution.py:231

commit v8 on v7

--- a/solution.py
+++ b/solution.py
@@ -17,10 +17,19 @@
     return lax.broadcasted_iota(jnp.int32, shape, dim)
 
 
-def swapped(value, odd):
+def swaps(group):
+    return (group + 1) // 2 % 2
+
+
+def turns(group):
+    return group // 2 * (1 - group % 2)
+
+
+def placed(value, group):
     up, down = jnp.roll(value, -1, axis=0), jnp.roll(value, 1, axis=0)
-    other = jnp.where(iota(value.shape, 0) % 2 == 0, up, down)
-    return jnp.where(odd, other, value)
+    value = jnp.where(swaps(group) == 1, jnp.where(iota(value.shape, 0) % 2 == 0, up, down), value)
+    half = value.shape[0] // 2
+    return jnp.where(turns(group) == 1, jnp.concatenate([value[half:], value[:half]], axis=0), value)
 
 
 def pack_kernel(far_ref, u_ref, g_ref, y_ref, k_ref, out_ref, landed, rows, sems):
@@ -31,10 +40,9 @@
     ]
     for copy in copies:
         copy.start()
-    odd = swaps(far_ref[0]) == 1
     for role, copy in enumerate(copies):
         copy.wait()
-        rows[pl.ds(role, chans, stride=ROLES), :] = swapped(landed[role].astype(F32), odd)
+        rows[pl.ds(role, chans, stride=ROLES), :] = placed(landed[role].astype(F32), far_ref[0])
     out_ref[...] = rows[...].astype(BF16)
 
 
@@ -165,16 +173,16 @@
     out_ref[...] = left_ref[...] + right_ref[...]
 
 
-def total_kernel(far_ref, pair_ref, from_3_or_2_ref, from_2_ref, first_ref, own_ref, out_ref):
-    last = far_ref[0] == 3
-    front = jnp.where(last, first_ref[...], pair_ref[...])
-    out_ref[...] = front + (from_3_or_2_ref[...] + jnp.where(last, own_ref[...], from_2_ref[...]))
-
-
-def spread_kernel(blocks, far_ref, gate_ref, input_ref, total_ref, whole_ref, out_ref, rows):
+def sum_kernel(front_ref, left_ref, right_ref, out_ref):
+    out_ref[...] = front_ref[...] + (left_ref[...] + right_ref[...])
+
+
+def spread_kernel(blocks, far_ref, gate_ref, input_ref, *refs):
+    *sums, out_ref, rows = refs
     count = GROUP * blocks
-    got = (far_ref[0] == 1) | (far_ref[0] == 2)
-    filt = jnp.where(got, whole_ref[...], total_ref[...])
+    group = far_ref[0]
+    on_0, on_1, on_2, on_3 = [ref[...] for ref in sums]
+    filt = jnp.where(group < 2, jnp.where(group == 0, on_0, on_1), jnp.where(group == 2, on_2, on_3))
     high = filt.astype(BF16).astype(F32)
     low = filt - high
     rows[pl.ds(0, count, stride=ROLES), :] = gate_ref[...].astype(F32)
@@ -188,11 +196,11 @@
 
 def unpack_kernel(far_ref, in_ref, input_ref, gate_ref, filt_ref, rows):
     chans = input_ref.shape[0]
-    odd = swaps(far_ref[0]) == 1
     rows[...] = in_ref[...].astype(F32)
-    gate_ref[...] = swapped(take(rows, 0, chans), odd).astype(BF16)
-    input_ref[...] = swapped(take(rows, 1, chans), odd).astype(BF16)
-    filt_ref[...] = swapped(take(rows, 2, chans) + take(rows, 3, chans), odd) * (1.0 / 64.0)
+    group = far_ref[0]
+    gate_ref[...] = placed(take(rows, 0, chans), group).astype(BF16)
+    input_ref[...] = placed(take(rows, 1, chans), group).astype(BF16)
+    filt_ref[...] = placed(take(rows, 2, chans) + take(rows, 3, chans), group) * (1.0 / 64.0)
 
 
 VMEM = pl.BlockSpec(memory_space=pltpu.VMEM)
@@ -221,14 +229,15 @@
     )
 
 
-def swaps(group):
-    return (group + 1) // 2 % 2
-
-
 def send(array, *edges):
-    seq = lax.axis_size("seq")
-    pairs = [(i * seq + j, k * seq + (j ^ swaps(i) ^ swaps(k))) for i, k in edges for j in range(seq)]
-    return lax.ppermute(array, ("far", "seq"), pairs)
+    near, seq = lax.axis_size("near"), lax.axis_size("seq")
+    pairs = []
+    for source, target in edges:
+        turned, crossed = turns(source) ^ turns(target), swaps(source) ^ swaps(target)
+        for i in range(near):
+            to = (i + turned * near // 2) % near
+            pairs += [((source * near + i) * seq + j, (target * near + to) * seq + (j ^ crossed)) for j in range(seq)]
+    return lax.ppermute(array, ("far", "near", "seq"), pairs)
 
 
 def body(inputs, gate_values, grad_out, filter_raw, skip_gain):
@@ -254,7 +263,9 @@
         [VMEM],
         [rows, pltpu.VMEM((2 * GROUP, 2 * blocks, LANES), F32)],
     )(packed)
-    chan = lax.axis_index("near") * blocks + (lax.axis_index("seq") ^ swaps(far))
+    near = lax.axis_index("near")
+    near = (near + turns(far) * GROUP // 2) % GROUP
+    chan = near * blocks + (lax.axis_index("seq") ^ swaps(far))
     out = shape((count, LANES), BF16)
     part = shape((blocks, LANES), F32)
     scratch = [
@@ -272,17 +283,19 @@
     from_1 = send(filt, (1, 0))
     pair = call(add_kernel, part, [VMEM] * 2, [])(same, from_1)
     first = send(pair, (0, 3))
-    total = call(total_kernel, part, [SMEM] + [VMEM] * 5, [])(far, pair, from_3_or_2, from_2, first, same)
-    whole = send(total, (0, 1), (3, 2))
+    total = call(sum_kernel, part, [VMEM] * 3, [])(pair, from_2, from_3_or_2)
+    to_1 = send(total, (0, 1))
+    total_3 = call(sum_kernel, part, [VMEM] * 3, [])(first, same, from_3_or_2)
+    to_2 = send(total_3, (3, 2))
     gate, d_in = call(
         lambda *refs: late_kernel(blocks, *refs), (out, out), [SMEM, SMEM, HBM] + [VMEM] * 4, scratch
-    )(far, chan, gain, packed, gate, d_in, total)
+    )(far, chan, gain, packed, gate, d_in, total_3)
     packed = call(
         lambda *refs: spread_kernel(blocks, *refs),
         shape((count * ROLES, LANES), BF16),
-        [SMEM] + [VMEM] * 4,
+        [SMEM] + [VMEM] * 6,
         [rows],
-    )(far, gate, d_in, total, whole)
+    )(far, gate, d_in, total, to_1, to_2, total_3)
     packed = lax.all_to_all(packed, ("near", "seq"), 0, 0, tiled=True)
     d_input, d_gate, d_filter = call(
         unpack_kernel,

time: 62.3 us -> 61.3 us (0.984)
  waiting for transfers between devices: 7.93 us -> 5.39 us
  starting transfers between devices: 7.81 us -> 8.52 us
    ppermute x5 -> x6, waiting for transfers between devices: 7.93 us -> 5.39 us  [send(): return lax.ppermute(array, ('far', 'near', 'seq'), pairs)]
    ppermute x5 -> x6, starting transfers between devices: 7.81 us -> 8.52 us  [send(): return lax.ppermute(array, ('far', 'near', 'seq'), pairs)]
    all_to_all x2, blocking collectives: 41.3 us -> 41.9 us  [body(): packed = lax.all_to_all(packed, ('near', 'seq'), 0, 0, tiled=True)]
  transfers between devices with their start and end apart: 5 -> 6, of which waited for: 3 -> 3; matrix products, arithmetic and copies ran while one was open for 0% -> 0% of each run, Pallas kernels for 3% -> 3%
where the time goes in v8:
time: 61.3 us; the launch traced here: 60.9 us
  blocking collectives  41.9 us (68%)
  starting transfers between devices  8.52 us (14%)
  waiting for transfers between devices  5.39 us (9%)
  Pallas kernels  4.27 us (7%)
  between operations  0.82 us (1%)
    all_to_all x2, blocking collectives, body(): packed = lax.all_to_all(packed, ('near', 'seq'), 0, 0, tiled=True)  41.9 us
    ppermute x6, starting transfers between devices, send(): return lax.ppermute(array, ('far', 'near', 'seq'), pairs)  8.52 us
    ppermute x6, waiting for transfers between devices, send(): return lax.ppermute(array, ('far', 'near', 'seq'), pairs)  5.39 us
    pallas_call x1, Pallas kernels, body(): call(lambda *refs: early_kernel(blocks, *refs), (out, out, part), [SMEM,...  1.58 us
  transfers between devices with their start and end apart: 6, of which 3 were waited for; matrix products, arithmetic and copies ran while one was open for 0% of the time, Pallas kernels for 3%

profile of v8, /device:TPU:1, one launch (start us, length us, event | category | flops | bytes accessed | tf_op | source)
XLA Modules:
  0.0 60.9 jit_solution(10990184053472954900)
XLA Ops:
  0.6 0.9 %shard_map.76 = bf16[512,128]{1,0:T(8,128)(2,1)S(1)} custom-call(s32[1]{0:T(128)} %bitcast.far_ref.refs_0_, bf16[128,128]{1,0:T(8,128)(2,1)} %bitcast.18, bf16[128,128]{1,0:T(8,128)(2,1)} %bitcast.19, bf16[128,128]{1,0:T(8,128)(2,1)} %bitcast.20, bf16[128,128]{1,0:T(8,128)(2,1)} %k_ref.1), custom_call_target="tpu_custom_call" | custom-call | tf_op jit(solution)/shard_map/pallas_call | solution.py:249
  1.6 24.6 %all_to_all.22 = bf16[128,4,128]{2,1,0:T(4,128)(2,1)S(1)} all-to-all(bf16[128,4,128]{2,1,0:T(4,128)(2,1)S(1)} %bitcast.17), channel_id=1, replica_groups=mesh['far'=4,'near'=4,'seq'=32] {'near','seq'}, dimensions={0} | all-to-all | bytes 262144 | tf_op jit(solution)/shard_map/all_to_all | solution.py:259
  26.1 1.0 %shard_map.77.refs_4_ = f32[32,128]{1,0:T(8,128)S(1)} custom-call(bf16[512,128]{1,0:T(8,128)(2,1)S(1)} %bitcast.12), custom_call_target="tpu_custom_call" | custom-call | tf_op jit(solution)/shard_map/pallas_call | solution.py:260
  27.1 1.3 %collective-permute-start = (f32[32,128]{1,0:T(8,128)S(1)}, f32[32,128]{1,0:T(8,128)S(1)}, u32[]{:S(2)}, u32[]{:S(2)}) collective-permute-start(f32[32,128]{1,0:T(8,128)S(1)} %shard_map.77.refs_4_), channel_id=1, source_target_pairs={{128,1},{129,0},{130,3},{131,2},{132,5},{133,4},{134,7},{135,6},{1... | collective-permute-start | bytes 49160 | tf_op jit(solution)/shard_map/ppermute | solution.py:240
  28.5 1.3 %collective-permute-start.3 = (f32[32,128]{1,0:T(8,128)S(1)}, f32[32,128]{1,0:T(8,128)S(1)}, u32[]{:S(2)}, u32[]{:S(2)}) collective-permute-start(f32[32,128]{1,0:T(8,128)S(1)} %shard_map.77.refs_4_), channel_id=1, source_target_pairs={{256,65},{257,64},{258,67},{259,66},{260,69},{261,68},{262,71},{26... | collective-permute-start | bytes 49160 | tf_op jit(solution)/shard_map/ppermute | solution.py:240
  29.8 1.3 %collective-permute-start.2 = (f32[32,128]{1,0:T(8,128)S(1)}, f32[32,128]{1,0:T(8,128)S(1)}, u32[]{:S(2)}, u32[]{:S(2)}) collective-permute-start(f32[32,128]{1,0:T(8,128)S(1)} %shard_map.77.refs_4_), channel_id=1, source_target_pairs={{384,0},{385,1},{386,2},{387,3},{388,4},{389,5},{390,6},{391,7},{3... | collective-permute-start | bytes 49160 | tf_op jit(solution)/shard_map/ppermute | solution.py:240
  31.1 1.6 %shard_map.78 = (bf16[128,128]{1,0:T(8,128)(2,1)S(1)}, bf16[128,128]{1,0:T(8,128)(2,1)S(1)}, f32[32,128]{1,0:T(8,128)S(1)}) custom-call(s32[1]{0:T(128)} %bitcast.far_ref.refs_0_, s32[1]{0:T(128)S(6)} %add.35.refs_1_, f32[128]{0:T(128)} %refs_2_.3, bf16[512,128]{1,0:T(8,128)(2,1)S(1)} %bitcast.13, f32[32,128]{1,0:T(8,128)S(1)} %shard_map.77.refs_4_), custom_call_target="tpu_custom_call" | custom-call | tf_op jit(solution)/shard_map/pallas_call | solution.py:278
  32.7 4.9 %collective-permute-done.right_ref = f32[32,128]{1,0:T(8,128)S(1)} collective-permute-done((f32[32,128]{1,0:T(8,128)S(1)}, f32[32,128]{1,0:T(8,128)S(1)}, u32[]{:S(2)}, u32[]{:S(2)}) %collective-permute-start) | collective-permute-done | bytes 16416 | tf_op jit(solution)/shard_map/ppermute | solution.py:240
  37.6 2.7 %collective-permute-start.1 = (f32[32,128]{1,0:T(8,128)S(1)}, f32[32,128]{1,0:T(8,128)S(1)}, u32[]{:S(2)}, u32[]{:S(2)}) collective-permute-start(f32[32,128]{1,0:T(8,128)S(1)} %shard_map.79.front_ref), channel_id=1, source_target_pairs={{0,384},{1,385},{2,386},{3,387},{4,388},{5,389},{6,390},{7,391},{8... | collective-permute-start | bytes 49160 | tf_op jit(solution)/shard_map/ppermute | solution.py:240
  40.3 0.4 collective-permute-done.3.left_ref
  40.7 0.0 collective-permute-done.2.right_ref
  40.7 1.3 %collective-permute-start.4 = (f32[32,128]{1,0:T(8,128)S(1)}, f32[32,128]{1,0:T(8,128)S(1)}, u32[]{:S(2)}, u32[]{:S(2)}) collective-permute-start(f32[32,128]{1,0:T(8,128)S(1)} %shard_map.82.refs_3_), channel_id=1, source_target_pairs={{0,129},{1,128},{2,131},{3,130},{4,133},{5,132},{6,135},{7,134},{8... | collective-permute-start | bytes 49160 | tf_op jit(solution)/shard_map/ppermute | solution.py:240
  42.0 0.0 collective-permute-done.1.front_ref
  42.0 0.7 %collective-permute-start.5 = (f32[32,128]{1,0:T(8,128)S(1)}, f32[32,128]{1,0:T(8,128)S(1)}, u32[]{:S(2)}, u32[]{:S(2)}) collective-permute-start(f32[32,128]{1,0:T(8,128)S(1)} %shard_map.80.refs_6_), channel_id=1, source_target_pairs={{384,321},{385,320},{386,323},{387,322},{388,325},{389,324},{390,3... | collective-permute-start | bytes 49160 | tf_op jit(solution)/shard_map/ppermute | solution.py:240
  42.7 0.1 collective-permute-done.4.refs_4_
  42.8 0.0 collective-permute-done.5.refs_5_
  42.9 17.3 %all_to_all.23 = bf16[128,4,128]{2,1,0:T(4,128)(2,1)S(1)} all-to-all(bf16[128,4,128]{2,1,0:T(4,128)(2,1)S(1)} %bitcast.15), channel_id=1, replica_groups=mesh['far'=4,'near'=4,'seq'=32] {'near','seq'}, dimensions={0} | all-to-all | bytes 262144 | tf_op jit(solution)/shard_map/all_to_all | solution.py:299
  60.2 0.7 %shard_map.84 = (bf16[128,128]{1,0:T(8,128)(2,1)}, bf16[128,128]{1,0:T(8,128)(2,1)}, f32[128,128]{1,0:T(8,128)}) custom-call(s32[1]{0:T(128)} %bitcast.far_ref.refs_0_, bf16[512,128]{1,0:T(8,128)(2,1)S(1)} %bitcast.16), custom_call_target="tpu_custom_call" | custom-call | tf_op jit(solution)/shard_map/pallas_call | solution.py:300
  (5 shorter events, 0.1 us)
Async XLA Ops:
  27.1 10.5 %collective-permute-start = (f32[32,128]{1,0:T(8,128)S(1)}, f32[32,128]{1,0:T(8,128)S(1)}, u32[]{:S(2)}, u32[]{:S(2)}) collective-permute-start(f32[32,128]{1,0:T(8,128)S(1)} %shard_map.77.refs_4_), channel_id=1, source_target_pairs={{128,1},{129,0},{130,3},{131,2},{132,5},{133,4},{134,7},{135,6},{1... | collective-permute-start | bytes 49160 | tf_op jit(solution)/shard_map/ppermute | solution.py:240
  28.5 12.2 %collective-permute-start.3 = (f32[32,128]{1,0:T(8,128)S(1)}, f32[32,128]{1,0:T(8,128)S(1)}, u32[]{:S(2)}, u32[]{:S(2)}) collective-permute-start(f32[32,128]{1,0:T(8,128)S(1)} %shard_map.77.refs_4_), channel_id=1, source_target_pairs={{256,65},{257,64},{258,67},{259,66},{260,69},{261,68},{262,71},{26... | collective-permute-start | bytes 49160 | tf_op jit(solution)/shard_map/ppermute | solution.py:240
  29.8 10.9 %collective-permute-start.2 = (f32[32,128]{1,0:T(8,128)S(1)}, f32[32,128]{1,0:T(8,128)S(1)}, u32[]{:S(2)}, u32[]{:S(2)}) collective-permute-start(f32[32,128]{1,0:T(8,128)S(1)} %shard_map.77.refs_4_), channel_id=1, source_target_pairs={{384,0},{385,1},{386,2},{387,3},{388,4},{389,5},{390,6},{391,7},{3... | collective-permute-start | bytes 49160 | tf_op jit(solution)/shard_map/ppermute | solution.py:240
  37.6 4.4 %collective-permute-start.1 = (f32[32,128]{1,0:T(8,128)S(1)}, f32[32,128]{1,0:T(8,128)S(1)}, u32[]{:S(2)}, u32[]{:S(2)}) collective-permute-start(f32[32,128]{1,0:T(8,128)S(1)} %shard_map.79.front_ref), channel_id=1, source_target_pairs={{0,384},{1,385},{2,386},{3,387},{4,388},{5,389},{6,390},{7,391},{8... | collective-permute-start | bytes 49160 | tf_op jit(solution)/shard_map/ppermute | solution.py:240
  40.7 2.1 %collective-permute-start.4 = (f32[32,128]{1,0:T(8,128)S(1)}, f32[32,128]{1,0:T(8,128)S(1)}, u32[]{:S(2)}, u32[]{:S(2)}) collective-permute-start(f32[32,128]{1,0:T(8,128)S(1)} %shard_map.82.refs_3_), channel_id=1, source_target_pairs={{0,129},{1,128},{2,131},{3,130},{4,133},{5,132},{6,135},{7,134},{8... | collective-permute-start | bytes 49160 | tf_op jit(solution)/shard_map/ppermute | solution.py:240
  42.0 0.8 %collective-permute-start.5 = (f32[32,128]{1,0:T(8,128)S(1)}, f32[32,128]{1,0:T(8,128)S(1)}, u32[]{:S(2)}, u32[]{:S(2)}) collective-permute-start(f32[32,128]{1,0:T(8,128)S(1)} %shard_map.80.refs_6_), channel_id=1, source_target_pairs={{384,321},{385,320},{386,323},{387,322},{388,325},{389,324},{390,3... | collective-permute-start | bytes 49160 | tf_op jit(solution)/shard_map/ppermute | solution.py:240

commit v9 on v8

--- a/solution.py
+++ b/solution.py
@@ -18,7 +18,7 @@
 
 
 def swaps(group):
-    return (group + 1) // 2 % 2
+    return (group + 3) // 4
 
 
 def turns(group):
@@ -173,15 +173,16 @@
     out_ref[...] = left_ref[...] + right_ref[...]
 
 
-def sum_kernel(front_ref, left_ref, right_ref, out_ref):
-    out_ref[...] = front_ref[...] + (left_ref[...] + right_ref[...])
+def last_kernel(pair_ref, own_ref, from_2_ref, after_ref, out_ref):
+    out_ref[...] = (pair_ref[...] + own_ref[...]) + from_2_ref[...]
 
 
 def spread_kernel(blocks, far_ref, gate_ref, input_ref, *refs):
     *sums, out_ref, rows = refs
     count = GROUP * blocks
     group = far_ref[0]
-    on_0, on_1, on_2, on_3 = [ref[...] for ref in sums]
+    three, from_2, early, first, on_2, on_3 = [ref[...] for ref in sums]
+    on_0, on_1 = three + from_2, early + first
     filt = jnp.where(group < 2, jnp.where(group == 0, on_0, on_1), jnp.where(group == 2, on_2, on_3))
     high = filt.astype(BF16).astype(F32)
     low = filt - high
@@ -282,20 +283,20 @@
     from_3_or_2 = send(filt, (3, 0), (2, 3))
     from_1 = send(filt, (1, 0))
     pair = call(add_kernel, part, [VMEM] * 2, [])(same, from_1)
-    first = send(pair, (0, 3))
-    total = call(sum_kernel, part, [VMEM] * 3, [])(pair, from_2, from_3_or_2)
-    to_1 = send(total, (0, 1))
-    total_3 = call(sum_kernel, part, [VMEM] * 3, [])(first, same, from_3_or_2)
+    first = send(pair, (0, 3), (2, 1))
+    three = call(add_kernel, part, [VMEM] * 2, [])(pair, from_3_or_2)
+    early = send(three, (0, 1))
+    total_3 = call(last_kernel, part, [VMEM] * 4, [])(first, same, from_3_or_2, from_2)
     to_2 = send(total_3, (3, 2))
     gate, d_in = call(
         lambda *refs: late_kernel(blocks, *refs), (out, out), [SMEM, SMEM, HBM] + [VMEM] * 4, scratch
-    )(far, chan, gain, packed, gate, d_in, total_3)
+    )(far, chan, gain, packed, gate, d_in, three)
     packed = call(
         lambda *refs: spread_kernel(blocks, *refs),
         shape((count * ROLES, LANES), BF16),
-        [SMEM] + [VMEM] * 6,
+        [SMEM] + [VMEM] * 8,
         [rows],
-    )(far, gate, d_in, total, to_1, to_2, total_3)
+    )(far, gate, d_in, three, from_2, early, first, to_2, total_3)
     packed = lax.all_to_all(packed, ("near", "seq"), 0, 0, tiled=True)
     d_input, d_gate, d_filter = call(
         unpack_kernel,

time: 61.3 us -> 60.6 us (0.989)
  blocking collectives: 41.9 us -> 40.9 us
    all_to_all x2, blocking collectives: 41.9 us -> 40.9 us  [body(): packed = lax.all_to_all(packed, ('near', 'seq'), 0, 0, tiled=True)]
  transfers between devices with their start and end apart: 6 -> 6, of which waited for: 3 -> 2; matrix products, arithmetic and copies ran while one was open for 0% -> 0% of each run, Pallas kernels for 3% -> 3%
where the time goes in v9:
time: 60.6 us; the launch traced here: 59.9 us
  blocking collectives  40.9 us (67%)
  starting transfers between devices  8.93 us (15%)
  waiting for transfers between devices  5.03 us (8%)
  Pallas kernels  4.26 us (7%)
  between operations  0.83 us (1%)
    all_to_all x2, blocking collectives, body(): packed = lax.all_to_all(packed, ('near', 'seq'), 0, 0, tiled=True)  40.9 us
    ppermute x6, starting transfers between devices, send(): return lax.ppermute(array, ('far', 'near', 'seq'), pairs)  8.93 us
    ppermute x6, waiting for transfers between devices, send(): return lax.ppermute(array, ('far', 'near', 'seq'), pairs)  5.03 us
    pallas_call x1, Pallas kernels, body(): call(lambda *refs: early_kernel(blocks, *refs), (out, out, part), [SMEM,...  1.58 us
  transfers between devices with their start and end apart: 6, of which 2 were waited for; matrix products, arithmetic and copies ran while one was open for 0% of the time, Pallas kernels for 3%

profile of v9, /device:TPU:1, one launch (start us, length us, event | category | flops | bytes accessed | tf_op | source)
XLA Modules:
  0.0 59.9 jit_solution(13134372467391420118)
XLA Ops:
  0.6 0.9 %shard_map.76 = bf16[512,128]{1,0:T(8,128)(2,1)S(1)} custom-call(s32[1]{0:T(128)} %bitcast.far_ref.refs_0_, bf16[128,128]{1,0:T(8,128)(2,1)} %bitcast.18, bf16[128,128]{1,0:T(8,128)(2,1)} %bitcast.19, bf16[128,128]{1,0:T(8,128)(2,1)} %bitcast.20, bf16[128,128]{1,0:T(8,128)(2,1)} %k_ref.1), custom_call_target="tpu_custom_call" | custom-call | tf_op jit(solution)/shard_map/pallas_call | solution.py:250
  1.5 24.6 %all_to_all.22 = bf16[128,4,128]{2,1,0:T(4,128)(2,1)S(1)} all-to-all(bf16[128,4,128]{2,1,0:T(4,128)(2,1)S(1)} %bitcast.17), channel_id=1, replica_groups=mesh['far'=4,'near'=4,'seq'=32] {'near','seq'}, dimensions={0} | all-to-all | bytes 262144 | tf_op jit(solution)/shard_map/all_to_all | solution.py:260
  26.1 1.0 %shard_map.77.refs_4_ = f32[32,128]{1,0:T(8,128)S(1)} custom-call(bf16[512,128]{1,0:T(8,128)(2,1)S(1)} %bitcast.12), custom_call_target="tpu_custom_call" | custom-call | tf_op jit(solution)/shard_map/pallas_call | solution.py:261
  27.1 1.3 %collective-permute-start = (f32[32,128]{1,0:T(8,128)S(1)}, f32[32,128]{1,0:T(8,128)S(1)}, u32[]{:S(2)}, u32[]{:S(2)}) collective-permute-start(f32[32,128]{1,0:T(8,128)S(1)} %shard_map.77.refs_4_), channel_id=1, source_target_pairs={{128,1},{129,0},{130,3},{131,2},{132,5},{133,4},{134,7},{135,6},{1... | collective-permute-start | bytes 49160 | tf_op jit(solution)/shard_map/ppermute | solution.py:241
  28.5 1.3 %collective-permute-start.2 = (f32[32,128]{1,0:T(8,128)S(1)}, f32[32,128]{1,0:T(8,128)S(1)}, u32[]{:S(2)}, u32[]{:S(2)}) collective-permute-start(f32[32,128]{1,0:T(8,128)S(1)} %shard_map.77.refs_4_), channel_id=1, source_target_pairs={{256,65},{257,64},{258,67},{259,66},{260,69},{261,68},{262,71},{26... | collective-permute-start | bytes 49160 | tf_op jit(solution)/shard_map/ppermute | solution.py:241
  29.8 1.3 %collective-permute-start.1 = (f32[32,128]{1,0:T(8,128)S(1)}, f32[32,128]{1,0:T(8,128)S(1)}, u32[]{:S(2)}, u32[]{:S(2)}) collective-permute-start(f32[32,128]{1,0:T(8,128)S(1)} %shard_map.77.refs_4_), channel_id=1, source_target_pairs={{384,1},{385,0},{386,3},{387,2},{388,5},{389,4},{390,7},{391,6},{3... | collective-permute-start | bytes 49160 | tf_op jit(solution)/shard_map/ppermute | solution.py:241
  31.1 1.6 %shard_map.78 = (bf16[128,128]{1,0:T(8,128)(2,1)S(1)}, bf16[128,128]{1,0:T(8,128)(2,1)S(1)}, f32[32,128]{1,0:T(8,128)S(1)}) custom-call(s32[1]{0:T(128)} %bitcast.far_ref.refs_0_, s32[1]{0:T(128)S(6)} %add.30.refs_1_, f32[128]{0:T(128)} %refs_2_.3, bf16[512,128]{1,0:T(8,128)(2,1)S(1)} %bitcast.13, f32[32,128]{1,0:T(8,128)S(1)} %shard_map.77.refs_4_), custom_call_target="tpu_custom_call" | custom-call | tf_op jit(solution)/shard_map/pallas_call | solution.py:279
  32.7 4.9 %collective-permute-done.right_ref = f32[32,128]{1,0:T(8,128)S(1)} collective-permute-done((f32[32,128]{1,0:T(8,128)S(1)}, f32[32,128]{1,0:T(8,128)S(1)}, u32[]{:S(2)}, u32[]{:S(2)}) %collective-permute-start) | collective-permute-done | bytes 16416 | tf_op jit(solution)/shard_map/ppermute | solution.py:241
  37.6 3.1 %collective-permute-start.4 = (f32[32,128]{1,0:T(8,128)S(1)}, f32[32,128]{1,0:T(8,128)S(1)}, u32[]{:S(2)}, u32[]{:S(2)}) collective-permute-start(f32[32,128]{1,0:T(8,128)S(1)} %shard_map.79.left_ref), channel_id=1, source_target_pairs={{0,385},{1,384},{2,387},{3,386},{4,389},{5,388},{6,391},{7,390},{8... | collective-permute-start | bytes 49160 | tf_op jit(solution)/shard_map/ppermute | solution.py:241
  40.7 0.0 collective-permute-done.1.right_ref.from_2_ref
  40.7 1.3 %collective-permute-start.3 = (f32[32,128]{1,0:T(8,128)S(1)}, f32[32,128]{1,0:T(8,128)S(1)}, u32[]{:S(2)}, u32[]{:S(2)}) collective-permute-start(f32[32,128]{1,0:T(8,128)S(1)} %shard_map.80.refs_6_.refs_3_), channel_id=1, source_target_pairs={{0,129},{1,128},{2,131},{3,130},{4,133},{5,132},{6,135},{7,134},{8... | collective-permute-start | bytes 49160 | tf_op jit(solution)/shard_map/ppermute | solution.py:241
  42.0 0.0 collective-permute-done.2.after_ref.refs_4_
  42.0 0.0 collective-permute-done.4.pair_ref.refs_6_
  42.1 0.7 %collective-permute-start.5 = (f32[32,128]{1,0:T(8,128)S(1)}, f32[32,128]{1,0:T(8,128)S(1)}, u32[]{:S(2)}, u32[]{:S(2)}) collective-permute-start(f32[32,128]{1,0:T(8,128)S(1)} %shard_map.82.refs_8_), channel_id=1, source_target_pairs={{384,320},{385,321},{386,322},{387,323},{388,324},{389,325},{390,3... | collective-permute-start | bytes 49160 | tf_op jit(solution)/shard_map/ppermute | solution.py:241
  42.8 0.1 collective-permute-done.3.refs_5_
  42.9 0.0 collective-permute-done.5.refs_7_
  42.9 16.3 %all_to_all.23 = bf16[128,4,128]{2,1,0:T(4,128)(2,1)S(1)} all-to-all(bf16[128,4,128]{2,1,0:T(4,128)(2,1)S(1)} %bitcast.15), channel_id=1, replica_groups=mesh['far'=4,'near'=4,'seq'=32] {'near','seq'}, dimensions={0} | all-to-all | bytes 262144 | tf_op jit(solution)/shard_map/all_to_all | solution.py:300
  59.2 0.7 %shard_map.84 = (bf16[128,128]{1,0:T(8,128)(2,1)}, bf16[128,128]{1,0:T(8,128)(2,1)}, f32[128,128]{1,0:T(8,128)}) custom-call(s32[1]{0:T(128)} %bitcast.far_ref.refs_0_, bf16[512,128]{1,0:T(8,128)(2,1)S(1)} %bitcast.16), custom_call_target="tpu_custom_call" | custom-call | tf_op jit(solution)/shard_map/pallas_call | solution.py:301
  (5 shorter events, 0.1 us)
Async XLA Ops:
  27.1 10.5 %collective-permute-start = (f32[32,128]{1,0:T(8,128)S(1)}, f32[32,128]{1,0:T(8,128)S(1)}, u32[]{:S(2)}, u32[]{:S(2)}) collective-permute-start(f32[32,128]{1,0:T(8,128)S(1)} %shard_map.77.refs_4_), channel_id=1, source_target_pairs={{128,1},{129,0},{130,3},{131,2},{132,5},{133,4},{134,7},{135,6},{1... | collective-permute-start | bytes 49160 | tf_op jit(solution)/shard_map/ppermute | solution.py:241
  28.5 13.5 %collective-permute-start.2 = (f32[32,128]{1,0:T(8,128)S(1)}, f32[32,128]{1,0:T(8,128)S(1)}, u32[]{:S(2)}, u32[]{:S(2)}) collective-permute-start(f32[32,128]{1,0:T(8,128)S(1)} %shard_map.77.refs_4_), channel_id=1, source_target_pairs={{256,65},{257,64},{258,67},{259,66},{260,69},{261,68},{262,71},{26... | collective-permute-start | bytes 49160 | tf_op jit(solution)/shard_map/ppermute | solution.py:241
  29.8 10.9 %collective-permute-start.1 = (f32[32,128]{1,0:T(8,128)S(1)}, f32[32,128]{1,0:T(8,128)S(1)}, u32[]{:S(2)}, u32[]{:S(2)}) collective-permute-start(f32[32,128]{1,0:T(8,128)S(1)} %shard_map.77.refs_4_), channel_id=1, source_target_pairs={{384,1},{385,0},{386,3},{387,2},{388,5},{389,4},{390,7},{391,6},{3... | collective-permute-start | bytes 49160 | tf_op jit(solution)/shard_map/ppermute | solution.py:241
  37.6 4.4 %collective-permute-start.4 = (f32[32,128]{1,0:T(8,128)S(1)}, f32[32,128]{1,0:T(8,128)S(1)}, u32[]{:S(2)}, u32[]{:S(2)}) collective-permute-start(f32[32,128]{1,0:T(8,128)S(1)} %shard_map.79.left_ref), channel_id=1, source_target_pairs={{0,385},{1,384},{2,387},{3,386},{4,389},{5,388},{6,391},{7,390},{8... | collective-permute-start | bytes 49160 | tf_op jit(solution)/shard_map/ppermute | solution.py:241
  40.7 2.1 %collective-permute-start.3 = (f32[32,128]{1,0:T(8,128)S(1)}, f32[32,128]{1,0:T(8,128)S(1)}, u32[]{:S(2)}, u32[]{:S(2)}) collective-permute-start(f32[32,128]{1,0:T(8,128)S(1)} %shard_map.80.refs_6_.refs_3_), channel_id=1, source_target_pairs={{0,129},{1,128},{2,131},{3,130},{4,133},{5,132},{6,135},{7,134},{8... | collective-permute-start | bytes 49160 | tf_op jit(solution)/shard_map/ppermute | solution.py:241
  42.1 0.8 %collective-permute-start.5 = (f32[32,128]{1,0:T(8,128)S(1)}, f32[32,128]{1,0:T(8,128)S(1)}, u32[]{:S(2)}, u32[]{:S(2)}) collective-permute-start(f32[32,128]{1,0:T(8,128)S(1)} %shard_map.82.refs_8_), channel_id=1, source_target_pairs={{384,320},{385,321},{386,322},{387,323},{388,324},{389,325},{390,3... | collective-permute-start | bytes 49160 | tf_op jit(solution)/shard_map/ppermute | solution.py:241

commit v10 on v9

--- a/solution.py
+++ b/solution.py
@@ -18,7 +18,7 @@
 
 
 def swaps(group):
-    return (group + 3) // 4
+    return group // 2 * (1 - group % 2)
 
 
 def turns(group):
@@ -173,16 +173,16 @@
     out_ref[...] = left_ref[...] + right_ref[...]
 
 
-def last_kernel(pair_ref, own_ref, from_2_ref, after_ref, out_ref):
-    out_ref[...] = (pair_ref[...] + own_ref[...]) + from_2_ref[...]
+def last_kernel(pair_ref, own_ref, after_ref, out_ref):
+    out_ref[...] = pair_ref[...] + own_ref[...]
 
 
 def spread_kernel(blocks, far_ref, gate_ref, input_ref, *refs):
     *sums, out_ref, rows = refs
     count = GROUP * blocks
     group = far_ref[0]
-    three, from_2, early, first, on_2, on_3 = [ref[...] for ref in sums]
-    on_0, on_1 = three + from_2, early + first
+    own, from_2, three, early, first, three_3, to_2 = [ref[...] for ref in sums]
+    on_0, on_1, on_2, on_3 = three + from_2, early + first, to_2 + own, three_3 + early
     filt = jnp.where(group < 2, jnp.where(group == 0, on_0, on_1), jnp.where(group == 2, on_2, on_3))
     high = filt.astype(BF16).astype(F32)
     low = filt - high
@@ -280,23 +280,23 @@
         lambda *refs: early_kernel(blocks, *refs), (out, out, part), [SMEM, SMEM, HBM, VMEM, VMEM], scratch
     )(far, chan, gain, packed, filt)
     from_2 = send(filt, (2, 0))
-    from_3_or_2 = send(filt, (3, 0), (2, 3))
+    from_3 = send(filt, (3, 0))
     from_1 = send(filt, (1, 0))
     pair = call(add_kernel, part, [VMEM] * 2, [])(same, from_1)
     first = send(pair, (0, 3), (2, 1))
-    three = call(add_kernel, part, [VMEM] * 2, [])(pair, from_3_or_2)
-    early = send(three, (0, 1))
-    total_3 = call(last_kernel, part, [VMEM] * 4, [])(first, same, from_3_or_2, from_2)
-    to_2 = send(total_3, (3, 2))
+    three = call(add_kernel, part, [VMEM] * 2, [])(pair, from_3)
+    early = send(three, (0, 1), (2, 3))
+    three_3 = call(last_kernel, part, [VMEM] * 3, [])(first, same, from_2)
+    to_2 = send(three_3, (3, 2))
     gate, d_in = call(
         lambda *refs: late_kernel(blocks, *refs), (out, out), [SMEM, SMEM, HBM] + [VMEM] * 4, scratch
     )(far, chan, gain, packed, gate, d_in, three)
     packed = call(
         lambda *refs: spread_kernel(blocks, *refs),
         shape((count * ROLES, LANES), BF16),
-        [SMEM] + [VMEM] * 8,
+        [SMEM] + [VMEM] * 9,
         [rows],
-    )(far, gate, d_in, three, from_2, early, first, to_2, total_3)
+    )(far, gate, d_in, same, from_2, three, early, first, three_3, to_2)
     packed = lax.all_to_all(packed, ("near", "seq"), 0, 0, tiled=True)
     d_input, d_gate, d_filter = call(
         unpack_kernel,

time: 60.6 us -> 59.9 us (0.988)
  waiting for transfers between devices: 5.03 us -> 4.16 us
  blocking collectives: 40.9 us -> 41.6 us
    ppermute x6, waiting for transfers between devices: 5.03 us -> 4.16 us  [send(): return lax.ppermute(array, ('far', 'near', 'seq'), pairs)]
    all_to_all x2, blocking collectives: 40.9 us -> 41.6 us  [body(): packed = lax.all_to_all(packed, ('near', 'seq'), 0, 0, tiled=True)]
where the time goes in v10:
time: 59.9 us; the launch traced here: 59.6 us
  blocking collectives  41.6 us (69%)
  starting transfers between devices  8.74 us (15%)
  Pallas kernels  4.27 us (7%)
  waiting for transfers between devices  4.16 us (7%)
  between operations  0.83 us (1%)
    all_to_all x2, blocking collectives, body(): packed = lax.all_to_all(packed, ('near', 'seq'), 0, 0, tiled=True)  41.6 us
    ppermute x6, starting transfers between devices, send(): return lax.ppermute(array, ('far', 'near', 'seq'), pairs)  8.74 us
    ppermute x6, waiting for transfers between devices, send(): return lax.ppermute(array, ('far', 'near', 'seq'), pairs)  4.16 us
    pallas_call x1, Pallas kernels, body(): call(lambda *refs: early_kernel(blocks, *refs), (out, out, part), [SMEM,...  1.58 us
  transfers between devices with their start and end apart: 6, of which 2 were waited for; matrix products, arithmetic and copies ran while one was open for 0% of the time, Pallas kernels for 3%

profile of v10, /device:TPU:1, one launch (start us, length us, event | category | flops | bytes accessed | tf_op | source)
XLA Modules:
  0.0 59.6 jit_solution(6255257324126154678)
XLA Ops:
  0.6 0.9 %shard_map.76 = bf16[512,128]{1,0:T(8,128)(2,1)S(1)} custom-call(s32[1]{0:T(128)} %bitcast.far_ref.refs_0_, bf16[128,128]{1,0:T(8,128)(2,1)} %bitcast.18, bf16[128,128]{1,0:T(8,128)(2,1)} %bitcast.19, bf16[128,128]{1,0:T(8,128)(2,1)} %bitcast.20, bf16[128,128]{1,0:T(8,128)(2,1)} %k_ref.1), custom_call_target="tpu_custom_call" | custom-call | tf_op jit(solution)/shard_map/pallas_call | solution.py:250
  1.5 24.6 %all_to_all.22 = bf16[128,4,128]{2,1,0:T(4,128)(2,1)S(1)} all-to-all(bf16[128,4,128]{2,1,0:T(4,128)(2,1)S(1)} %bitcast.17), channel_id=1, replica_groups=mesh['far'=4,'near'=4,'seq'=32] {'near','seq'}, dimensions={0} | all-to-all | bytes 262144 | tf_op jit(solution)/shard_map/all_to_all | solution.py:260
  26.1 1.0 %shard_map.77.refs_4_ = f32[32,128]{1,0:T(8,128)S(1)} custom-call(bf16[512,128]{1,0:T(8,128)(2,1)S(1)} %bitcast.12), custom_call_target="tpu_custom_call" | custom-call | tf_op jit(solution)/shard_map/pallas_call | solution.py:261
  27.1 1.3 %collective-permute-start = (f32[32,128]{1,0:T(8,128)S(1)}, f32[32,128]{1,0:T(8,128)S(1)}, u32[]{:S(2)}, u32[]{:S(2)}) collective-permute-start(f32[32,128]{1,0:T(8,128)S(1)} %shard_map.77.refs_4_), channel_id=1, source_target_pairs={{128,0},{129,1},{130,2},{131,3},{132,4},{133,5},{134,6},{135,7},{1... | collective-permute-start | bytes 49160 | tf_op jit(solution)/shard_map/ppermute | solution.py:241
  28.5 1.3 %collective-permute-start.2 = (f32[32,128]{1,0:T(8,128)S(1)}, f32[32,128]{1,0:T(8,128)S(1)}, u32[]{:S(2)}, u32[]{:S(2)}) collective-permute-start(f32[32,128]{1,0:T(8,128)S(1)} %shard_map.77.refs_4_), channel_id=1, source_target_pairs={{256,65},{257,64},{258,67},{259,66},{260,69},{261,68},{262,71},{26... | collective-permute-start | bytes 49160 | tf_op jit(solution)/shard_map/ppermute | solution.py:241
  29.8 1.3 %collective-permute-start.1 = (f32[32,128]{1,0:T(8,128)S(1)}, f32[32,128]{1,0:T(8,128)S(1)}, u32[]{:S(2)}, u32[]{:S(2)}) collective-permute-start(f32[32,128]{1,0:T(8,128)S(1)} %shard_map.77.refs_4_), channel_id=1, source_target_pairs={{384,0},{385,1},{386,2},{387,3},{388,4},{389,5},{390,6},{391,7},{3... | collective-permute-start | bytes 49160 | tf_op jit(solution)/shard_map/ppermute | solution.py:241
  31.1 1.6 %shard_map.78 = (bf16[128,128]{1,0:T(8,128)(2,1)S(1)}, bf16[128,128]{1,0:T(8,128)(2,1)S(1)}, f32[32,128]{1,0:T(8,128)S(1)}) custom-call(s32[1]{0:T(128)} %bitcast.far_ref.refs_0_, s32[1]{0:T(128)S(6)} %add.27.refs_1_, f32[128]{0:T(128)} %refs_2_.3, bf16[512,128]{1,0:T(8,128)(2,1)S(1)} %bitcast.13, f32[32,128]{1,0:T(8,128)S(1)} %shard_map.77.refs_4_), custom_call_target="tpu_custom_call" | custom-call | tf_op jit(solution)/shard_map/pallas_call | solution.py:279
  32.7 4.0 %collective-permute-done.right_ref = f32[32,128]{1,0:T(8,128)S(1)} collective-permute-done((f32[32,128]{1,0:T(8,128)S(1)}, f32[32,128]{1,0:T(8,128)S(1)}, u32[]{:S(2)}, u32[]{:S(2)}) %collective-permute-start) | collective-permute-done | bytes 16416 | tf_op jit(solution)/shard_map/ppermute | solution.py:241
  36.7 2.9 %collective-permute-start.4 = (f32[32,128]{1,0:T(8,128)S(1)}, f32[32,128]{1,0:T(8,128)S(1)}, u32[]{:S(2)}, u32[]{:S(2)}) collective-permute-start(f32[32,128]{1,0:T(8,128)S(1)} %shard_map.79.left_ref), channel_id=1, source_target_pairs={{0,384},{1,385},{2,386},{3,387},{4,388},{5,389},{6,390},{7,391},{8... | collective-permute-start | bytes 49160 | tf_op jit(solution)/shard_map/ppermute | solution.py:241
  39.6 0.0 collective-permute-done.1.right_ref
  39.7 1.3 %collective-permute-start.3 = (f32[32,128]{1,0:T(8,128)S(1)}, f32[32,128]{1,0:T(8,128)S(1)}, u32[]{:S(2)}, u32[]{:S(2)}) collective-permute-start(f32[32,128]{1,0:T(8,128)S(1)} %shard_map.80.refs_6_.refs_5_), channel_id=1, source_target_pairs={{0,128},{1,129},{2,130},{3,131},{4,132},{5,133},{6,134},{7,135},{8... | collective-permute-start | bytes 49160 | tf_op jit(solution)/shard_map/ppermute | solution.py:241
  41.0 0.0 collective-permute-done.2.after_ref.refs_4_
  41.0 0.0 collective-permute-done.4.pair_ref.refs_7_
  41.0 0.7 %collective-permute-start.5 = (f32[32,128]{1,0:T(8,128)S(1)}, f32[32,128]{1,0:T(8,128)S(1)}, u32[]{:S(2)}, u32[]{:S(2)}) collective-permute-start(f32[32,128]{1,0:T(8,128)S(1)} %shard_map.82.refs_8_), channel_id=1, source_target_pairs={{384,321},{385,320},{386,323},{387,322},{388,325},{389,324},{390,3... | collective-permute-start | bytes 49160 | tf_op jit(solution)/shard_map/ppermute | solution.py:241
  41.7 0.1 collective-permute-done.3.refs_6_
  41.8 0.0 collective-permute-done.5.refs_9_
  41.9 17.0 %all_to_all.23 = bf16[128,4,128]{2,1,0:T(4,128)(2,1)S(1)} all-to-all(bf16[128,4,128]{2,1,0:T(4,128)(2,1)S(1)} %bitcast.15), channel_id=1, replica_groups=mesh['far'=4,'near'=4,'seq'=32] {'near','seq'}, dimensions={0} | all-to-all | bytes 262144 | tf_op jit(solution)/shard_map/all_to_all | solution.py:300
  58.8 0.7 %shard_map.84 = (bf16[128,128]{1,0:T(8,128)(2,1)}, bf16[128,128]{1,0:T(8,128)(2,1)}, f32[128,128]{1,0:T(8,128)}) custom-call(s32[1]{0:T(128)} %bitcast.far_ref.refs_0_, bf16[512,128]{1,0:T(8,128)(2,1)S(1)} %bitcast.16), custom_call_target="tpu_custom_call" | custom-call | tf_op jit(solution)/shard_map/pallas_call | solution.py:301
  (5 shorter events, 0.1 us)
Async XLA Ops:
  27.1 9.6 %collective-permute-start = (f32[32,128]{1,0:T(8,128)S(1)}, f32[32,128]{1,0:T(8,128)S(1)}, u32[]{:S(2)}, u32[]{:S(2)}) collective-permute-start(f32[32,128]{1,0:T(8,128)S(1)} %shard_map.77.refs_4_), channel_id=1, source_target_pairs={{128,0},{129,1},{130,2},{131,3},{132,4},{133,5},{134,6},{135,7},{1... | collective-permute-start | bytes 49160 | tf_op jit(solution)/shard_map/ppermute | solution.py:241
  28.5 12.5 %collective-permute-start.2 = (f32[32,128]{1,0:T(8,128)S(1)}, f32[32,128]{1,0:T(8,128)S(1)}, u32[]{:S(2)}, u32[]{:S(2)}) collective-permute-start(f32[32,128]{1,0:T(8,128)S(1)} %shard_map.77.refs_4_), channel_id=1, source_target_pairs={{256,65},{257,64},{258,67},{259,66},{260,69},{261,68},{262,71},{26... | collective-permute-start | bytes 49160 | tf_op jit(solution)/shard_map/ppermute | solution.py:241
  29.8 9.9 %collective-permute-start.1 = (f32[32,128]{1,0:T(8,128)S(1)}, f32[32,128]{1,0:T(8,128)S(1)}, u32[]{:S(2)}, u32[]{:S(2)}) collective-permute-start(f32[32,128]{1,0:T(8,128)S(1)} %shard_map.77.refs_4_), channel_id=1, source_target_pairs={{384,0},{385,1},{386,2},{387,3},{388,4},{389,5},{390,6},{391,7},{3... | collective-permute-start | bytes 49160 | tf_op jit(solution)/shard_map/ppermute | solution.py:241
  36.7 4.3 %collective-permute-start.4 = (f32[32,128]{1,0:T(8,128)S(1)}, f32[32,128]{1,0:T(8,128)S(1)}, u32[]{:S(2)}, u32[]{:S(2)}) collective-permute-start(f32[32,128]{1,0:T(8,128)S(1)} %shard_map.79.left_ref), channel_id=1, source_target_pairs={{0,384},{1,385},{2,386},{3,387},{4,388},{5,389},{6,390},{7,391},{8... | collective-permute-start | bytes 49160 | tf_op jit(solution)/shard_map/ppermute | solution.py:241
  39.7 2.1 %collective-permute-start.3 = (f32[32,128]{1,0:T(8,128)S(1)}, f32[32,128]{1,0:T(8,128)S(1)}, u32[]{:S(2)}, u32[]{:S(2)}) collective-permute-start(f32[32,128]{1,0:T(8,128)S(1)} %shard_map.80.refs_6_.refs_5_), channel_id=1, source_target_pairs={{0,128},{1,129},{2,130},{3,131},{4,132},{5,133},{6,134},{7,135},{8... | collective-permute-start | bytes 49160 | tf_op jit(solution)/shard_map/ppermute | solution.py:241
  41.0 0.8 %collective-permute-start.5 = (f32[32,128]{1,0:T(8,128)S(1)}, f32[32,128]{1,0:T(8,128)S(1)}, u32[]{:S(2)}, u32[]{:S(2)}) collective-permute-start(f32[32,128]{1,0:T(8,128)S(1)} %shard_map.82.refs_8_), channel_id=1, source_target_pairs={{384,321},{385,320},{386,323},{387,322},{388,325},{389,324},{390,3... | collective-permute-start | bytes 49160 | tf_op jit(solution)/shard_map/ppermute | solution.py:241

commit v11 on v10

--- a/solution.py
+++ b/solution.py
@@ -18,18 +18,27 @@
 
 
 def swaps(group):
-    return group // 2 * (1 - group % 2)
+    return group % 2
 
 
 def turns(group):
     return group // 2 * (1 - group % 2)
 
 
-def placed(value, group):
+def by_group(group, plain, swapped, turned):
+    pl.when(group == 0)(plain)
+    pl.when(swaps(group) == 1)(swapped)
+    pl.when(turns(group) == 1)(turned)
+
+
+def neighbours(value):
     up, down = jnp.roll(value, -1, axis=0), jnp.roll(value, 1, axis=0)
-    value = jnp.where(swaps(group) == 1, jnp.where(iota(value.shape, 0) % 2 == 0, up, down), value)
+    return jnp.where(iota(value.shape, 0) % 2 == 0, up, down)
+
+
+def halves(value):
     half = value.shape[0] // 2
-    return jnp.where(turns(group) == 1, jnp.concatenate([value[half:], value[:half]], axis=0), value)
+    return jnp.concatenate([value[half:], value[:half]], axis=0)
 
 
 def pack_kernel(far_ref, u_ref, g_ref, y_ref, k_ref, out_ref, landed, rows, sems):
@@ -40,10 +49,15 @@
     ]
     for copy in copies:
         copy.start()
-    for role, copy in enumerate(copies):
+    for copy in copies:
         copy.wait()
-        rows[pl.ds(role, chans, stride=ROLES), :] = placed(landed[role].astype(F32), far_ref[0])
-    out_ref[...] = rows[...].astype(BF16)
+
+    def store(order):
+        for role in range(ROLES):
+            rows[pl.ds(role, chans, stride=ROLES), :] = order(landed[role].astype(F32))
+        out_ref[...] = rows[...].astype(BF16)
+
+    by_group(far_ref[0], lambda: store(lambda value: value), lambda: store(neighbours), lambda: store(halves))
 
 
 def flip_rows(count, span):
@@ -198,10 +212,13 @@
 def unpack_kernel(far_ref, in_ref, input_ref, gate_ref, filt_ref, rows):
     chans = input_ref.shape[0]
     rows[...] = in_ref[...].astype(F32)
-    group = far_ref[0]
-    gate_ref[...] = placed(take(rows, 0, chans), group).astype(BF16)
-    input_ref[...] = placed(take(rows, 1, chans), group).astype(BF16)
-    filt_ref[...] = placed(take(rows, 2, chans) + take(rows, 3, chans), group) * (1.0 / 64.0)
+
+    def store(order):
+        gate_ref[...] = order(take(rows, 0, chans)).astype(BF16)
+        input_ref[...] = order(take(rows, 1, chans)).astype(BF16)
+        filt_ref[...] = order(take(rows, 2, chans) + take(rows, 3, chans)) * (1.0 / 64.0)
+
+    by_group(far_ref[0], lambda: store(lambda value: value), lambda: store(neighbours), lambda: store(halves))
 
 
 VMEM = pl.BlockSpec(memory_space=pltpu.VMEM)

time: 59.9 us -> 59.7 us (level)
  waiting for transfers between devices: 4.16 us -> 5.08 us
  blocking collectives: 41.6 us -> 40.9 us
    ppermute x6, waiting for transfers between devices: 4.16 us -> 5.08 us  [send(): return lax.ppermute(array, ('far', 'near', 'seq'), pairs)]
    all_to_all x2, blocking collectives: 41.6 us -> 40.9 us  [body(): packed = lax.all_to_all(packed, ('near', 'seq'), 0, 0, tiled=True)]
where the time goes in v11:
time: 59.7 us; the launch traced here: 59.4 us
  blocking collectives  40.9 us (69%)
  starting transfers between devices  8.3 us (14%)
  waiting for transfers between devices  5.08 us (9%)
  Pallas kernels  4.24 us (7%)
  between operations  0.83 us (1%)
    all_to_all x2, blocking collectives, body(): packed = lax.all_to_all(packed, ('near', 'seq'), 0, 0, tiled=True)  40.9 us
    ppermute x6, starting transfers between devices, send(): return lax.ppermute(array, ('far', 'near', 'seq'), pairs)  8.3 us
    ppermute x6, waiting for transfers between devices, send(): return lax.ppermute(array, ('far', 'near', 'seq'), pairs)  5.08 us
    pallas_call x1, Pallas kernels, body(): call(lambda *refs: early_kernel(blocks, *refs), (out, out, part), [SMEM,...  1.58 us
  transfers between devices with their start and end apart: 6, of which 2 were waited for; matrix products, arithmetic and copies ran while one was open for 0% of the time, Pallas kernels for 3%

profile of v11, /device:TPU:1, one launch (start us, length us, event | category | flops | bytes accessed | tf_op | source)
XLA Modules:
  0.0 59.4 jit_solution(795129508848841889)
XLA Ops:
  0.6 0.9 %shard_map.76 = bf16[512,128]{1,0:T(8,128)(2,1)S(1)} custom-call(s32[1]{0:T(128)} %bitcast.far_ref.refs_0_, bf16[128,128]{1,0:T(8,128)(2,1)} %bitcast.18, bf16[128,128]{1,0:T(8,128)(2,1)} %bitcast.19, bf16[128,128]{1,0:T(8,128)(2,1)} %bitcast.20, bf16[128,128]{1,0:T(8,128)(2,1)} %k_ref.1), custom_call_target="tpu_custom_call" | custom-call | tf_op jit(solution)/shard_map/pallas_call | solution.py:267
  1.5 24.6 %all_to_all.22 = bf16[128,4,128]{2,1,0:T(4,128)(2,1)S(1)} all-to-all(bf16[128,4,128]{2,1,0:T(4,128)(2,1)S(1)} %bitcast.17), channel_id=1, replica_groups=mesh['far'=4,'near'=4,'seq'=32] {'near','seq'}, dimensions={0} | all-to-all | bytes 262144 | tf_op jit(solution)/shard_map/all_to_all | solution.py:277
  26.1 1.0 %shard_map.77.refs_4_ = f32[32,128]{1,0:T(8,128)S(1)} custom-call(bf16[512,128]{1,0:T(8,128)(2,1)S(1)} %bitcast.12), custom_call_target="tpu_custom_call" | custom-call | tf_op jit(solution)/shard_map/pallas_call | solution.py:278
  27.1 1.3 %collective-permute-start = (f32[32,128]{1,0:T(8,128)S(1)}, f32[32,128]{1,0:T(8,128)S(1)}, u32[]{:S(2)}, u32[]{:S(2)}) collective-permute-start(f32[32,128]{1,0:T(8,128)S(1)} %shard_map.77.refs_4_), channel_id=1, source_target_pairs={{128,1},{129,0},{130,3},{131,2},{132,5},{133,4},{134,7},{135,6},{1... | collective-permute-start | bytes 49160 | tf_op jit(solution)/shard_map/ppermute | solution.py:258
  28.5 1.3 %collective-permute-start.2 = (f32[32,128]{1,0:T(8,128)S(1)}, f32[32,128]{1,0:T(8,128)S(1)}, u32[]{:S(2)}, u32[]{:S(2)}) collective-permute-start(f32[32,128]{1,0:T(8,128)S(1)} %shard_map.77.refs_4_), channel_id=1, source_target_pairs={{256,64},{257,65},{258,66},{259,67},{260,68},{261,69},{262,70},{26... | collective-permute-start | bytes 49160 | tf_op jit(solution)/shard_map/ppermute | solution.py:258
  29.8 1.3 %collective-permute-start.1 = (f32[32,128]{1,0:T(8,128)S(1)}, f32[32,128]{1,0:T(8,128)S(1)}, u32[]{:S(2)}, u32[]{:S(2)}) collective-permute-start(f32[32,128]{1,0:T(8,128)S(1)} %shard_map.77.refs_4_), channel_id=1, source_target_pairs={{384,1},{385,0},{386,3},{387,2},{388,5},{389,4},{390,7},{391,6},{3... | collective-permute-start | bytes 49160 | tf_op jit(solution)/shard_map/ppermute | solution.py:258
  31.1 1.6 %shard_map.78 = (bf16[128,128]{1,0:T(8,128)(2,1)S(1)}, bf16[128,128]{1,0:T(8,128)(2,1)S(1)}, f32[32,128]{1,0:T(8,128)S(1)}) custom-call(s32[1]{0:T(128)} %bitcast.far_ref.refs_0_, s32[1]{0:T(128)S(6)} %add.27.refs_1_, f32[128]{0:T(128)} %refs_2_.3, bf16[512,128]{1,0:T(8,128)(2,1)S(1)} %bitcast.13, f32[32,128]{1,0:T(8,128)S(1)} %shard_map.77.refs_4_), custom_call_target="tpu_custom_call" | custom-call | tf_op jit(solution)/shard_map/pallas_call | solution.py:296
  32.7 5.0 %collective-permute-done.right_ref = f32[32,128]{1,0:T(8,128)S(1)} collective-permute-done((f32[32,128]{1,0:T(8,128)S(1)}, f32[32,128]{1,0:T(8,128)S(1)}, u32[]{:S(2)}, u32[]{:S(2)}) %collective-permute-start) | collective-permute-done | bytes 16416 | tf_op jit(solution)/shard_map/ppermute | solution.py:258
  37.6 2.5 %collective-permute-start.4 = (f32[32,128]{1,0:T(8,128)S(1)}, f32[32,128]{1,0:T(8,128)S(1)}, u32[]{:S(2)}, u32[]{:S(2)}) collective-permute-start(f32[32,128]{1,0:T(8,128)S(1)} %shard_map.79.left_ref), channel_id=1, source_target_pairs={{0,385},{1,384},{2,387},{3,386},{4,389},{5,388},{6,391},{7,390},{8... | collective-permute-start | bytes 49160 | tf_op jit(solution)/shard_map/ppermute | solution.py:258
  40.1 0.0 collective-permute-done.1.right_ref
  40.1 1.3 %collective-permute-start.3 = (f32[32,128]{1,0:T(8,128)S(1)}, f32[32,128]{1,0:T(8,128)S(1)}, u32[]{:S(2)}, u32[]{:S(2)}) collective-permute-start(f32[32,128]{1,0:T(8,128)S(1)} %shard_map.80.refs_6_.refs_5_), channel_id=1, source_target_pairs={{0,129},{1,128},{2,131},{3,130},{4,133},{5,132},{6,135},{7,134},{8... | collective-permute-start | bytes 49160 | tf_op jit(solution)/shard_map/ppermute | solution.py:258
  41.4 0.0 collective-permute-done.2.after_ref.refs_4_
  41.4 0.0 collective-permute-done.4.pair_ref.refs_7_
  41.5 0.7 %collective-permute-start.5 = (f32[32,128]{1,0:T(8,128)S(1)}, f32[32,128]{1,0:T(8,128)S(1)}, u32[]{:S(2)}, u32[]{:S(2)}) collective-permute-start(f32[32,128]{1,0:T(8,128)S(1)} %shard_map.82.refs_8_), channel_id=1, source_target_pairs={{384,321},{385,320},{386,323},{387,322},{388,325},{389,324},{390,3... | collective-permute-start | bytes 49160 | tf_op jit(solution)/shard_map/ppermute | solution.py:258
  42.2 0.1 collective-permute-done.3.refs_6_
  42.3 0.0 collective-permute-done.5.refs_9_
  42.3 16.3 %all_to_all.23 = bf16[128,4,128]{2,1,0:T(4,128)(2,1)S(1)} all-to-all(bf16[128,4,128]{2,1,0:T(4,128)(2,1)S(1)} %bitcast.15), channel_id=1, replica_groups=mesh['far'=4,'near'=4,'seq'=32] {'near','seq'}, dimensions={0} | all-to-all | bytes 262144 | tf_op jit(solution)/shard_map/all_to_all | solution.py:317
  58.7 0.7 %shard_map.84 = (bf16[128,128]{1,0:T(8,128)(2,1)}, bf16[128,128]{1,0:T(8,128)(2,1)}, f32[128,128]{1,0:T(8,128)}) custom-call(s32[1]{0:T(128)} %bitcast.far_ref.refs_0_, bf16[512,128]{1,0:T(8,128)(2,1)S(1)} %bitcast.16), custom_call_target="tpu_custom_call" | custom-call | tf_op jit(solution)/shard_map/pallas_call | solution.py:318
  (5 shorter events, 0.1 us)
Async XLA Ops:
  27.1 10.5 %collective-permute-start = (f32[32,128]{1,0:T(8,128)S(1)}, f32[32,128]{1,0:T(8,128)S(1)}, u32[]{:S(2)}, u32[]{:S(2)}) collective-permute-start(f32[32,128]{1,0:T(8,128)S(1)} %shard_map.77.refs_4_), channel_id=1, source_target_pairs={{128,1},{129,0},{130,3},{131,2},{132,5},{133,4},{134,7},{135,6},{1... | collective-permute-start | bytes 49160 | tf_op jit(solution)/shard_map/ppermute | solution.py:258
  28.5 12.9 %collective-permute-start.2 = (f32[32,128]{1,0:T(8,128)S(1)}, f32[32,128]{1,0:T(8,128)S(1)}, u32[]{:S(2)}, u32[]{:S(2)}) collective-permute-start(f32[32,128]{1,0:T(8,128)S(1)} %shard_map.77.refs_4_), channel_id=1, source_target_pairs={{256,64},{257,65},{258,66},{259,67},{260,68},{261,69},{262,70},{26... | collective-permute-start | bytes 49160 | tf_op jit(solution)/shard_map/ppermute | solution.py:258
  29.8 10.3 %collective-permute-start.1 = (f32[32,128]{1,0:T(8,128)S(1)}, f32[32,128]{1,0:T(8,128)S(1)}, u32[]{:S(2)}, u32[]{:S(2)}) collective-permute-start(f32[32,128]{1,0:T(8,128)S(1)} %shard_map.77.refs_4_), channel_id=1, source_target_pairs={{384,1},{385,0},{386,3},{387,2},{388,5},{389,4},{390,7},{391,6},{3... | collective-permute-start | bytes 49160 | tf_op jit(solution)/shard_map/ppermute | solution.py:258
  37.6 3.8 %collective-permute-start.4 = (f32[32,128]{1,0:T(8,128)S(1)}, f32[32,128]{1,0:T(8,128)S(1)}, u32[]{:S(2)}, u32[]{:S(2)}) collective-permute-start(f32[32,128]{1,0:T(8,128)S(1)} %shard_map.79.left_ref), channel_id=1, source_target_pairs={{0,385},{1,384},{2,387},{3,386},{4,389},{5,388},{6,391},{7,390},{8... | collective-permute-start | bytes 49160 | tf_op jit(solution)/shard_map/ppermute | solution.py:258
  40.1 2.1 %collective-permute-start.3 = (f32[32,128]{1,0:T(8,128)S(1)}, f32[32,128]{1,0:T(8,128)S(1)}, u32[]{:S(2)}, u32[]{:S(2)}) collective-permute-start(f32[32,128]{1,0:T(8,128)S(1)} %shard_map.80.refs_6_.refs_5_), channel_id=1, source_target_pairs={{0,129},{1,128},{2,131},{3,130},{4,133},{5,132},{6,135},{7,134},{8... | collective-permute-start | bytes 49160 | tf_op jit(solution)/shard_map/ppermute | solution.py:258
  41.5 0.8 %collective-permute-start.5 = (f32[32,128]{1,0:T(8,128)S(1)}, f32[32,128]{1,0:T(8,128)S(1)}, u32[]{:S(2)}, u32[]{:S(2)}) collective-permute-start(f32[32,128]{1,0:T(8,128)S(1)} %shard_map.82.refs_8_), channel_id=1, source_target_pairs={{384,321},{385,320},{386,323},{387,322},{388,325},{389,324},{390,3... | collective-permute-start | bytes 49160 | tf_op jit(solution)/shard_map/ppermute | solution.py:258

commit v12 on v11

--- a/solution.py
+++ b/solution.py
@@ -21,6 +21,10 @@
     return group % 2
 
 
+HELD = (1, 3, 0, 2)
+HOLDER = (2, 0, 3, 1)
+
+
 def turns(group):
     return group // 2 * (1 - group % 2)
 
@@ -36,9 +40,9 @@
     return jnp.where(iota(value.shape, 0) % 2 == 0, up, down)
 
 
-def halves(value):
-    half = value.shape[0] // 2
-    return jnp.concatenate([value[half:], value[:half]], axis=0)
+def dealt(value, order):
+    share = value.shape[0] // GROUP
+    return jnp.concatenate([value[part * share : (part + 1) * share] for part in order], axis=0)
 
 
 def pack_kernel(far_ref, u_ref, g_ref, y_ref, k_ref, out_ref, landed, rows, sems):
@@ -57,7 +61,7 @@
             rows[pl.ds(role, chans, stride=ROLES), :] = order(landed[role].astype(F32))
         out_ref[...] = rows[...].astype(BF16)
 
-    by_group(far_ref[0], lambda: store(lambda value: value), lambda: store(neighbours), lambda: store(halves))
+    by_group(far_ref[0], lambda: store(lambda value: value), lambda: store(neighbours), lambda: store(lambda value: dealt(value, HELD)))
 
 
 def flip_rows(count, span):
@@ -218,7 +222,7 @@
         input_ref[...] = order(take(rows, 1, chans)).astype(BF16)
         filt_ref[...] = order(take(rows, 2, chans) + take(rows, 3, chans)) * (1.0 / 64.0)
 
-    by_group(far_ref[0], lambda: store(lambda value: value), lambda: store(neighbours), lambda: store(halves))
+    by_group(far_ref[0], lambda: store(lambda value: value), lambda: store(neighbours), lambda: store(lambda value: dealt(value, HOLDER)))
 
 
 VMEM = pl.BlockSpec(memory_space=pltpu.VMEM)
@@ -251,9 +255,10 @@
     near, seq = lax.axis_size("near"), lax.axis_size("seq")
     pairs = []
     for source, target in edges:
-        turned, crossed = turns(source) ^ turns(target), swaps(source) ^ swaps(target)
+        crossed = swaps(source) ^ swaps(target)
         for i in range(near):
-            to = (i + turned * near // 2) % near
+            share = HELD[i] if turns(source) else i
+            to = HOLDER[share] if turns(target) else share
             pairs += [((source * near + i) * seq + j, (target * near + to) * seq + (j ^ crossed)) for j in range(seq)]
     return lax.ppermute(array, ("far", "near", "seq"), pairs)
 
@@ -282,7 +287,8 @@
         [rows, pltpu.VMEM((2 * GROUP, 2 * blocks, LANES), F32)],
     )(packed)
     near = lax.axis_index("near")
-    near = (near + turns(far) * GROUP // 2) % GROUP
+    held = sum(jnp.where(near == i, share, 0) for i, share in enumerate(HELD))
+    near = jnp.where(turns(far) == 1, held, near)
     chan = near * blocks + (lax.axis_index("seq") ^ swaps(far))
     out = shape((count, LANES), BF16)
     part = shape((blocks, LANES), F32)

time: 59.7 us -> 59.9 us (level)
  no operation moved by 1% of the time
where the time goes in v12:
time: 59.9 us; the launch traced here: 59.5 us
  blocking collectives  41.1 us (69%)
  starting transfers between devices  8.28 us (14%)
  waiting for transfers between devices  5.1 us (9%)
  Pallas kernels  4.24 us (7%)
  between operations  0.8 us (1%)
    all_to_all x2, blocking collectives, body(): packed = lax.all_to_all(packed, ('near', 'seq'), 0, 0, tiled=True)  41.1 us
    ppermute x6, starting transfers between devices, send(): return lax.ppermute(array, ('far', 'near', 'seq'), pairs)  8.28 us
    ppermute x6, waiting for transfers between devices, send(): return lax.ppermute(array, ('far', 'near', 'seq'), pairs)  5.1 us
    pallas_call x1, Pallas kernels, body(): call(lambda *refs: early_kernel(blocks, *refs), (out, out, part), [SMEM,...  1.58 us
  transfers between devices with their start and end apart: 6, of which 2 were waited for; matrix products, arithmetic and copies ran while one was open for 0% of the time, Pallas kernels for 3%

profile of v12, /device:TPU:1, one launch (start us, length us, event | category | flops | bytes accessed | tf_op | source)
XLA Modules:
  0.0 59.5 jit_solution(9187454815737597364)
XLA Ops:
  0.6 0.9 %shard_map.76 = bf16[512,128]{1,0:T(8,128)(2,1)S(1)} custom-call(s32[1]{0:T(128)} %bitcast.far_ref.refs_0_, bf16[128,128]{1,0:T(8,128)(2,1)} %bitcast.19, bf16[128,128]{1,0:T(8,128)(2,1)} %bitcast.20, bf16[128,128]{1,0:T(8,128)(2,1)} %bitcast.21, bf16[128,128]{1,0:T(8,128)(2,1)} %k_ref.1), custom_call_target="tpu_custom_call" | custom-call | tf_op jit(solution)/shard_map/pallas_call | solution.py:272
  1.5 24.6 %all_to_all.22 = bf16[128,4,128]{2,1,0:T(4,128)(2,1)S(1)} all-to-all(bf16[128,4,128]{2,1,0:T(4,128)(2,1)S(1)} %bitcast.18), channel_id=1, replica_groups=mesh['far'=4,'near'=4,'seq'=32] {'near','seq'}, dimensions={0} | all-to-all | bytes 262144 | tf_op jit(solution)/shard_map/all_to_all | solution.py:282
  26.1 1.0 %shard_map.77.refs_4_ = f32[32,128]{1,0:T(8,128)S(1)} custom-call(bf16[512,128]{1,0:T(8,128)(2,1)S(1)} %bitcast.13), custom_call_target="tpu_custom_call" | custom-call | tf_op jit(solution)/shard_map/pallas_call | solution.py:283
  27.1 1.3 %collective-permute-start = (f32[32,128]{1,0:T(8,128)S(1)}, f32[32,128]{1,0:T(8,128)S(1)}, u32[]{:S(2)}, u32[]{:S(2)}) collective-permute-start(f32[32,128]{1,0:T(8,128)S(1)} %shard_map.77.refs_4_), channel_id=1, source_target_pairs={{128,1},{129,0},{130,3},{131,2},{132,5},{133,4},{134,7},{135,6},{1... | collective-permute-start | bytes 49160 | tf_op jit(solution)/shard_map/ppermute | solution.py:263
  28.5 1.3 %collective-permute-start.2 = (f32[32,128]{1,0:T(8,128)S(1)}, f32[32,128]{1,0:T(8,128)S(1)}, u32[]{:S(2)}, u32[]{:S(2)}) collective-permute-start(f32[32,128]{1,0:T(8,128)S(1)} %shard_map.77.refs_4_), channel_id=1, source_target_pairs={{256,32},{257,33},{258,34},{259,35},{260,36},{261,37},{262,38},{26... | collective-permute-start | bytes 49160 | tf_op jit(solution)/shard_map/ppermute | solution.py:263
  29.8 1.3 %collective-permute-start.1 = (f32[32,128]{1,0:T(8,128)S(1)}, f32[32,128]{1,0:T(8,128)S(1)}, u32[]{:S(2)}, u32[]{:S(2)}) collective-permute-start(f32[32,128]{1,0:T(8,128)S(1)} %shard_map.77.refs_4_), channel_id=1, source_target_pairs={{384,1},{385,0},{386,3},{387,2},{388,5},{389,4},{390,7},{391,6},{3... | collective-permute-start | bytes 49160 | tf_op jit(solution)/shard_map/ppermute | solution.py:263
  31.1 1.6 %shard_map.78 = (bf16[128,128]{1,0:T(8,128)(2,1)S(1)}, bf16[128,128]{1,0:T(8,128)(2,1)S(1)}, f32[32,128]{1,0:T(8,128)S(1)}) custom-call(s32[1]{0:T(128)} %bitcast.far_ref.refs_0_, s32[1]{0:T(128)S(6)} %add.22.refs_1_, f32[128]{0:T(128)} %refs_2_.3, bf16[512,128]{1,0:T(8,128)(2,1)S(1)} %bitcast.14, f32[32,128]{1,0:T(8,128)S(1)} %shard_map.77.refs_4_), custom_call_target="tpu_custom_call" | custom-call | tf_op jit(solution)/shard_map/pallas_call | solution.py:302
  32.6 5.0 %collective-permute-done.right_ref = f32[32,128]{1,0:T(8,128)S(1)} collective-permute-done((f32[32,128]{1,0:T(8,128)S(1)}, f32[32,128]{1,0:T(8,128)S(1)}, u32[]{:S(2)}, u32[]{:S(2)}) %collective-permute-start) | collective-permute-done | bytes 16416 | tf_op jit(solution)/shard_map/ppermute | solution.py:263
  37.6 2.4 %collective-permute-start.4 = (f32[32,128]{1,0:T(8,128)S(1)}, f32[32,128]{1,0:T(8,128)S(1)}, u32[]{:S(2)}, u32[]{:S(2)}) collective-permute-start(f32[32,128]{1,0:T(8,128)S(1)} %shard_map.79.left_ref), channel_id=1, source_target_pairs={{0,385},{1,384},{2,387},{3,386},{4,389},{5,388},{6,391},{7,390},{8... | collective-permute-start | bytes 49160 | tf_op jit(solution)/shard_map/ppermute | solution.py:263
  40.1 0.0 collective-permute-done.1.right_ref
  40.1 1.3 %collective-permute-start.3 = (f32[32,128]{1,0:T(8,128)S(1)}, f32[32,128]{1,0:T(8,128)S(1)}, u32[]{:S(2)}, u32[]{:S(2)}) collective-permute-start(f32[32,128]{1,0:T(8,128)S(1)} %shard_map.80.refs_6_.refs_5_), channel_id=1, source_target_pairs={{0,129},{1,128},{2,131},{3,130},{4,133},{5,132},{6,135},{7,134},{8... | collective-permute-start | bytes 49160 | tf_op jit(solution)/shard_map/ppermute | solution.py:263
  41.4 0.0 collective-permute-done.2.after_ref.refs_4_
  41.4 0.0 collective-permute-done.4.pair_ref.refs_7_
  41.4 0.7 %collective-permute-start.5 = (f32[32,128]{1,0:T(8,128)S(1)}, f32[32,128]{1,0:T(8,128)S(1)}, u32[]{:S(2)}, u32[]{:S(2)}) collective-permute-start(f32[32,128]{1,0:T(8,128)S(1)} %shard_map.82.refs_8_), channel_id=1, source_target_pairs={{384,321},{385,320},{386,323},{387,322},{388,325},{389,324},{390,3... | collective-permute-start | bytes 49160 | tf_op jit(solution)/shard_map/ppermute | solution.py:263
  42.1 0.1 collective-permute-done.3.refs_6_
  42.3 0.0 collective-permute-done.5.refs_9_
  42.3 16.5 %all_to_all.23 = bf16[128,4,128]{2,1,0:T(4,128)(2,1)S(1)} all-to-all(bf16[128,4,128]{2,1,0:T(4,128)(2,1)S(1)} %bitcast.16), channel_id=1, replica_groups=mesh['far'=4,'near'=4,'seq'=32] {'near','seq'}, dimensions={0} | all-to-all | bytes 262144 | tf_op jit(solution)/shard_map/all_to_all | solution.py:323
  58.8 0.7 %shard_map.84 = (bf16[128,128]{1,0:T(8,128)(2,1)}, bf16[128,128]{1,0:T(8,128)(2,1)}, f32[128,128]{1,0:T(8,128)}) custom-call(s32[1]{0:T(128)} %bitcast.far_ref.refs_0_, bf16[512,128]{1,0:T(8,128)(2,1)S(1)} %bitcast.17), custom_call_target="tpu_custom_call" | custom-call | tf_op jit(solution)/shard_map/pallas_call | solution.py:324
  (5 shorter events, 0.1 us)
Async XLA Ops:
  27.1 10.5 %collective-permute-start = (f32[32,128]{1,0:T(8,128)S(1)}, f32[32,128]{1,0:T(8,128)S(1)}, u32[]{:S(2)}, u32[]{:S(2)}) collective-permute-start(f32[32,128]{1,0:T(8,128)S(1)} %shard_map.77.refs_4_), channel_id=1, source_target_pairs={{128,1},{129,0},{130,3},{131,2},{132,5},{133,4},{134,7},{135,6},{1... | collective-permute-start | bytes 49160 | tf_op jit(solution)/shard_map/ppermute | solution.py:263
  28.5 12.9 %collective-permute-start.2 = (f32[32,128]{1,0:T(8,128)S(1)}, f32[32,128]{1,0:T(8,128)S(1)}, u32[]{:S(2)}, u32[]{:S(2)}) collective-permute-start(f32[32,128]{1,0:T(8,128)S(1)} %shard_map.77.refs_4_), channel_id=1, source_target_pairs={{256,32},{257,33},{258,34},{259,35},{260,36},{261,37},{262,38},{26... | collective-permute-start | bytes 49160 | tf_op jit(solution)/shard_map/ppermute | solution.py:263
  29.8 10.3 %collective-permute-start.1 = (f32[32,128]{1,0:T(8,128)S(1)}, f32[32,128]{1,0:T(8,128)S(1)}, u32[]{:S(2)}, u32[]{:S(2)}) collective-permute-start(f32[32,128]{1,0:T(8,128)S(1)} %shard_map.77.refs_4_), channel_id=1, source_target_pairs={{384,1},{385,0},{386,3},{387,2},{388,5},{389,4},{390,7},{391,6},{3... | collective-permute-start | bytes 49160 | tf_op jit(solution)/shard_map/ppermute | solution.py:263
  37.6 3.8 %collective-permute-start.4 = (f32[32,128]{1,0:T(8,128)S(1)}, f32[32,128]{1,0:T(8,128)S(1)}, u32[]{:S(2)}, u32[]{:S(2)}) collective-permute-start(f32[32,128]{1,0:T(8,128)S(1)} %shard_map.79.left_ref), channel_id=1, source_target_pairs={{0,385},{1,384},{2,387},{3,386},{4,389},{5,388},{6,391},{7,390},{8... | collective-permute-start | bytes 49160 | tf_op jit(solution)/shard_map/ppermute | solution.py:263
  40.1 2.1 %collective-permute-start.3 = (f32[32,128]{1,0:T(8,128)S(1)}, f32[32,128]{1,0:T(8,128)S(1)}, u32[]{:S(2)}, u32[]{:S(2)}) collective-permute-start(f32[32,128]{1,0:T(8,128)S(1)} %shard_map.80.refs_6_.refs_5_), channel_id=1, source_target_pairs={{0,129},{1,128},{2,131},{3,130},{4,133},{5,132},{6,135},{7,134},{8... | collective-permute-start | bytes 49160 | tf_op jit(solution)/shard_map/ppermute | solution.py:263
  41.4 0.8 %collective-permute-start.5 = (f32[32,128]{1,0:T(8,128)S(1)}, f32[32,128]{1,0:T(8,128)S(1)}, u32[]{:S(2)}, u32[]{:S(2)}) collective-permute-start(f32[32,128]{1,0:T(8,128)S(1)} %shard_map.82.refs_8_), channel_id=1, source_target_pairs={{384,321},{385,320},{386,323},{387,322},{388,325},{389,324},{390,3... | collective-permute-start | bytes 49160 | tf_op jit(solution)/shard_map/ppermute | solution.py:263

commit v13 on v12

--- a/solution.py
+++ b/solution.py
@@ -21,8 +21,8 @@
     return group % 2
 
 
-HELD = (1, 3, 0, 2)
-HOLDER = (2, 0, 3, 1)
+HELD = (1, 0, 3, 2)
+HOLDER = (1, 0, 3, 2)
 
 
 def turns(group):

time: 59.9 us -> 59.9 us (level)
  no operation moved by 1% of the time
where the time goes in v13:
time: 59.9 us; the launch traced here: 59.5 us
  blocking collectives  41.1 us (69%)
  starting transfers between devices  8.28 us (14%)
  waiting for transfers between devices  5.1 us (9%)
  Pallas kernels  4.24 us (7%)
  between operations  0.8 us (1%)
    all_to_all x2, blocking collectives, body(): packed = lax.all_to_all(packed, ('near', 'seq'), 0, 0, tiled=True)  41.1 us
    ppermute x6, starting transfers between devices, send(): return lax.ppermute(array, ('far', 'near', 'seq'), pairs)  8.28 us
    ppermute x6, waiting for transfers between devices, send(): return lax.ppermute(array, ('far', 'near', 'seq'), pairs)  5.1 us
    pallas_call x1, Pallas kernels, body(): call(lambda *refs: early_kernel(blocks, *refs), (out, out, part), [SMEM,...  1.58 us
  transfers between devices with their start and end apart: 6, of which 2 were waited for; matrix products, arithmetic and copies ran while one was open for 0% of the time, Pallas kernels for 3%

profile of v13, /device:TPU:1, one launch (start us, length us, event | category | flops | bytes accessed | tf_op | source)
XLA Modules:
  0.0 59.5 jit_solution(12298557128905871429)
XLA Ops:
  0.6 0.9 %shard_map.76 = bf16[512,128]{1,0:T(8,128)(2,1)S(1)} custom-call(s32[1]{0:T(128)} %bitcast.far_ref.refs_0_, bf16[128,128]{1,0:T(8,128)(2,1)} %bitcast.19, bf16[128,128]{1,0:T(8,128)(2,1)} %bitcast.20, bf16[128,128]{1,0:T(8,128)(2,1)} %bitcast.21, bf16[128,128]{1,0:T(8,128)(2,1)} %k_ref.1), custom_call_target="tpu_custom_call" | custom-call | tf_op jit(solution)/shard_map/pallas_call | solution.py:272
  1.5 24.6 %all_to_all.22 = bf16[128,4,128]{2,1,0:T(4,128)(2,1)S(1)} all-to-all(bf16[128,4,128]{2,1,0:T(4,128)(2,1)S(1)} %bitcast.18), channel_id=1, replica_groups=mesh['far'=4,'near'=4,'seq'=32] {'near','seq'}, dimensions={0} | all-to-all | bytes 262144 | tf_op jit(solution)/shard_map/all_to_all | solution.py:282
  26.1 1.0 %shard_map.77.refs_4_ = f32[32,128]{1,0:T(8,128)S(1)} custom-call(bf16[512,128]{1,0:T(8,128)(2,1)S(1)} %bitcast.13), custom_call_target="tpu_custom_call" | custom-call | tf_op jit(solution)/shard_map/pallas_call | solution.py:283
  27.1 1.3 %collective-permute-start = (f32[32,128]{1,0:T(8,128)S(1)}, f32[32,128]{1,0:T(8,128)S(1)}, u32[]{:S(2)}, u32[]{:S(2)}) collective-permute-start(f32[32,128]{1,0:T(8,128)S(1)} %shard_map.77.refs_4_), channel_id=1, source_target_pairs={{128,1},{129,0},{130,3},{131,2},{132,5},{133,4},{134,7},{135,6},{1... | collective-permute-start | bytes 49160 | tf_op jit(solution)/shard_map/ppermute | solution.py:263
  28.5 1.3 %collective-permute-start.2 = (f32[32,128]{1,0:T(8,128)S(1)}, f32[32,128]{1,0:T(8,128)S(1)}, u32[]{:S(2)}, u32[]{:S(2)}) collective-permute-start(f32[32,128]{1,0:T(8,128)S(1)} %shard_map.77.refs_4_), channel_id=1, source_target_pairs={{256,32},{257,33},{258,34},{259,35},{260,36},{261,37},{262,38},{26... | collective-permute-start | bytes 49160 | tf_op jit(solution)/shard_map/ppermute | solution.py:263
  29.8 1.3 %collective-permute-start.1 = (f32[32,128]{1,0:T(8,128)S(1)}, f32[32,128]{1,0:T(8,128)S(1)}, u32[]{:S(2)}, u32[]{:S(2)}) collective-permute-start(f32[32,128]{1,0:T(8,128)S(1)} %shard_map.77.refs_4_), channel_id=1, source_target_pairs={{384,1},{385,0},{386,3},{387,2},{388,5},{389,4},{390,7},{391,6},{3... | collective-permute-start | bytes 49160 | tf_op jit(solution)/shard_map/ppermute | solution.py:263
  31.1 1.6 %shard_map.78 = (bf16[128,128]{1,0:T(8,128)(2,1)S(1)}, bf16[128,128]{1,0:T(8,128)(2,1)S(1)}, f32[32,128]{1,0:T(8,128)S(1)}) custom-call(s32[1]{0:T(128)} %bitcast.far_ref.refs_0_, s32[1]{0:T(128)S(6)} %add.22.refs_1_, f32[128]{0:T(128)} %refs_2_.3, bf16[512,128]{1,0:T(8,128)(2,1)S(1)} %bitcast.14, f32[32,128]{1,0:T(8,128)S(1)} %shard_map.77.refs_4_), custom_call_target="tpu_custom_call" | custom-call | tf_op jit(solution)/shard_map/pallas_call | solution.py:302
  32.6 5.0 %collective-permute-done.right_ref = f32[32,128]{1,0:T(8,128)S(1)} collective-permute-done((f32[32,128]{1,0:T(8,128)S(1)}, f32[32,128]{1,0:T(8,128)S(1)}, u32[]{:S(2)}, u32[]{:S(2)}) %collective-permute-start) | collective-permute-done | bytes 16416 | tf_op jit(solution)/shard_map/ppermute | solution.py:263
  37.6 2.4 %collective-permute-start.4 = (f32[32,128]{1,0:T(8,128)S(1)}, f32[32,128]{1,0:T(8,128)S(1)}, u32[]{:S(2)}, u32[]{:S(2)}) collective-permute-start(f32[32,128]{1,0:T(8,128)S(1)} %shard_map.79.left_ref), channel_id=1, source_target_pairs={{0,385},{1,384},{2,387},{3,386},{4,389},{5,388},{6,391},{7,390},{8... | collective-permute-start | bytes 49160 | tf_op jit(solution)/shard_map/ppermute | solution.py:263
  40.1 0.0 collective-permute-done.1.right_ref
  40.1 1.3 %collective-permute-start.3 = (f32[32,128]{1,0:T(8,128)S(1)}, f32[32,128]{1,0:T(8,128)S(1)}, u32[]{:S(2)}, u32[]{:S(2)}) collective-permute-start(f32[32,128]{1,0:T(8,128)S(1)} %shard_map.80.refs_6_.refs_5_), channel_id=1, source_target_pairs={{0,129},{1,128},{2,131},{3,130},{4,133},{5,132},{6,135},{7,134},{8... | collective-permute-start | bytes 49160 | tf_op jit(solution)/shard_map/ppermute | solution.py:263
  41.4 0.0 collective-permute-done.2.after_ref.refs_4_
  41.4 0.0 collective-permute-done.4.pair_ref.refs_7_
  41.4 0.7 %collective-permute-start.5 = (f32[32,128]{1,0:T(8,128)S(1)}, f32[32,128]{1,0:T(8,128)S(1)}, u32[]{:S(2)}, u32[]{:S(2)}) collective-permute-start(f32[32,128]{1,0:T(8,128)S(1)} %shard_map.82.refs_8_), channel_id=1, source_target_pairs={{384,289},{385,288},{386,291},{387,290},{388,293},{389,292},{390,2... | collective-permute-start | bytes 49160 | tf_op jit(solution)/shard_map/ppermute | solution.py:263
  42.1 0.1 collective-permute-done.3.refs_6_
  42.3 0.0 collective-permute-done.5.refs_9_
  42.3 16.5 %all_to_all.23 = bf16[128,4,128]{2,1,0:T(4,128)(2,1)S(1)} all-to-all(bf16[128,4,128]{2,1,0:T(4,128)(2,1)S(1)} %bitcast.16), channel_id=1, replica_groups=mesh['far'=4,'near'=4,'seq'=32] {'near','seq'}, dimensions={0} | all-to-all | bytes 262144 | tf_op jit(solution)/shard_map/all_to_all | solution.py:323
  58.8 0.7 %shard_map.84 = (bf16[128,128]{1,0:T(8,128)(2,1)}, bf16[128,128]{1,0:T(8,128)(2,1)}, f32[128,128]{1,0:T(8,128)}) custom-call(s32[1]{0:T(128)} %bitcast.far_ref.refs_0_, bf16[512,128]{1,0:T(8,128)(2,1)S(1)} %bitcast.17), custom_call_target="tpu_custom_call" | custom-call | tf_op jit(solution)/shard_map/pallas_call | solution.py:324
  (5 shorter events, 0.1 us)
Async XLA Ops:
  27.1 10.5 %collective-permute-start = (f32[32,128]{1,0:T(8,128)S(1)}, f32[32,128]{1,0:T(8,128)S(1)}, u32[]{:S(2)}, u32[]{:S(2)}) collective-permute-start(f32[32,128]{1,0:T(8,128)S(1)} %shard_map.77.refs_4_), channel_id=1, source_target_pairs={{128,1},{129,0},{130,3},{131,2},{132,5},{133,4},{134,7},{135,6},{1... | collective-permute-start | bytes 49160 | tf_op jit(solution)/shard_map/ppermute | solution.py:263
  28.5 12.9 %collective-permute-start.2 = (f32[32,128]{1,0:T(8,128)S(1)}, f32[32,128]{1,0:T(8,128)S(1)}, u32[]{:S(2)}, u32[]{:S(2)}) collective-permute-start(f32[32,128]{1,0:T(8,128)S(1)} %shard_map.77.refs_4_), channel_id=1, source_target_pairs={{256,32},{257,33},{258,34},{259,35},{260,36},{261,37},{262,38},{26... | collective-permute-start | bytes 49160 | tf_op jit(solution)/shard_map/ppermute | solution.py:263
  29.8 10.3 %collective-permute-start.1 = (f32[32,128]{1,0:T(8,128)S(1)}, f32[32,128]{1,0:T(8,128)S(1)}, u32[]{:S(2)}, u32[]{:S(2)}) collective-permute-start(f32[32,128]{1,0:T(8,128)S(1)} %shard_map.77.refs_4_), channel_id=1, source_target_pairs={{384,1},{385,0},{386,3},{387,2},{388,5},{389,4},{390,7},{391,6},{3... | collective-permute-start | bytes 49160 | tf_op jit(solution)/shard_map/ppermute | solution.py:263
  37.6 3.8 %collective-permute-start.4 = (f32[32,128]{1,0:T(8,128)S(1)}, f32[32,128]{1,0:T(8,128)S(1)}, u32[]{:S(2)}, u32[]{:S(2)}) collective-permute-start(f32[32,128]{1,0:T(8,128)S(1)} %shard_map.79.left_ref), channel_id=1, source_target_pairs={{0,385},{1,384},{2,387},{3,386},{4,389},{5,388},{6,391},{7,390},{8... | collective-permute-start | bytes 49160 | tf_op jit(solution)/shard_map/ppermute | solution.py:263
  40.1 2.1 %collective-permute-start.3 = (f32[32,128]{1,0:T(8,128)S(1)}, f32[32,128]{1,0:T(8,128)S(1)}, u32[]{:S(2)}, u32[]{:S(2)}) collective-permute-start(f32[32,128]{1,0:T(8,128)S(1)} %shard_map.80.refs_6_.refs_5_), channel_id=1, source_target_pairs={{0,129},{1,128},{2,131},{3,130},{4,133},{5,132},{6,135},{7,134},{8... | collective-permute-start | bytes 49160 | tf_op jit(solution)/shard_map/ppermute | solution.py:263
  41.4 0.8 %collective-permute-start.5 = (f32[32,128]{1,0:T(8,128)S(1)}, f32[32,128]{1,0:T(8,128)S(1)}, u32[]{:S(2)}, u32[]{:S(2)}) collective-permute-start(f32[32,128]{1,0:T(8,128)S(1)} %shard_map.82.refs_8_), channel_id=1, source_target_pairs={{384,289},{385,288},{386,291},{387,290},{388,293},{389,292},{390,2... | collective-permute-start | bytes 49160 | tf_op jit(solution)/shard_map/ppermute | solution.py:263

commit v14 on v13

--- a/solution.py
+++ b/solution.py
@@ -18,7 +18,7 @@
 
 
 def swaps(group):
-    return group % 2
+    return 1 - (group + 3) // 4
 
 
 HELD = (1, 0, 3, 2)
@@ -30,7 +30,7 @@
 
 
 def by_group(group, plain, swapped, turned):
-    pl.when(group == 0)(plain)
+    pl.when(group % 2 == 1)(plain)
     pl.when(swaps(group) == 1)(swapped)
     pl.when(turns(group) == 1)(turned)
 

time: 59.9 us -> 59.7 us (level)
  no operation moved by 1% of the time
where the time goes in v14:
time: 59.7 us; the launch traced here: 59.4 us
  blocking collectives  40.9 us (69%)
  starting transfers between devices  8.29 us (14%)
  waiting for transfers between devices  5.08 us (9%)
  Pallas kernels  4.32 us (7%)
  between operations  0.8 us (1%)
    all_to_all x2, blocking collectives, body(): packed = lax.all_to_all(packed, ('near', 'seq'), 0, 0, tiled=True)  40.9 us
    ppermute x6, starting transfers between devices, send(): return lax.ppermute(array, ('far', 'near', 'seq'), pairs)  8.29 us
    ppermute x6, waiting for transfers between devices, send(): return lax.ppermute(array, ('far', 'near', 'seq'), pairs)  5.08 us
    pallas_call x1, Pallas kernels, body(): call(lambda *refs: early_kernel(blocks, *refs), (out, out, part), [SMEM,...  1.58 us
  transfers between devices with their start and end apart: 6, of which 2 were waited for; matrix products, arithmetic and copies ran while one was open for 0% of the time, Pallas kernels for 3%

profile of v14, /device:TPU:1, one launch (start us, length us, event | category | flops | bytes accessed | tf_op | source)
XLA Modules:
  0.0 59.4 jit_solution(14414855056100797467)
XLA Ops:
  0.6 0.9 %shard_map.76 = bf16[512,128]{1,0:T(8,128)(2,1)S(1)} custom-call(s32[1]{0:T(128)} %bitcast.far_ref.refs_0_, bf16[128,128]{1,0:T(8,128)(2,1)} %bitcast.19, bf16[128,128]{1,0:T(8,128)(2,1)} %bitcast.20, bf16[128,128]{1,0:T(8,128)(2,1)} %bitcast.21, bf16[128,128]{1,0:T(8,128)(2,1)} %k_ref.1), custom_call_target="tpu_custom_call" | custom-call | tf_op jit(solution)/shard_map/pallas_call | solution.py:272
  1.6 24.6 %all_to_all.22 = bf16[128,4,128]{2,1,0:T(4,128)(2,1)S(1)} all-to-all(bf16[128,4,128]{2,1,0:T(4,128)(2,1)S(1)} %bitcast.18), channel_id=1, replica_groups=mesh['far'=4,'near'=4,'seq'=32] {'near','seq'}, dimensions={0} | all-to-all | bytes 262144 | tf_op jit(solution)/shard_map/all_to_all | solution.py:282
  26.2 1.0 %shard_map.77.refs_4_ = f32[32,128]{1,0:T(8,128)S(1)} custom-call(bf16[512,128]{1,0:T(8,128)(2,1)S(1)} %bitcast.13), custom_call_target="tpu_custom_call" | custom-call | tf_op jit(solution)/shard_map/pallas_call | solution.py:283
  27.2 1.3 %collective-permute-start = (f32[32,128]{1,0:T(8,128)S(1)}, f32[32,128]{1,0:T(8,128)S(1)}, u32[]{:S(2)}, u32[]{:S(2)}) collective-permute-start(f32[32,128]{1,0:T(8,128)S(1)} %shard_map.77.refs_4_), channel_id=1, source_target_pairs={{128,1},{129,0},{130,3},{131,2},{132,5},{133,4},{134,7},{135,6},{1... | collective-permute-start | bytes 49160 | tf_op jit(solution)/shard_map/ppermute | solution.py:263
  28.5 1.3 %collective-permute-start.2 = (f32[32,128]{1,0:T(8,128)S(1)}, f32[32,128]{1,0:T(8,128)S(1)}, u32[]{:S(2)}, u32[]{:S(2)}) collective-permute-start(f32[32,128]{1,0:T(8,128)S(1)} %shard_map.77.refs_4_), channel_id=1, source_target_pairs={{256,33},{257,32},{258,35},{259,34},{260,37},{261,36},{262,39},{26... | collective-permute-start | bytes 49160 | tf_op jit(solution)/shard_map/ppermute | solution.py:263
  29.8 1.3 %collective-permute-start.1 = (f32[32,128]{1,0:T(8,128)S(1)}, f32[32,128]{1,0:T(8,128)S(1)}, u32[]{:S(2)}, u32[]{:S(2)}) collective-permute-start(f32[32,128]{1,0:T(8,128)S(1)} %shard_map.77.refs_4_), channel_id=1, source_target_pairs={{384,1},{385,0},{386,3},{387,2},{388,5},{389,4},{390,7},{391,6},{3... | collective-permute-start | bytes 49160 | tf_op jit(solution)/shard_map/ppermute | solution.py:263
  31.1 1.6 %shard_map.78 = (bf16[128,128]{1,0:T(8,128)(2,1)S(1)}, bf16[128,128]{1,0:T(8,128)(2,1)S(1)}, f32[32,128]{1,0:T(8,128)S(1)}) custom-call(s32[1]{0:T(128)} %bitcast.far_ref.refs_0_, s32[1]{0:T(128)S(6)} %add.25.refs_1_, f32[128]{0:T(128)} %refs_2_.3, bf16[512,128]{1,0:T(8,128)(2,1)S(1)} %bitcast.14, f32[32,128]{1,0:T(8,128)S(1)} %shard_map.77.refs_4_), custom_call_target="tpu_custom_call" | custom-call | tf_op jit(solution)/shard_map/pallas_call | solution.py:302
  32.7 4.9 %collective-permute-done.right_ref = f32[32,128]{1,0:T(8,128)S(1)} collective-permute-done((f32[32,128]{1,0:T(8,128)S(1)}, f32[32,128]{1,0:T(8,128)S(1)}, u32[]{:S(2)}, u32[]{:S(2)}) %collective-permute-start) | collective-permute-done | bytes 16416 | tf_op jit(solution)/shard_map/ppermute | solution.py:263
  37.6 2.5 %collective-permute-start.4 = (f32[32,128]{1,0:T(8,128)S(1)}, f32[32,128]{1,0:T(8,128)S(1)}, u32[]{:S(2)}, u32[]{:S(2)}) collective-permute-start(f32[32,128]{1,0:T(8,128)S(1)} %shard_map.79.left_ref), channel_id=1, source_target_pairs={{0,385},{1,384},{2,387},{3,386},{4,389},{5,388},{6,391},{7,390},{8... | collective-permute-start | bytes 49160 | tf_op jit(solution)/shard_map/ppermute | solution.py:263
  40.0 0.0 collective-permute-done.1.right_ref
  40.1 1.3 %collective-permute-start.3 = (f32[32,128]{1,0:T(8,128)S(1)}, f32[32,128]{1,0:T(8,128)S(1)}, u32[]{:S(2)}, u32[]{:S(2)}) collective-permute-start(f32[32,128]{1,0:T(8,128)S(1)} %shard_map.80.refs_6_.refs_5_), channel_id=1, source_target_pairs={{0,129},{1,128},{2,131},{3,130},{4,133},{5,132},{6,135},{7,134},{8... | collective-permute-start | bytes 49160 | tf_op jit(solution)/shard_map/ppermute | solution.py:263
  41.4 0.2 collective-permute-done.2.after_ref.refs_4_
  41.6 0.0 collective-permute-done.4.pair_ref.refs_7_
  41.6 0.7 %collective-permute-start.5 = (f32[32,128]{1,0:T(8,128)S(1)}, f32[32,128]{1,0:T(8,128)S(1)}, u32[]{:S(2)}, u32[]{:S(2)}) collective-permute-start(f32[32,128]{1,0:T(8,128)S(1)} %shard_map.82.refs_8_), channel_id=1, source_target_pairs={{384,288},{385,289},{386,290},{387,291},{388,292},{389,293},{390,2... | collective-permute-start | bytes 49160 | tf_op jit(solution)/shard_map/ppermute | solution.py:263
  42.3 0.0 collective-permute-done.3.refs_6_
  42.3 0.0 collective-permute-done.5.refs_9_
  42.3 16.3 %all_to_all.23 = bf16[128,4,128]{2,1,0:T(4,128)(2,1)S(1)} all-to-all(bf16[128,4,128]{2,1,0:T(4,128)(2,1)S(1)} %bitcast.16), channel_id=1, replica_groups=mesh['far'=4,'near'=4,'seq'=32] {'near','seq'}, dimensions={0} | all-to-all | bytes 262144 | tf_op jit(solution)/shard_map/all_to_all | solution.py:323
  58.7 0.7 %shard_map.84 = (bf16[128,128]{1,0:T(8,128)(2,1)}, bf16[128,128]{1,0:T(8,128)(2,1)}, f32[128,128]{1,0:T(8,128)}) custom-call(s32[1]{0:T(128)} %bitcast.far_ref.refs_0_, bf16[512,128]{1,0:T(8,128)(2,1)S(1)} %bitcast.17), custom_call_target="tpu_custom_call" | custom-call | tf_op jit(solution)/shard_map/pallas_call | solution.py:324
  (5 shorter events, 0.1 us)
Async XLA Ops:
  27.2 10.4 %collective-permute-start = (f32[32,128]{1,0:T(8,128)S(1)}, f32[32,128]{1,0:T(8,128)S(1)}, u32[]{:S(2)}, u32[]{:S(2)}) collective-permute-start(f32[32,128]{1,0:T(8,128)S(1)} %shard_map.77.refs_4_), channel_id=1, source_target_pairs={{128,1},{129,0},{130,3},{131,2},{132,5},{133,4},{134,7},{135,6},{1... | collective-permute-start | bytes 49160 | tf_op jit(solution)/shard_map/ppermute | solution.py:263
  28.5 13.0 %collective-permute-start.2 = (f32[32,128]{1,0:T(8,128)S(1)}, f32[32,128]{1,0:T(8,128)S(1)}, u32[]{:S(2)}, u32[]{:S(2)}) collective-permute-start(f32[32,128]{1,0:T(8,128)S(1)} %shard_map.77.refs_4_), channel_id=1, source_target_pairs={{256,33},{257,32},{258,35},{259,34},{260,37},{261,36},{262,39},{26... | collective-permute-start | bytes 49160 | tf_op jit(solution)/shard_map/ppermute | solution.py:263
  29.8 10.2 %collective-permute-start.1 = (f32[32,128]{1,0:T(8,128)S(1)}, f32[32,128]{1,0:T(8,128)S(1)}, u32[]{:S(2)}, u32[]{:S(2)}) collective-permute-start(f32[32,128]{1,0:T(8,128)S(1)} %shard_map.77.refs_4_), channel_id=1, source_target_pairs={{384,1},{385,0},{386,3},{387,2},{388,5},{389,4},{390,7},{391,6},{3... | collective-permute-start | bytes 49160 | tf_op jit(solution)/shard_map/ppermute | solution.py:263
  37.6 4.0 %collective-permute-start.4 = (f32[32,128]{1,0:T(8,128)S(1)}, f32[32,128]{1,0:T(8,128)S(1)}, u32[]{:S(2)}, u32[]{:S(2)}) collective-permute-start(f32[32,128]{1,0:T(8,128)S(1)} %shard_map.79.left_ref), channel_id=1, source_target_pairs={{0,385},{1,384},{2,387},{3,386},{4,389},{5,388},{6,391},{7,390},{8... | collective-permute-start | bytes 49160 | tf_op jit(solution)/shard_map/ppermute | solution.py:263
  40.1 2.2 %collective-permute-start.3 = (f32[32,128]{1,0:T(8,128)S(1)}, f32[32,128]{1,0:T(8,128)S(1)}, u32[]{:S(2)}, u32[]{:S(2)}) collective-permute-start(f32[32,128]{1,0:T(8,128)S(1)} %shard_map.80.refs_6_.refs_5_), channel_id=1, source_target_pairs={{0,129},{1,128},{2,131},{3,130},{4,133},{5,132},{6,135},{7,134},{8... | collective-permute-start | bytes 49160 | tf_op jit(solution)/shard_map/ppermute | solution.py:263
  41.6 0.7 %collective-permute-start.5 = (f32[32,128]{1,0:T(8,128)S(1)}, f32[32,128]{1,0:T(8,128)S(1)}, u32[]{:S(2)}, u32[]{:S(2)}) collective-permute-start(f32[32,128]{1,0:T(8,128)S(1)} %shard_map.82.refs_8_), channel_id=1, source_target_pairs={{384,288},{385,289},{386,290},{387,291},{388,292},{389,293},{390,2... | collective-permute-start | bytes 49160 | tf_op jit(solution)/shard_map/ppermute | solution.py:263

commit v15 on v14

--- a/solution.py
+++ b/solution.py
@@ -18,7 +18,7 @@
 
 
 def swaps(group):
-    return 1 - (group + 3) // 4
+    return group // 3
 
 
 HELD = (1, 0, 3, 2)
@@ -30,7 +30,7 @@
 
 
 def by_group(group, plain, swapped, turned):
-    pl.when(group % 2 == 1)(plain)
+    pl.when(group < 2)(plain)
     pl.when(swaps(group) == 1)(swapped)
     pl.when(turns(group) == 1)(turned)
 

time: 59.7 us -> 59.9 us (level)
  starting transfers between devices: 8.29 us -> 9.22 us
  waiting for transfers between devices: 5.08 us -> 4.16 us
    ppermute x6, starting transfers between devices: 8.29 us -> 9.22 us  [send(): return lax.ppermute(array, ('far', 'near', 'seq'), pairs)]
    ppermute x6, waiting for transfers between devices: 5.08 us -> 4.16 us  [send(): return lax.ppermute(array, ('far', 'near', 'seq'), pairs)]
where the time goes in v15:
time: 59.9 us; the launch traced here: 59.6 us
  blocking collectives  41.1 us (69%)
  starting transfers between devices  9.22 us (15%)
  Pallas kernels  4.25 us (7%)
  waiting for transfers between devices  4.16 us (7%)
  between operations  0.82 us (1%)
    all_to_all x2, blocking collectives, body(): packed = lax.all_to_all(packed, ('near', 'seq'), 0, 0, tiled=True)  41.1 us
    ppermute x6, starting transfers between devices, send(): return lax.ppermute(array, ('far', 'near', 'seq'), pairs)  9.22 us
    ppermute x6, waiting for transfers between devices, send(): return lax.ppermute(array, ('far', 'near', 'seq'), pairs)  4.16 us
    pallas_call x1, Pallas kernels, body(): call(lambda *refs: early_kernel(blocks, *refs), (out, out, part), [SMEM,...  1.58 us
  transfers between devices with their start and end apart: 6, of which 2 were waited for; matrix products, arithmetic and copies ran while one was open for 0% of the time, Pallas kernels for 3%

profile of v15, /device:TPU:1, one launch (start us, length us, event | category | flops | bytes accessed | tf_op | source)
XLA Modules:
  0.0 59.6 jit_solution(16980105824896730561)
XLA Ops:
  0.6 0.9 %shard_map.76 = bf16[512,128]{1,0:T(8,128)(2,1)S(1)} custom-call(s32[1]{0:T(128)} %bitcast.far_ref.refs_0_, bf16[128,128]{1,0:T(8,128)(2,1)} %bitcast.19, bf16[128,128]{1,0:T(8,128)(2,1)} %bitcast.20, bf16[128,128]{1,0:T(8,128)(2,1)} %bitcast.21, bf16[128,128]{1,0:T(8,128)(2,1)} %k_ref.1), custom_call_target="tpu_custom_call" | custom-call | tf_op jit(solution)/shard_map/pallas_call | solution.py:272
  1.5 24.6 %all_to_all.22 = bf16[128,4,128]{2,1,0:T(4,128)(2,1)S(1)} all-to-all(bf16[128,4,128]{2,1,0:T(4,128)(2,1)S(1)} %bitcast.18), channel_id=1, replica_groups=mesh['far'=4,'near'=4,'seq'=32] {'near','seq'}, dimensions={0} | all-to-all | bytes 262144 | tf_op jit(solution)/shard_map/all_to_all | solution.py:282
  26.1 1.0 %shard_map.77.refs_4_ = f32[32,128]{1,0:T(8,128)S(1)} custom-call(bf16[512,128]{1,0:T(8,128)(2,1)S(1)} %bitcast.13), custom_call_target="tpu_custom_call" | custom-call | tf_op jit(solution)/shard_map/pallas_call | solution.py:283
  27.1 1.3 %collective-permute-start = (f32[32,128]{1,0:T(8,128)S(1)}, f32[32,128]{1,0:T(8,128)S(1)}, u32[]{:S(2)}, u32[]{:S(2)}) collective-permute-start(f32[32,128]{1,0:T(8,128)S(1)} %shard_map.77.refs_4_), channel_id=1, source_target_pairs={{128,0},{129,1},{130,2},{131,3},{132,4},{133,5},{134,6},{135,7},{1... | collective-permute-start | bytes 49160 | tf_op jit(solution)/shard_map/ppermute | solution.py:263
  28.5 1.3 %collective-permute-start.2 = (f32[32,128]{1,0:T(8,128)S(1)}, f32[32,128]{1,0:T(8,128)S(1)}, u32[]{:S(2)}, u32[]{:S(2)}) collective-permute-start(f32[32,128]{1,0:T(8,128)S(1)} %shard_map.77.refs_4_), channel_id=1, source_target_pairs={{256,32},{257,33},{258,34},{259,35},{260,36},{261,37},{262,38},{26... | collective-permute-start | bytes 49160 | tf_op jit(solution)/shard_map/ppermute | solution.py:263
  29.8 1.3 %collective-permute-start.1 = (f32[32,128]{1,0:T(8,128)S(1)}, f32[32,128]{1,0:T(8,128)S(1)}, u32[]{:S(2)}, u32[]{:S(2)}) collective-permute-start(f32[32,128]{1,0:T(8,128)S(1)} %shard_map.77.refs_4_), channel_id=1, source_target_pairs={{384,1},{385,0},{386,3},{387,2},{388,5},{389,4},{390,7},{391,6},{3... | collective-permute-start | bytes 49160 | tf_op jit(solution)/shard_map/ppermute | solution.py:263
  31.1 1.6 %shard_map.78 = (bf16[128,128]{1,0:T(8,128)(2,1)S(1)}, bf16[128,128]{1,0:T(8,128)(2,1)S(1)}, f32[32,128]{1,0:T(8,128)S(1)}) custom-call(s32[1]{0:T(128)} %bitcast.far_ref.refs_0_, s32[1]{0:T(128)S(6)} %add.21.refs_1_, f32[128]{0:T(128)} %refs_2_.3, bf16[512,128]{1,0:T(8,128)(2,1)S(1)} %bitcast.14, f32[32,128]{1,0:T(8,128)S(1)} %shard_map.77.refs_4_), custom_call_target="tpu_custom_call" | custom-call | tf_op jit(solution)/shard_map/pallas_call | solution.py:302
  32.7 4.0 %collective-permute-done.right_ref = f32[32,128]{1,0:T(8,128)S(1)} collective-permute-done((f32[32,128]{1,0:T(8,128)S(1)}, f32[32,128]{1,0:T(8,128)S(1)}, u32[]{:S(2)}, u32[]{:S(2)}) %collective-permute-start) | collective-permute-done | bytes 16416 | tf_op jit(solution)/shard_map/ppermute | solution.py:263
  36.7 3.4 %collective-permute-start.4 = (f32[32,128]{1,0:T(8,128)S(1)}, f32[32,128]{1,0:T(8,128)S(1)}, u32[]{:S(2)}, u32[]{:S(2)}) collective-permute-start(f32[32,128]{1,0:T(8,128)S(1)} %shard_map.79.left_ref), channel_id=1, source_target_pairs={{0,385},{1,384},{2,387},{3,386},{4,389},{5,388},{6,391},{7,390},{8... | collective-permute-start | bytes 49160 | tf_op jit(solution)/shard_map/ppermute | solution.py:263
  40.1 0.0 collective-permute-done.1.right_ref
  40.1 1.3 %collective-permute-start.3 = (f32[32,128]{1,0:T(8,128)S(1)}, f32[32,128]{1,0:T(8,128)S(1)}, u32[]{:S(2)}, u32[]{:S(2)}) collective-permute-start(f32[32,128]{1,0:T(8,128)S(1)} %shard_map.80.refs_6_.refs_5_), channel_id=1, source_target_pairs={{0,128},{1,129},{2,130},{3,131},{4,132},{5,133},{6,134},{7,135},{8... | collective-permute-start | bytes 49160 | tf_op jit(solution)/shard_map/ppermute | solution.py:263
  41.4 0.0 collective-permute-done.2.after_ref.refs_4_
  41.4 0.0 collective-permute-done.4.pair_ref.refs_7_
  41.5 0.7 %collective-permute-start.5 = (f32[32,128]{1,0:T(8,128)S(1)}, f32[32,128]{1,0:T(8,128)S(1)}, u32[]{:S(2)}, u32[]{:S(2)}) collective-permute-start(f32[32,128]{1,0:T(8,128)S(1)} %shard_map.82.refs_8_), channel_id=1, source_target_pairs={{384,289},{385,288},{386,291},{387,290},{388,293},{389,292},{390,2... | collective-permute-start | bytes 49160 | tf_op jit(solution)/shard_map/ppermute | solution.py:263
  42.2 0.1 collective-permute-done.3.refs_6_
  42.3 0.0 collective-permute-done.5.refs_9_
  42.3 16.5 %all_to_all.23 = bf16[128,4,128]{2,1,0:T(4,128)(2,1)S(1)} all-to-all(bf16[128,4,128]{2,1,0:T(4,128)(2,1)S(1)} %bitcast.16), channel_id=1, replica_groups=mesh['far'=4,'near'=4,'seq'=32] {'near','seq'}, dimensions={0} | all-to-all | bytes 262144 | tf_op jit(solution)/shard_map/all_to_all | solution.py:323
  58.8 0.7 %shard_map.84 = (bf16[128,128]{1,0:T(8,128)(2,1)}, bf16[128,128]{1,0:T(8,128)(2,1)}, f32[128,128]{1,0:T(8,128)}) custom-call(s32[1]{0:T(128)} %bitcast.far_ref.refs_0_, bf16[512,128]{1,0:T(8,128)(2,1)S(1)} %bitcast.17), custom_call_target="tpu_custom_call" | custom-call | tf_op jit(solution)/shard_map/pallas_call | solution.py:324
  (5 shorter events, 0.1 us)
Async XLA Ops:
  27.1 9.6 %collective-permute-start = (f32[32,128]{1,0:T(8,128)S(1)}, f32[32,128]{1,0:T(8,128)S(1)}, u32[]{:S(2)}, u32[]{:S(2)}) collective-permute-start(f32[32,128]{1,0:T(8,128)S(1)} %shard_map.77.refs_4_), channel_id=1, source_target_pairs={{128,0},{129,1},{130,2},{131,3},{132,4},{133,5},{134,6},{135,7},{1... | collective-permute-start | bytes 49160 | tf_op jit(solution)/shard_map/ppermute | solution.py:263
  28.5 13.0 %collective-permute-start.2 = (f32[32,128]{1,0:T(8,128)S(1)}, f32[32,128]{1,0:T(8,128)S(1)}, u32[]{:S(2)}, u32[]{:S(2)}) collective-permute-start(f32[32,128]{1,0:T(8,128)S(1)} %shard_map.77.refs_4_), channel_id=1, source_target_pairs={{256,32},{257,33},{258,34},{259,35},{260,36},{261,37},{262,38},{26... | collective-permute-start | bytes 49160 | tf_op jit(solution)/shard_map/ppermute | solution.py:263
  29.8 10.3 %collective-permute-start.1 = (f32[32,128]{1,0:T(8,128)S(1)}, f32[32,128]{1,0:T(8,128)S(1)}, u32[]{:S(2)}, u32[]{:S(2)}) collective-permute-start(f32[32,128]{1,0:T(8,128)S(1)} %shard_map.77.refs_4_), channel_id=1, source_target_pairs={{384,1},{385,0},{386,3},{387,2},{388,5},{389,4},{390,7},{391,6},{3... | collective-permute-start | bytes 49160 | tf_op jit(solution)/shard_map/ppermute | solution.py:263
  36.7 4.7 %collective-permute-start.4 = (f32[32,128]{1,0:T(8,128)S(1)}, f32[32,128]{1,0:T(8,128)S(1)}, u32[]{:S(2)}, u32[]{:S(2)}) collective-permute-start(f32[32,128]{1,0:T(8,128)S(1)} %shard_map.79.left_ref), channel_id=1, source_target_pairs={{0,385},{1,384},{2,387},{3,386},{4,389},{5,388},{6,391},{7,390},{8... | collective-permute-start | bytes 49160 | tf_op jit(solution)/shard_map/ppermute | solution.py:263
  40.1 2.1 %collective-permute-start.3 = (f32[32,128]{1,0:T(8,128)S(1)}, f32[32,128]{1,0:T(8,128)S(1)}, u32[]{:S(2)}, u32[]{:S(2)}) collective-permute-start(f32[32,128]{1,0:T(8,128)S(1)} %shard_map.80.refs_6_.refs_5_), channel_id=1, source_target_pairs={{0,128},{1,129},{2,130},{3,131},{4,132},{5,133},{6,134},{7,135},{8... | collective-permute-start | bytes 49160 | tf_op jit(solution)/shard_map/ppermute | solution.py:263
  41.5 0.8 %collective-permute-start.5 = (f32[32,128]{1,0:T(8,128)S(1)}, f32[32,128]{1,0:T(8,128)S(1)}, u32[]{:S(2)}, u32[]{:S(2)}) collective-permute-start(f32[32,128]{1,0:T(8,128)S(1)} %shard_map.82.refs_8_), channel_id=1, source_target_pairs={{384,289},{385,288},{386,291},{387,290},{388,293},{389,292},{390,2... | collective-permute-start | bytes 49160 | tf_op jit(solution)/shard_map/ppermute | solution.py:263
